TPU v7x, 512 devices: a whole 4x8x8 slice. The times are simulated.
512 devices in a mesh: ctx: 8 (over x, y_hi), tp: 64 (over y_lo, z, core).
Axes of the slice: x: 4, y: 8 (y_hi: 2, y_lo: 4; y = y_hi * 4 + y_lo), z: 8, core: 2. Of those that a mesh axis runs over, the one named last changes fastest.
Arguments:
- tokens: bfloat16 [1024, 8192], P('ctx', 'tp'), may hold values from -6 to 6
- feat_weight: bfloat16 [8192, 3, 8192], P('ctx', None, 'tp'), may hold values from -0.0625 to 0.0625
- short_taps: float32 [3, 3, 8192], P(None, None, 'tp'), may hold values from -1 to 1
- long_filter: float32 [512, 128], P('tp'), may hold values from -0.5 to 0.5
- skip_gain: float32 [8192], P('tp'), may hold values from -1 to 1
- out_grad: bfloat16 [1024, 8192], P('ctx', 'tp'), may hold values from -16 to 16
Outputs:
- input_grad: bfloat16 [1024, 8192], P('ctx', 'tp')
- filter_grad: float32 [512, 128], P('tp')
- skip_grad: float32 [8192], P('tp')
- short_grad: float32 [3, 3, 8192], P(None, None, 'tp')
All inputs are finite; a program needn't handle non-finite values.
Results may differ from a plain program's by a relative error of at most 0.011.
Values may be sent and summed in bfloat16 or wider, within the bound.
No kernel may reach another device: no remote copies, remote signals or barrier semaphores. Data moves between devices by JAX's collectives and lax.ppermute only.
A program may use at most 64 MiB of HBM per device.

v0:
```python
import jax
import jax.numpy as jnp
from jax import lax
from jax.sharding import PartitionSpec as P


def from_behind(block, axis, distance):
    devices = range(lax.axis_size(axis))
    route = [(i - distance, i) for i in devices if i - distance in devices]
    return lax.ppermute(block, axis, route)


def banded(table, tok_rows):
    group_count = table.shape[0]
    period = table.shape[1]
    tiled = jnp.tile(table, (1, tok_rows))[:, : tok_rows * (period - 1)]
    return tiled.reshape(group_count, tok_rows, period - 1)


def on_device(tokens, feat_weight, short_taps, long_filter, skip_gain, out_grad):
    tok_rows = tokens.shape[0]
    chan_count = tokens.shape[1]
    group_count = long_filter.shape[0]
    tap_count = long_filter.shape[1]
    short_count = short_taps.shape[0]
    group_width = chan_count // group_count
    span_rows = tok_rows + tap_count - 1
    whole_in = lax.all_gather(tokens, "tp", axis=1, tiled=True)
    flat_weight = feat_weight.reshape(feat_weight.shape[0], 3 * chan_count)
    full_weight = lax.all_gather(flat_weight, "ctx", axis=0, tiled=True)
    projected = jnp.dot(whole_in, full_weight, preferred_element_type=jnp.float32)
    feats = projected.astype(jnp.bfloat16).reshape(tok_rows, 3, chan_count)
    tail_feats = from_behind(feats[tok_rows - (short_count - 1) :], "ctx", 1)
    feat_ext = jnp.concatenate([tail_feats, feats], axis=0)
    mixed = jnp.zeros((tok_rows, 3, chan_count), jnp.float32)
    for offset in range(short_count):
        mixed = mixed + short_taps[offset] * feat_ext[
            short_count - 1 - offset : short_count - 1 - offset + tok_rows
        ].astype(jnp.float32)
    query_feat = mixed[:, 0]
    key_feat = mixed[:, 1]
    value_feat = mixed[:, 2]
    product = (key_feat * value_feat).astype(jnp.bfloat16)
    product_f = product.astype(jnp.float32)
    tail_prod = from_behind(product[tok_rows - (tap_count - 1) :], "ctx", 1)
    prod_cat = jnp.concatenate([tail_prod, product], axis=0).reshape(
        span_rows, group_count, group_width
    )
    prod_wide = prod_cat.astype(jnp.float32)
    fwd_band = banded(jnp.pad(long_filter[:, ::-1], ((0, 0), (0, tok_rows))), tok_rows)
    long_conv = jnp.einsum(
        "gts,sgc->tgc", fwd_band, prod_wide, precision=lax.Precision.HIGHEST
    ).reshape(tok_rows, chan_count)
    long_conv = long_conv + skip_gain * product_f
    grad_out = out_grad.astype(jnp.float32)
    dconv = (grad_out * query_feat).astype(jnp.bfloat16)
    dconv_f = dconv.astype(jnp.float32)
    dquery = grad_out * long_conv
    head_conv = from_behind(dconv[: tap_count - 1], "ctx", -1)
    dconv_wide = (
        jnp.concatenate([dconv, head_conv], axis=0)
        .astype(jnp.float32)
        .reshape(span_rows, group_count, group_width)
    )
    back_band = banded(jnp.pad(long_filter, ((0, 0), (0, tok_rows))), tok_rows)
    dproduct = jnp.einsum(
        "gts,sgc->tgc", back_band, dconv_wide, precision=lax.Precision.HIGHEST
    ).reshape(tok_rows, chan_count)
    dproduct = dproduct + skip_gain * dconv_f
    cross_terms = jnp.einsum(
        "sgc,tgc->gts",
        prod_cat,
        dconv.reshape(tok_rows, group_count, group_width),
        preferred_element_type=jnp.float32,
    )
    folded = jnp.pad(
        cross_terms.reshape(group_count, tok_rows * span_rows), ((0, 0), (0, tok_rows))
    )
    folded = folded.reshape(group_count, tok_rows, span_rows + 1).sum(axis=1)
    filter_grad = folded[:, :tap_count][:, ::-1]
    skip_grad = jnp.sum(dconv_f * product_f, axis=0)
    dmixed = jnp.stack([dquery, dproduct * value_feat, dproduct * key_feat], axis=1)
    head_grad = from_behind(dmixed[: short_count - 1], "ctx", -1)
    dmixed_ext = jnp.concatenate([dmixed, head_grad], axis=0)
    dfeats = jnp.zeros((tok_rows, 3, chan_count), jnp.float32)
    short_list = []
    for offset in range(short_count):
        dfeats = dfeats + short_taps[offset] * dmixed_ext[offset : offset + tok_rows]
        short_list.append(
            jnp.sum(
                dmixed
                * feat_ext[short_count - 1 - offset : short_count - 1 - offset + tok_rows].astype(
                    jnp.float32
                ),
                axis=0,
            )
        )
    short_grad = jnp.stack(short_list, axis=0)
    dfeats = dfeats.astype(jnp.bfloat16).reshape(tok_rows, 3 * chan_count)
    partial_grad = lax.dot_general(
        dfeats, full_weight, (((1,), (1,)), ((), ())), preferred_element_type=jnp.float32
    )
    input_grad = lax.psum_scatter(partial_grad, "tp", scatter_dimension=1, tiled=True).astype(
        jnp.bfloat16
    )
    filter_grad, skip_grad, short_grad = lax.psum((filter_grad, skip_grad, short_grad), "ctx")
    return (input_grad, filter_grad, skip_grad, short_grad)


def solution(mesh):
    in_specs = (
        P("ctx", "tp"),
        P("ctx", None, "tp"),
        P(None, None, "tp"),
        P("tp", None),
        P("tp"),
        P("ctx", "tp"),
    )
    out_specs = (P("ctx", "tp"), P("tp", None), P("tp"), P(None, None, "tp"))
    return jax.shard_map(
        on_device, mesh=mesh, in_specs=in_specs, out_specs=out_specs, check_vma=False
    )
```

profile of v0, /device:TPU:2, one launch (start us, length us, event | category | flops | bytes accessed | tf_op | source)
XLA Modules:
  0.0 630.8 jit_solution(1916373714837353039)
XLA Ops:
  7.2 0.7 all-gather.3.cloned.1.call-update
  8.0 2.3 copy.20
  10.4 119.6 %all-gather.3.cloned.1.call-done = bf16[128,8192]{1,0:T(8,128)(2,1)} async-done(((bf16[128,128]{1,0:T(8,128)(2,1)}), bf16[128,8192]{1,0:T(8,128)(2,1)}) %all-gather.3.cloned.1.call-update) | async-done | bytes 2097168 | tf_op jit(solution)/shard_map/all_gather | solution.py:28
  130.0 143.9 %all-gather.5.cloned.1.call-done = bf16[8192,384]{0,1:T(8,128)(2,1)} async-done(((bf16[1024,384]{0,1:T(8,128)(2,1)}), bf16[8192,384]{0,1:T(8,128)(2,1)}) %all-gather.5.cloned.1.call-update) | async-done | bytes 6291472 | tf_op jit(solution)/shard_map/all_gather | solution.py:30
  273.9 5.4 convolution_convert_fusion
  279.3 0.2 copy.24
  279.5 1.9 collective-permute-start
  281.7 11.0 %collective-permute-done = bf16[2,3,128]{0,2,1:T(8,128)(2,1)S(1)} collective-permute-done((bf16[2,3,128]{0,2,1:T(8,128)(2,1)S(1)}, bf16[2,3,128]{0,2,1:T(8,128)(2,1)S(1)}, u32[]{:S(2)}, u32[]{:S(2)}) %collective-permute-start) | collective-permute-done | bytes 1568 | tf_op jit(solution)/shard_map/ppermute | solution.py:10
  292.7 0.3 fusion.1
  293.0 0.6 fusion.12
  293.7 1.9 collective-permute-start.2
  295.8 1.4 reshape.63
  297.4 1.4 reshape.60
  298.8 0.8 slice.82
  299.7 7.8 %collective-permute-start.1 = (bf16[127,128]{0,1:T(8,128)(2,1)S(1)}, bf16[127,128]{0,1:T(8,128)(2,1)S(1)}, u32[]{:S(2)}, u32[]{:S(2)}) collective-permute-start(bf16[127,128]{0,1:T(8,128)(2,1)S(1)} %slice.82), channel_id=1, source_target_pairs={{0,64},{64,128},{128,192},{192,256},{256,320},{320,384},{384,448},... | collective-permute-start | bytes 97544 | tf_op jit(solution)/shard_map/ppermute | solution.py:10
  307.5 0.8 pad_maximum_fusion.4
  308.3 0.6 fusion.15
  308.9 1.5 collective-permute-done.1
  310.4 0.8 pad_maximum_fusion.3
  311.2 0.6 fusion.14
  311.8 0.9 multiply_bitcast_fusion.1
  312.7 1.9 collective-permute-start.3
  314.7 11.3 %collective-permute-done.3 = f32[2,3,128]{0,2,1:T(8,128)S(1)} collective-permute-done((f32[2,3,128]{0,2,1:T(8,128)S(1)}, f32[2,3,128]{0,2,1:T(8,128)S(1)}, u32[]{:S(2)}, u32[]{:S(2)}) %collective-permute-start.3) | collective-permute-done | bytes 3104 | tf_op jit(solution)/shard_map/ppermute | solution.py:10
  326.0 1.5 fusion.2
  327.5 6.1 fusion.16
  333.7 0.1 copy.23
  333.8 1.1 fusion.17
  334.9 0.6 reshape.67
  335.6 0.1 reduce_sum.45
  335.9 50.2 %all-reduce.3 = (f32[8,128]{1,0:T(8,128)}, f32[128]{0:T(128)}, f32[3,3,128]{2,1,0:T(4,128)}) all-reduce(f32[8,128]{1,0:T(8,128)S(1)} %rev.7, f32[128]{0:T(128)S(1)} %get-tuple-element.9, f32[3,3,128]{2,1,0:T(4,128)S(1)} %pad_maximum_fusion.5), channel_id=1, replica_groups=mesh['ctx'=8,'tp'=64] {'ctx'}, use_global_device_ids=true, to_apply=%region_2.3 | all-reduce | flops 2304 | bytes 18432 | tf_op jit(solution)/shard_map/psum | solution.py:106
  386.1 236.8 %reduce-scatter.2.cloned.1.call-done = f32[128,128]{1,0:T(8,128)} async-done(((f32[128,8192]{1,0:T(8,128)}), f32[128,128]{1,0:T(8,128)}) %reduce-scatter.2.cloned.1.call-update) | async-done | bytes 65552 | tf_op jit(solution)/shard_map/reduce_scatter | solution.py:103
  622.8 1.5 convert_element_type.56
  (36 shorter events, 1.0 us)
Async XLA Ops:
  7.2 274.3 %copy-start.4 = (f32[3,3,128]{2,1,0:T(4,128)S(1)}, f32[3,3,128]{2,1,0:T(4,128)}, u32[]{:S(2)}) copy-start(f32[3,3,128]{2,1,0:T(4,128)} %param.8) | copy-start | bytes 13828
  7.2 274.3 %copy-start.2 = (bf16[128,128]{1,0:T(8,128)(2,1)S(1)}, bf16[128,128]{1,0:T(8,128)(2,1)}, u32[]{:S(2)}) copy-start(bf16[128,128]{1,0:T(8,128)(2,1)} %param.11) | copy-start | bytes 98308
  7.2 288.4 %copy-start.3 = (f32[8,128]{1,0:T(8,128)S(1)}, f32[8,128]{1,0:T(8,128)}, u32[]{:S(2)}) copy-start(f32[8,128]{1,0:T(8,128)} %param.9) | copy-start | bytes 12292
  7.2 122.8 %all-gather.3.cloned.1.call-start = ((), (), s32[]{:S(2)}) async-start(), calls=%async_computation.1 | async-start | bytes 2129920 | tf_op jit(solution)/shard_map/all_gather | solution.py:28
  7.9 266.0 %all-gather.5.cloned.1.call-start = ((), (), s32[]{:S(2)}) async-start(), calls=%async_computation.2 | async-start | bytes 7077888 | tf_op jit(solution)/shard_map/all_gather | solution.py:30
  10.3 612.5 %reduce-scatter.2.cloned.1.call-start = ((), (), s32[]{:S(2)}) async-start(), calls=%async_computation.3 | async-start | bytes 4259840 | tf_op jit(solution)/shard_map/reduce_scatter | solution.py:103
  279.5 13.2 %collective-permute-start = (bf16[2,3,128]{0,2,1:T(8,128)(2,1)S(1)}, bf16[2,3,128]{0,2,1:T(8,128)(2,1)S(1)}, u32[]{:S(2)}, u32[]{:S(2)}) collective-permute-start(bf16[2,3,128]{0,2,1:T(8,128)(2,1)S(1)} %bitcast.81), channel_id=1, source_target_pairs={{0,64},{64,128},{128,192},{192,256},{256,320},{320,384},{384,448},... | collective-permute-start | bytes 4616 | tf_op jit(solution)/shard_map/ppermute | solution.py:10
  281.6 14.2 %copy-start.1 = (bf16[128,128]{0,1:T(8,128)(2,1)}, bf16[128,128]{0,1:T(8,128)(2,1)S(1)}, u32[]{:S(2)}) copy-start(bf16[128,128]{0,1:T(8,128)(2,1)S(1)} %copy.19) | copy-start | bytes 98308
  292.7 3.0 copy-start
  293.7 13.8 %collective-permute-start.2 = (bf16[127,128]{0,1:T(8,128)(2,1)}, bf16[127,128]{0,1:T(8,128)(2,1)}, u32[]{:S(2)}, u32[]{:S(2)}) collective-permute-start(bf16[127,128]{0,1:T(8,128)(2,1)} %bitcast.67), channel_id=1, source_target_pairs={{64,0},{128,64},{192,128},{256,192},{320,256},{384,320},{448,384},... | collective-permute-start | bytes 97544 | tf_op jit(solution)/shard_map/ppermute | solution.py:10
  295.8 16.1 %copy-start.5 = (f32[128]{0:T(128)S(1)}, f32[128]{0:T(128)}, u32[]{:S(2)}) copy-start(f32[128]{0:T(128)} %param.10) | copy-start | bytes 1540
  299.7 10.7 %collective-permute-start.1 = (bf16[127,128]{0,1:T(8,128)(2,1)S(1)}, bf16[127,128]{0,1:T(8,128)(2,1)S(1)}, u32[]{:S(2)}, u32[]{:S(2)}) collective-permute-start(bf16[127,128]{0,1:T(8,128)(2,1)S(1)} %slice.82), channel_id=1, source_target_pairs={{0,64},{64,128},{128,192},{192,256},{256,320},{320,384},{384,448},... | collective-permute-start | bytes 97544 | tf_op jit(solution)/shard_map/ppermute | solution.py:10
  312.7 13.2 %collective-permute-start.3 = (f32[2,3,128]{0,2,1:T(8,128)S(1)}, f32[2,3,128]{0,2,1:T(8,128)S(1)}, u32[]{:S(2)}, u32[]{:S(2)}) collective-permute-start(f32[2,3,128]{0,2,1:T(8,128)S(1)} %bitcast.75), channel_id=1, source_target_pairs={{64,0},{128,64},{192,128},{256,192},{320,256},{384,320},{448,384},... | collective-permute-start | bytes 9224 | tf_op jit(solution)/shard_map/ppermute | solution.py:10
Sparse Core Ops, SparseCore 0:
  10.1 119.8 all-gather.2
  133.2 140.6 all-gather.4
  333.8 288.9 reduce-scatter.1
where the time goes:
time: 632 us; the launch traced here: 631 us
  waiting for transfers between devices  525 us (83%)
  blocking collectives  50.2 us (8%)
  between operations  14 us (2%)
  matrix products  13.8 us (2%)
  starting transfers between devices  13.7 us (2%)
  local copies, waits for them, and re-layouts  7.66 us (1%)
  other arithmetic  6.66 us (1%)
    reduce_scatter x1, waiting for transfers between devices, on_device(): lax.psum_scatter(partial_grad, 'tp', scatter_dimension=1, tiled=True)  237 us
    all_gather x1, waiting for transfers between devices, on_device(): full_weight = lax.all_gather(flat_weight, 'ctx', axis=0, tiled=True)  144 us
    all_gather x1, waiting for transfers between devices, on_device(): whole_in = lax.all_gather(tokens, 'tp', axis=1, tiled=True)  120 us
    psum x1, blocking collectives, on_device(): lax.psum((filter_grad, skip_grad, short_grad), 'ctx')  50.2 us
    ppermute x4, waiting for transfers between devices, from_behind(): return lax.ppermute(block, axis, route)  23.8 us
    ppermute x4, starting transfers between devices, from_behind(): return lax.ppermute(block, axis, route)  13.6 us
  transfers between devices with their start and end apart: 7, of which 6 were waited for; matrix products, arithmetic and copies ran while one was open for 2% of the time, Pallas kernels for 0%

commit v1 on v0

v1 whole, which is shorter than its diff:
```python
import jax
import jax.numpy as jnp
import numpy as np
from jax import lax
from jax.experimental import pallas as pl
from jax.experimental.pallas import tpu as pltpu
from jax.sharding import Mesh
from jax.sharding import PartitionSpec as P

AXES = ("x", "yh", "yl", "zh", "zl", "core")
SIZES = (4, 2, 4, 2, 4, 2)
CTX = ("x", "yh")
TP = ("yl", "zh", "zl", "core")
PLANE = ("yl", "zh", "zl")
F32 = jnp.float32
BF16 = jnp.bfloat16
VMEM = pl.BlockSpec(memory_space=pltpu.VMEM)
SMEM = pl.BlockSpec(memory_space=pltpu.SMEM)
ROWS = 64
HALF = 128


def params(mib):
    return pltpu.CompilerParams(vmem_limit_bytes=mib * 1024 * 1024)


def rolled_rows(table, left):
    rows = lax.broadcasted_iota(jnp.int32, table.shape, 0)
    for bit in range(7):
        step = 1 << bit
        turned = pltpu.roll(table, 128 - step if left else step, 1)
        table = jnp.where((rows & step) != 0, turned, table)
    return table


def prepare_kernel(place, grad_ref, taps_ref, skip_ref, filter_ref, grad_t_ref, table_ref, band_ref):
    ctx = place[2]
    grad_t_ref[...] = grad_ref[...].astype(F32).T.astype(BF16).reshape(8, 16, HALF)
    rows = jnp.concatenate(
        [taps_ref[...], skip_ref[...], jnp.zeros((118, 128), F32)], axis=0
    )
    table_ref[...] = rows.T
    band = rolled_rows(
        jnp.broadcast_to(filter_ref[pl.ds(ctx, 1), :], (128, 128)), False
    )
    src = lax.broadcasted_iota(jnp.int32, (128, 128), 0)
    dst = lax.broadcasted_iota(jnp.int32, (128, 128), 1)
    near = jnp.where(dst >= src, band, 0.0)
    far = jnp.where(dst < src, band, 0.0)
    for place_at, part in ((0, near), (2, far)):
        high = part.astype(BF16)
        band_ref[place_at] = high
        band_ref[place_at + 1] = (part - high.astype(F32)).astype(BF16)


def weight_parts(w_own, w_prev, w_next, w_far0, w_far1):
    def whole(ref):
        return lambda side, proj: ref[side, proj].reshape(512, 128)

    def split(side, proj):
        return (w_far0 if side == 0 else w_far1)[proj].reshape(512, 128)

    return ((0, whole(w_own)), (3, whole(w_prev)), (1, whole(w_next)), (2, split))


def project_kernel(place, in_ref, w_own, w_prev, w_next, w_far0, w_far1, grad_ref, out_ref):
    x = place[0]
    core = place[1]
    parts = weight_parts(w_own, w_prev, w_next, w_far0, w_far1)
    rows = []
    for shift, _ in parts:
        block = lax.rem(x + shift, 4)
        rows.append(
            jnp.concatenate(
                [
                    jnp.concatenate([in_ref[block, half, z] for z in range(4)], axis=1)
                    for half in range(2)
                ],
                axis=0,
            )
        )
    for side in range(2):
        to_core = lax.rem(core + side, 2)
        for proj in range(3):
            total = jnp.zeros((256, 128), F32)
            for row, (_, weight) in zip(rows, parts):
                total = total + jnp.dot(row, weight(side, proj), preferred_element_type=F32)
            turned = total.T.astype(BF16)
            for group in range(8):
                out_ref[group, to_core, proj * 16 : proj * 16 + 16, :] = turned[
                    group * 16 : group * 16 + 16
                ]
        for group in range(8):
            out_ref[group, to_core, 48:ROWS, :] = jnp.concatenate(
                [grad_ref[group], jnp.zeros((16, 128), BF16)], axis=1
            )


def mixer_kernel(place, in_ref, table_ref, band_ref, out_ref):
    core = place[1]
    ctx = place[2]
    tokens = 1024
    lane = lax.broadcasted_iota(jnp.int32, (16, tokens), 1)
    table = table_ref[pl.ds(pl.multiple_of(ctx * 16, 16), 16), :]

    def column(k):
        return table[:, k : k + 1]

    def behind(block, k):
        if k == 0:
            return block
        return jnp.where(lane >= k, pltpu.roll(block, k, 1), 0.0)

    def ahead(block, k):
        if k == 0:
            return block
        return jnp.where(lane < tokens - k, pltpu.roll(block, tokens - k, 1), 0.0)

    def stacked(block):
        return jnp.concatenate([block[:, 128 * b : 128 * b + 128] for b in range(8)], axis=0)

    def flat(block):
        return jnp.concatenate([block[16 * b : 16 * b + 16] for b in range(8)], axis=1)

    grad_out = jnp.concatenate(
        [in_ref[i, core, 48:ROWS, 0:128] for i in range(8)], axis=1
    ).astype(F32)
    feats = []
    mixed = []
    for proj in range(3):
        quarters = []
        for x in range(4):
            total = jnp.zeros((16, 256), F32)
            for yh in range(2):
                for side in range(2):
                    total = total + in_ref[2 * x + yh, side, proj * 16 : proj * 16 + 16, :].astype(F32)
            quarters.append(total)
        feat = jnp.concatenate(quarters, axis=1).astype(BF16).astype(F32)
        shifted = [behind(feat, k) for k in range(3)]
        feats.append(shifted)
        running = jnp.zeros((16, tokens), F32)
        for k in range(3):
            running = running + column(3 * k + proj) * shifted[k]
        mixed.append(running)
    query, key, value = mixed
    skip = column(9)
    product = (key * value).astype(BF16)
    dconv = (grad_out * query).astype(BF16)
    prod_rows = stacked(product)
    conv_rows = stacked(dconv)
    none = jnp.zeros((16, 128), BF16)
    prod_prev = jnp.concatenate([none, prod_rows[:112]], axis=0)
    conv_next = jnp.concatenate([conv_rows[16:], none], axis=0)
    forward = jnp.zeros((128, 128), F32)
    backward = jnp.zeros((128, 128), F32)
    over_last = (((1,), (1,)), ((), ()))
    over_first = (((0,), (0,)), ((), ()))
    for at, (left, right) in enumerate(
        ((prod_rows, conv_rows), (prod_rows, conv_rows), (prod_prev, conv_next), (prod_prev, conv_next))
    ):
        band = band_ref[at]
        forward = forward + jnp.dot(left, band, preferred_element_type=F32)
        backward = backward + lax.dot_general(right, band, over_last, preferred_element_type=F32)
    product_f = product.astype(F32)
    dconv_f = dconv.astype(F32)
    long_conv = flat(forward) + skip * product_f
    dproduct = flat(backward) + skip * dconv_f
    near = lax.dot_general(prod_rows, conv_rows, over_first, preferred_element_type=F32)
    far = lax.dot_general(prod_prev, conv_rows, over_first, preferred_element_type=F32)
    src = lax.broadcasted_iota(jnp.int32, (128, 128), 0)
    dst = lax.broadcasted_iota(jnp.int32, (128, 128), 1)
    cross = rolled_rows(jnp.where(dst >= src, near, far), True)
    filter_grad = jnp.sum(cross, axis=0, keepdims=True)
    skip_grad = jnp.sum(dconv_f * product_f, axis=1, keepdims=True)
    dmixed = (grad_out * long_conv, dproduct * value, dproduct * key)
    row16 = lax.broadcasted_iota(jnp.int32, (16, 128), 0)
    lane16 = lax.broadcasted_iota(jnp.int32, (16, 128), 1)
    small = jnp.where((lane16 & 15) == 9, skip_grad, 0.0)
    for proj in range(3):
        dfeat = jnp.zeros((16, tokens), F32)
        for k in range(3):
            dfeat = dfeat + column(3 * k + proj) * ahead(dmixed[proj], k)
            short = jnp.sum(dmixed[proj] * feats[proj][k], axis=1, keepdims=True)
            small = jnp.where((lane16 & 15) == 3 * k + proj, short, small)
        dfeat = dfeat.astype(BF16)
        for x in range(4):
            for other in range(4):
                out_ref[2 * x + other // 2, other % 2, proj * 16 : proj * 16 + 16, :] = dfeat[
                    :, 256 * x : 256 * x + 256
                ]
    small_high = small.astype(BF16).astype(F32)
    small_both = jnp.where(lane16 < 16, small_high, small - small_high)
    filter_high = filter_grad.astype(BF16).astype(F32)
    filter_both = jnp.where(
        row16 == 0, filter_high, jnp.where(row16 == 1, filter_grad - filter_high, 0.0)
    )
    extra = jnp.concatenate([filter_both, small_both], axis=1).astype(BF16)
    for i in range(8):
        for side in range(2):
            out_ref[i, side, 48:ROWS, :] = extra


def back_kernel(place, in_ref, w_own, w_prev, w_next, w_far0, w_far1, out_ref, filter_ref, small_ref):
    x = place[0]
    core = place[1]
    columns = []
    for side in range(2):
        of_core = lax.rem(core + side, 2)
        for proj in range(3):
            block = jnp.concatenate(
                [in_ref[i, of_core, proj * 16 : proj * 16 + 16, :] for i in range(8)], axis=0
            )
            columns.append(block.astype(F32).T.astype(BF16))
    rows = jnp.concatenate(columns, axis=1)
    for shift, weight in weight_parts(w_own, w_prev, w_next, w_far0, w_far1):
        block = lax.rem(x + shift, 4)
        table = jnp.concatenate(
            [weight(side, proj) for side in range(2) for proj in range(3)], axis=1
        )
        result = lax.dot_general(
            rows, table, (((1,), (1,)), ((), ())), preferred_element_type=F32
        ).astype(BF16)
        for half in range(2):
            for z in range(4):
                out_ref[block, half, z] = result[
                    half * 128 : half * 128 + 128, z * 128 : z * 128 + 128
                ]
    small = jnp.concatenate([in_ref[i, core, 48:ROWS, 128:256] for i in range(8)], axis=0)
    turned = small.astype(F32).T
    small_ref[...] = turned[0:16] + turned[16:32]
    for i in range(8):
        tile = in_ref[i, core, 48:ROWS, 0:128].astype(F32)
        filter_ref[i : i + 1, :] = tile[0:1] + tile[1:2]


def on_device(tokens, feat_weight, short_taps, long_filter, skip_gain, out_grad):
    x = lax.axis_index("x")
    core = lax.axis_index("core")
    ctx = lax.axis_index(CTX)
    place = jnp.stack([x, core, ctx]).astype(jnp.int32)
    swap = [(2 * a + b, 2 * b + a) for a in range(2) for b in range(2)]
    cores = [(0, 1), (1, 0)]
    up = [(i, (i + 1) % 4) for i in range(4)]
    down = [(i, (i - 1) % 4) for i in range(4)]

    moved = lax.ppermute(tokens, ("yh", "zh"), swap)

    weight = jnp.transpose(feat_weight, (1, 0, 2)).reshape(3, 4, 2, 128, 128)
    kept = lax.dynamic_index_in_dim(weight, core, 2, keepdims=False)
    given = lax.dynamic_index_in_dim(weight, 1 - core, 2, keepdims=False)
    w_own = jnp.stack([kept, lax.ppermute(given, "core", cores)])
    w_prev = lax.ppermute(w_own, "x", up)
    w_next = lax.ppermute(w_own, "x", down)
    w_far0 = lax.ppermute(w_prev[0], "x", up)
    w_far1 = lax.ppermute(w_next[1], "x", down)
    weights = (w_own, w_prev, w_next, w_far0, w_far1)

    grad_t, table, band = pl.pallas_call(
        prepare_kernel,
        out_shape=(
            jax.ShapeDtypeStruct((8, 16, HALF), BF16),
            jax.ShapeDtypeStruct((128, 128), F32),
            jax.ShapeDtypeStruct((4, 128, 128), BF16),
        ),
        in_specs=[SMEM] + [VMEM] * 4,
        out_specs=(VMEM, VMEM, VMEM),
        name="prepare",
    )(place, out_grad, short_taps.reshape(9, 128), skip_gain.reshape(1, 128), long_filter)

    copies = jnp.broadcast_to(moved[None], (32, 128, 128))
    whole = lax.all_to_all(copies, PLANE, 0, 0, tiled=True).reshape(4, 2, 4, 128, 128)

    partial = pl.pallas_call(
        project_kernel,
        out_shape=jax.ShapeDtypeStruct((8, 2, ROWS, 256), BF16),
        in_specs=[SMEM] + [VMEM] * 7,
        out_specs=VMEM,
        compiler_params=params(40),
        cost_estimate=pl.CostEstimate(flops=2 * 256 * 2048 * 768, bytes_accessed=5 << 20, transcendentals=0),
        name="project",
    )(place, whole, *weights, grad_t)
    spread = lax.all_to_all(
        partial.reshape(16, ROWS, 256), ("x", "yh", "core"), 0, 0, tiled=True
    ).reshape(8, 2, ROWS, 256)

    cotangent = pl.pallas_call(
        mixer_kernel,
        out_shape=jax.ShapeDtypeStruct((8, 2, ROWS, 256), BF16),
        in_specs=[SMEM] + [VMEM] * 3,
        out_specs=VMEM,
        compiler_params=params(40),
        name="mixer",
    )(place, spread, table, band)
    gathered = lax.all_to_all(
        cotangent.reshape(16, ROWS, 256), ("x", "yh", "core"), 0, 0, tiled=True
    ).reshape(8, 2, ROWS, 256)

    back, filter_grad, small = pl.pallas_call(
        back_kernel,
        out_shape=(
            jax.ShapeDtypeStruct((4, 2, 4, 128, 128), BF16),
            jax.ShapeDtypeStruct((8, 128), F32),
            jax.ShapeDtypeStruct((16, 128), F32),
        ),
        in_specs=[SMEM] + [VMEM] * 6,
        out_specs=(VMEM, VMEM, VMEM),
        compiler_params=params(40),
        cost_estimate=pl.CostEstimate(flops=2 * 256 * 2048 * 768, bytes_accessed=5 << 20, transcendentals=0),
        name="back",
    )(place, gathered, *weights)
    parts = lax.all_to_all(back.reshape(32, 128, 128), PLANE, 0, 0, tiled=True)
    summed = jnp.sum(parts.astype(F32), axis=0).astype(BF16)
    input_grad = lax.ppermute(summed, ("yh", "zh"), swap)
    return input_grad, filter_grad, small[9], small[:9].reshape(3, 3, 128)


def solution(mesh):
    split = Mesh(np.asarray(mesh.devices).reshape(SIZES), AXES)
    in_specs = (
        P(CTX, TP),
        P(CTX, None, TP),
        P(None, None, TP),
        P(TP, None),
        P(TP),
        P(CTX, TP),
    )
    out_specs = (P(CTX, TP), P(TP, None), P(TP), P(None, None, TP))
    return jax.shard_map(
        on_device, mesh=split, in_specs=in_specs, out_specs=out_specs, check_vma=False
    )
```

time: 632 us -> 174 us (0.28)
  the two profiles are of different devices: /device:TPU:2 before, /device:TPU:48 now
where the time goes in v1:
time: 174 us; the launch traced here: 173 us
  blocking collectives  81.8 us (47%)
  starting transfers between devices  47.2 us (27%)
  waiting for transfers between devices  24.7 us (14%)
  Pallas kernels  9.1 us (5%)
  local copies, waits for them, and re-layouts  8.42 us (5%)
    all_to_all x1, blocking collectives, on_device(): parts = lax.all_to_all(back.reshape(32, 128, 128), PLANE, 0, 0, tiled=True)  39.2 us
    all_to_all x1, blocking collectives, on_device(): lax.all_to_all(partial.reshape(16, ROWS, 256), ('x', 'yh', 'core'), 0, 0,...  23.9 us
    all_to_all x1, blocking collectives, on_device(): lax.all_to_all(cotangent.reshape(16, ROWS, 256), ('x', 'yh', 'core'), 0,...  18.7 us
    ppermute x1, waiting for transfers between devices, on_device(): w_prev = lax.ppermute(w_own, 'x', up)  14.7 us
    ppermute x1, starting transfers between devices, on_device(): moved = lax.ppermute(tokens, ('yh', 'zh'), swap)  12.3 us
    all_to_all x1, starting transfers between devices, on_device(): lax.all_to_all(copies, PLANE, 0, 0, tiled=True).reshape(4, 2, 4, 128, 128)  10.3 us
    ppermute x1, starting transfers between devices, on_device(): input_grad = lax.ppermute(summed, ('yh', 'zh'), swap)  8.66 us
    ppermute x1, waiting for transfers between devices, on_device(): input_grad = lax.ppermute(summed, ('yh', 'zh'), swap)  4.88 us
  transfers between devices with their start and end apart: 8, of which 5 were waited for; matrix products, arithmetic and copies ran while one was open for 3% of the time, Pallas kernels for 1%

profile of v1, /device:TPU:48, one launch (start us, length us, event | category | flops | bytes accessed | tf_op | source)
XLA Modules:
  0.0 172.9 jit_solution(9528905074280149157)
XLA Ops:
  0.6 1.2 dynamic-slice_bitcast_fusion.1
  1.8 1.9 %collective-permute-start.1 = (bf16[3,4,128,128]{3,2,1,0:T(8,128)(2,1)S(1)}, bf16[3,4,128,128]{3,2,1,0:T(8,128)(2,1)S(1)}, u32[]{:S(2)}, u32[]{:S(2)}) collective-permute-start(bf16[3,4,128,128]{3,2,1,0:T(8,128)(2,1)S(1)} %get-tuple-element.17), channel_id=1, source_target_pairs={{0,1},{1,0},{2,3},{3,2},{4,5},{5,4},{6,7},{7,6},{8,9},{9,8},{10,11... | collective-permute-start | bytes 1179656 | tf_op jit(solution)/shard_map/ppermute | solution.py:251
  3.8 12.3 %collective-permute-start = (bf16[128,128]{1,0:T(8,128)(2,1)S(1)}, bf16[128,128]{1,0:T(8,128)(2,1)S(1)}, u32[]{:S(2)}, u32[]{:S(2)}) collective-permute-start(bf16[128,128]{1,0:T(8,128)(2,1)S(1)} %copy-done.5), channel_id=1, source_target_pairs={{0,0},{8,64},{64,8},{72,72},{1,1},{9,65},{65,9},{73,73},{2,2},{10,... | collective-permute-start | bytes 98312 | tf_op jit(solution)/shard_map/ppermute | solution.py:246
  16.0 2.3 %collective-permute-done = bf16[128,128]{1,0:T(8,128)(2,1)S(1)} collective-permute-done((bf16[128,128]{1,0:T(8,128)(2,1)S(1)}, bf16[128,128]{1,0:T(8,128)(2,1)S(1)}, u32[]{:S(2)}, u32[]{:S(2)}) %collective-permute-start) | collective-permute-done | bytes 32800 | tf_op jit(solution)/shard_map/ppermute | solution.py:246
  18.3 1.2 broadcast_in_dim.2
  19.5 10.3 %all-to-all-start = ((bf16[32,128,128]{2,1,0:T(8,128)(2,1)}), bf16[32,128,128]{2,1,0:T(8,128)(2,1)S(1)}, u32[]{:S(2)}, u32[]{:S(2)}) async-start(bf16[32,128,128]{2,1,0:T(8,128)(2,1)} %broadcast_in_dim.2), calls=%async_computation | async-start | bytes 2097152 | tf_op jit(solution)/shard_map/all_to_all | solution.py:271
  29.9 3.4 %collective-permute-start.2 = (bf16[2,3,4,128,128]{4,3,2,1,0:T(8,128)(2,1)S(1)}, bf16[2,3,4,128,128]{4,3,2,1,0:T(8,128)(2,1)S(1)}, u32[]{:S(2)}, u32[]{:S(2)}) collective-permute-start(bf16[2,3,4,128,128]{4,3,2,1,0:T(8,128)(2,1)S(1)} %pad_maximum_fusion.w_own), channel_id=1, source_target_pairs={{0,128},{128,256},{256,384},{384,0},{1,129},{129,257},{257,385},{3... | collective-permute-start | bytes 2359304 | tf_op jit(solution)/shard_map/ppermute | solution.py:252
  33.3 3.7 %collective-permute-start.3 = (bf16[2,3,4,128,128]{4,3,2,1,0:T(8,128)(2,1)S(1)}, bf16[2,3,4,128,128]{4,3,2,1,0:T(8,128)(2,1)S(1)}, u32[]{:S(2)}, u32[]{:S(2)}) collective-permute-start(bf16[2,3,4,128,128]{4,3,2,1,0:T(8,128)(2,1)S(1)} %pad_maximum_fusion.w_own), channel_id=1, source_target_pairs={{0,384},{128,0},{256,128},{384,256},{1,385},{129,1},{257,129},{385... | collective-permute-start | bytes 2359304 | tf_op jit(solution)/shard_map/ppermute | solution.py:253
  36.9 14.7 %collective-permute-done.2.w_prev = bf16[2,3,4,128,128]{4,3,2,1,0:T(8,128)(2,1)S(1)} collective-permute-done((bf16[2,3,4,128,128]{4,3,2,1,0:T(8,128)(2,1)S(1)}, bf16[2,3,4,128,128]{4,3,2,1,0:T(8,128)(2,1)S(1)}, u32[]{:S(2)}, u32[]{:S(2)}) %collective-permute-start.2) | collective-permute-done | bytes 786464 | tf_op jit(solution)/shard_map/ppermute | solution.py:252
  51.6 0.8 slice_bitcast_fusion.1
  52.4 2.2 %collective-permute-start.4 = (bf16[3,4,128,128]{3,2,1,0:T(8,128)(2,1)}, bf16[3,4,128,128]{3,2,1,0:T(8,128)(2,1)}, u32[]{:S(2)}, u32[]{:S(2)}) collective-permute-start(bf16[3,4,128,128]{3,2,1,0:T(8,128)(2,1)} %slice_bitcast_fusion.1), channel_id=1, source_target_pairs={{0,128},{128,256},{256,384},{384,0},{1,129},{129,257},{257,385},{3... | collective-permute-start | bytes 1179656 | tf_op jit(solution)/shard_map/ppermute | solution.py:254
  54.6 0.8 slice_bitcast_fusion
  55.4 4.9 %collective-permute-start.5 = (bf16[3,4,128,128]{3,2,1,0:T(8,128)(2,1)}, bf16[3,4,128,128]{3,2,1,0:T(8,128)(2,1)}, u32[]{:S(2)}, u32[]{:S(2)}) collective-permute-start(bf16[3,4,128,128]{3,2,1,0:T(8,128)(2,1)} %slice_bitcast_fusion), channel_id=1, source_target_pairs={{0,384},{128,0},{256,128},{384,256},{1,385},{129,1},{257,129},{385... | collective-permute-start | bytes 1179656 | tf_op jit(solution)/shard_map/ppermute | solution.py:255
  60.3 0.7 copy-done.4
  61.0 0.6 reshape.42.taps_ref
  61.6 0.7 pad_add_fusion.place
  62.2 2.0 %prepare.1 = (bf16[8,16,128]{2,1,0:T(8,128)(2,1)}, f32[128,128]{1,0:T(8,128)}, bf16[4,128,128]{2,1,0:T(8,128)(2,1)}) custom-call(s32[3]{0:T(128)} %pad_add_fusion.place, bf16[128,128]{1,0:T(8,128)(2,1)} %grad_ref.1, f32[9,128]{1,0:T(8,128)} %reshape.42.taps_ref, f32[1,128]{1,0:T(1,128)} %bitcast.38, f32[8,128]{1,0:T(8,128)} %filter_ref.1), custom_call_target="tpu_custom_call" | custom-call | tf_op jit(solution)/shard_map/prepare/pallas_call | solution.py:258
  64.2 0.9 collective-permute-done.4.w_far0
  65.2 2.0 %collective-permute-done.5.w_far1 = bf16[3,4,128,128]{3,2,1,0:T(8,128)(2,1)} collective-permute-done((bf16[3,4,128,128]{3,2,1,0:T(8,128)(2,1)}, bf16[3,4,128,128]{3,2,1,0:T(8,128)(2,1)}, u32[]{:S(2)}, u32[]{:S(2)}) %collective-permute-start.5) | collective-permute-done | bytes 393248 | tf_op jit(solution)/shard_map/ppermute | solution.py:255
  67.1 0.7 copy-done.3
  67.8 0.8 copy-done.2
  68.6 3.0 %project.1 = bf16[8,2,64,256]{3,2,1,0:T(8,128)(2,1)S(1)} custom-call(s32[3]{0:T(128)S(1)} %copy-done.3, bf16[4,2,4,128,128]{4,3,2,1,0:T(8,128)(2,1)S(1)} %bitcast.29, bf16[2,3,4,128,128]{4,3,2,1,0:T(8,128)(2,1)S(1)} %pad_maximum_fusion.w_own, bf16[2,3,4,128,128]{4,3,2,1,0:T(8,128)(2,1)S(1)} %collective-permute-done.2.w_prev, ...), custom_call_target="tpu_custom_call" | custom-call | flops 805306368 | bytes 5242880 | tf_op jit(solution)/shard_map/project/pallas_call | solution.py:273
  71.6 23.9 %all_to_all.20 = bf16[16,64,256]{2,1,0:T(8,128)(2,1)S(1)} all-to-all(bf16[16,64,256]{2,1,0:T(8,128)(2,1)S(1)} %bitcast.30), channel_id=1, replica_groups=mesh['x'=4,'yh'=2,'yl'=4,'zh'=2,'zl'=4,'core'=2] {'x','yh','core'}, dimensions={0} | all-to-all | bytes 1048576 | tf_op jit(solution)/shard_map/all_to_all | solution.py:282
  95.5 1.4 mixer.1
  96.9 18.7 %all_to_all.21 = bf16[16,64,256]{2,1,0:T(8,128)(2,1)S(1)} all-to-all(bf16[16,64,256]{2,1,0:T(8,128)(2,1)S(1)} %bitcast.32), channel_id=1, replica_groups=mesh['x'=4,'yh'=2,'yl'=4,'zh'=2,'zl'=4,'core'=2] {'x','yh','core'}, dimensions={0} | all-to-all | bytes 1048576 | tf_op jit(solution)/shard_map/all_to_all | solution.py:294
  115.6 2.7 %back.1 = (bf16[4,2,4,128,128]{4,3,2,1,0:T(8,128)(2,1)S(1)}, f32[8,128]{1,0:T(8,128)}, f32[16,128]{1,0:T(8,128)S(1)}) custom-call(s32[3]{0:T(128)S(1)} %copy-done.3, bf16[8,2,64,256]{3,2,1,0:T(8,128)(2,1)S(1)} %bitcast.33, bf16[2,3,4,128,128]{4,3,2,1,0:T(8,128)(2,1)S(1)} %pad_maximum_fusion.w_own, ...), custom_call_target="tpu_custom_call" | custom-call | flops 805306368 | bytes 5242880 | tf_op jit(solution)/shard_map/back/pallas_call | solution.py:298
  118.3 39.2 %all_to_all.22 = bf16[32,128,128]{2,1,0:T(8,128)(2,1)S(1)} all-to-all(bf16[32,128,128]{2,1,0:T(8,128)(2,1)S(1)} %bitcast.34), channel_id=1, replica_groups=mesh['x'=4,'yh'=2,'yl'=4,'zh'=2,'zl'=4,'core'=2] {'yl','zh','zl'}, dimensions={0} | all-to-all | bytes 2097152 | tf_op jit(solution)/shard_map/all_to_all | solution.py:311
  157.7 8.7 %collective-permute-start.6 = (bf16[128,128]{1,0:T(8,128)(2,1)S(1)}, bf16[128,128]{1,0:T(8,128)(2,1)S(1)}, u32[]{:S(2)}, u32[]{:S(2)}) collective-permute-start(bf16[128,128]{1,0:T(8,128)(2,1)S(1)} %reduce_sum.12), channel_id=1, source_target_pairs={{0,0},{8,64},{64,8},{72,72},{1,1},{9,65},{65,9},{73,73},{2,2},{10,... | collective-permute-start | bytes 98312 | tf_op jit(solution)/shard_map/ppermute | solution.py:313
  166.3 0.5 slice_bitcast_fusion.2
  166.8 0.6 reshape.49
  167.4 4.9 %collective-permute-done.6 = bf16[128,128]{1,0:T(8,128)(2,1)S(1)} collective-permute-done((bf16[128,128]{1,0:T(8,128)(2,1)S(1)}, bf16[128,128]{1,0:T(8,128)(2,1)S(1)}, u32[]{:S(2)}, u32[]{:S(2)}) %collective-permute-start.6) | collective-permute-done | bytes 32800 | tf_op jit(solution)/shard_map/ppermute | solution.py:313
  172.3 0.6 copy.15
  (14 shorter events, 0.3 us)
Async XLA Ops:
  0.6 3.1 %copy-start.5 = (bf16[128,128]{1,0:T(8,128)(2,1)S(1)}, bf16[128,128]{1,0:T(8,128)(2,1)}, u32[]{:S(2)}) copy-start(bf16[128,128]{1,0:T(8,128)(2,1)} %param.6) | copy-start | bytes 98308
  1.8 27.9 %collective-permute-start.1 = (bf16[3,4,128,128]{3,2,1,0:T(8,128)(2,1)S(1)}, bf16[3,4,128,128]{3,2,1,0:T(8,128)(2,1)S(1)}, u32[]{:S(2)}, u32[]{:S(2)}) collective-permute-start(bf16[3,4,128,128]{3,2,1,0:T(8,128)(2,1)S(1)} %get-tuple-element.17), channel_id=1, source_target_pairs={{0,1},{1,0},{2,3},{3,2},{4,5},{5,4},{6,7},{7,6},{8,9},{9,8},{10,11... | collective-permute-start | bytes 1179656 | tf_op jit(solution)/shard_map/ppermute | solution.py:251
  3.8 14.5 %collective-permute-start = (bf16[128,128]{1,0:T(8,128)(2,1)S(1)}, bf16[128,128]{1,0:T(8,128)(2,1)S(1)}, u32[]{:S(2)}, u32[]{:S(2)}) collective-permute-start(bf16[128,128]{1,0:T(8,128)(2,1)S(1)} %copy-done.5), channel_id=1, source_target_pairs={{0,0},{8,64},{64,8},{72,72},{1,1},{9,65},{65,9},{73,73},{2,2},{10,... | collective-permute-start | bytes 98312 | tf_op jit(solution)/shard_map/ppermute | solution.py:246
  19.5 47.6 %all-to-all-start = ((bf16[32,128,128]{2,1,0:T(8,128)(2,1)}), bf16[32,128,128]{2,1,0:T(8,128)(2,1)S(1)}, u32[]{:S(2)}, u32[]{:S(2)}) async-start(bf16[32,128,128]{2,1,0:T(8,128)(2,1)} %broadcast_in_dim.2), calls=%async_computation | async-start | bytes 2097152 | tf_op jit(solution)/shard_map/all_to_all | solution.py:271
  29.9 21.8 %collective-permute-start.2 = (bf16[2,3,4,128,128]{4,3,2,1,0:T(8,128)(2,1)S(1)}, bf16[2,3,4,128,128]{4,3,2,1,0:T(8,128)(2,1)S(1)}, u32[]{:S(2)}, u32[]{:S(2)}) collective-permute-start(bf16[2,3,4,128,128]{4,3,2,1,0:T(8,128)(2,1)S(1)} %pad_maximum_fusion.w_own), channel_id=1, source_target_pairs={{0,128},{128,256},{256,384},{384,0},{1,129},{129,257},{257,385},{3... | collective-permute-start | bytes 2359304 | tf_op jit(solution)/shard_map/ppermute | solution.py:252
  33.3 21.3 %collective-permute-start.3 = (bf16[2,3,4,128,128]{4,3,2,1,0:T(8,128)(2,1)S(1)}, bf16[2,3,4,128,128]{4,3,2,1,0:T(8,128)(2,1)S(1)}, u32[]{:S(2)}, u32[]{:S(2)}) collective-permute-start(bf16[2,3,4,128,128]{4,3,2,1,0:T(8,128)(2,1)S(1)} %pad_maximum_fusion.w_own), channel_id=1, source_target_pairs={{0,384},{128,0},{256,128},{384,256},{1,385},{129,1},{257,129},{385... | collective-permute-start | bytes 2359304 | tf_op jit(solution)/shard_map/ppermute | solution.py:253
  52.4 12.7 %collective-permute-start.4 = (bf16[3,4,128,128]{3,2,1,0:T(8,128)(2,1)}, bf16[3,4,128,128]{3,2,1,0:T(8,128)(2,1)}, u32[]{:S(2)}, u32[]{:S(2)}) collective-permute-start(bf16[3,4,128,128]{3,2,1,0:T(8,128)(2,1)} %slice_bitcast_fusion.1), channel_id=1, source_target_pairs={{0,128},{128,256},{256,384},{384,0},{1,129},{129,257},{257,385},{3... | collective-permute-start | bytes 1179656 | tf_op jit(solution)/shard_map/ppermute | solution.py:254
  55.4 11.7 %collective-permute-start.5 = (bf16[3,4,128,128]{3,2,1,0:T(8,128)(2,1)}, bf16[3,4,128,128]{3,2,1,0:T(8,128)(2,1)}, u32[]{:S(2)}, u32[]{:S(2)}) collective-permute-start(bf16[3,4,128,128]{3,2,1,0:T(8,128)(2,1)} %slice_bitcast_fusion), channel_id=1, source_target_pairs={{0,384},{128,0},{256,128},{384,256},{1,385},{129,1},{257,129},{385... | collective-permute-start | bytes 1179656 | tf_op jit(solution)/shard_map/ppermute | solution.py:255
  60.3 0.7 copy-start.4
  67.1 0.7 copy-start.3
  67.8 0.8 copy-start.2
  71.5 24.0 %copy-start = (bf16[4,128,128]{2,1,0:T(8,128)(2,1)S(1)}, bf16[4,128,128]{2,1,0:T(8,128)(2,1)}, u32[]{:S(2)}) copy-start(bf16[4,128,128]{2,1,0:T(8,128)(2,1)} %get-tuple-element.12.band_ref) | copy-start | bytes 393220
  71.6 24.0 %copy-start.1 = (f32[128,128]{1,0:T(8,128)S(1)}, f32[128,128]{1,0:T(8,128)}, u32[]{:S(2)}) copy-start(f32[128,128]{1,0:T(8,128)} %get-tuple-element.11.table_ref) | copy-start | bytes 196612
  157.7 14.7 %collective-permute-start.6 = (bf16[128,128]{1,0:T(8,128)(2,1)S(1)}, bf16[128,128]{1,0:T(8,128)(2,1)S(1)}, u32[]{:S(2)}, u32[]{:S(2)}) collective-permute-start(bf16[128,128]{1,0:T(8,128)(2,1)S(1)} %reduce_sum.12), channel_id=1, source_target_pairs={{0,0},{8,64},{64,8},{72,72},{1,1},{9,65},{65,9},{73,73},{2,2},{10,... | collective-permute-start | bytes 98312 | tf_op jit(solution)/shard_map/ppermute | solution.py:313

commit v2 on v1

v2 whole, which is shorter than its diff:
```python
import jax
import jax.numpy as jnp
import numpy as np
from jax import lax
from jax.experimental import pallas as pl
from jax.experimental.pallas import tpu as pltpu
from jax.sharding import Mesh
from jax.sharding import PartitionSpec as P

AXES = ("x", "yh", "yl", "zh", "zl", "core")
SIZES = (4, 2, 4, 2, 4, 2)
CTX = ("x", "yh")
TP = ("yl", "zh", "zl", "core")
PLANE = ("yl", "zh", "zl")
F32 = jnp.float32
BF16 = jnp.bfloat16
VMEM = pl.BlockSpec(memory_space=pltpu.VMEM)
SMEM = pl.BlockSpec(memory_space=pltpu.SMEM)
ROWS = 112
HALF = 128


def params(mib):
    return pltpu.CompilerParams(vmem_limit_bytes=mib * 1024 * 1024)


def rolled_rows(table, left):
    rows = lax.broadcasted_iota(jnp.int32, table.shape, 0)
    for bit in range(7):
        step = 1 << bit
        turned = pltpu.roll(table, 128 - step if left else step, 1)
        table = jnp.where((rows & step) != 0, turned, table)
    return table


def ctx_index():
    return 2 * lax.axis_index("x") + lax.axis_index("yh")


def copies_kernel(in_ref, out_ref):
    out_ref[...] = jnp.broadcast_to(in_ref[...][None], (32, 128, 128))


def prepare_kernel(grad_ref, taps_ref, skip_ref, filter_ref, grad_t_ref, table_ref, band_ref):
    ctx = ctx_index()
    grad_t_ref[...] = grad_ref[...].astype(F32).T.astype(BF16).reshape(8, 16, HALF)
    rows = jnp.concatenate(
        [taps_ref[...], skip_ref[...], jnp.zeros((118, 128), F32)], axis=0
    )
    table_ref[...] = rows.T
    band = rolled_rows(
        jnp.broadcast_to(filter_ref[pl.ds(ctx, 1), :], (128, 128)), False
    )
    src = lax.broadcasted_iota(jnp.int32, (128, 128), 0)
    dst = lax.broadcasted_iota(jnp.int32, (128, 128), 1)
    near = jnp.where(dst >= src, band, 0.0)
    far = jnp.where(dst < src, band, 0.0)
    for place_at, part in ((0, near), (2, far)):
        high = part.astype(BF16)
        band_ref[place_at] = high
        band_ref[place_at + 1] = (part - high.astype(F32)).astype(BF16)


def weight_rows(weight, proj, side):
    return jnp.concatenate([weight[proj, z, side] for z in range(4)], axis=0)


def project_kernel(own_ref, other_ref, w0, w1, w2, w3, grad_ref, out_ref):
    x = lax.axis_index("x")
    core = lax.axis_index("core")
    totals = [jnp.zeros((256, 128), F32) for _ in range(3)]
    for away, weight in enumerate((w0, w1, w2, w3)):
        block = lax.rem(x + away, 4)
        for ref, side in ((own_ref, core), (other_ref, 1 - core)):
            rows = jnp.concatenate(
                [
                    jnp.concatenate([ref[block, 1 - half, z] for z in range(4)], axis=1)
                    for half in range(2)
                ],
                axis=0,
            )
            for proj in range(3):
                totals[proj] = totals[proj] + jnp.dot(
                    rows, weight_rows(weight, proj, side), preferred_element_type=F32
                )
    for proj in range(3):
        turned = totals[proj].T.astype(BF16)
        for half in range(2):
            start = (2 * proj + half) * 16
            for group in range(8):
                out_ref[group, start : start + 16, :] = turned[
                    group * 16 : group * 16 + 16, half * 128 : half * 128 + 128
                ]
    for group in range(8):
        out_ref[group, 96:ROWS, :] = grad_ref[group]


def mixer_kernel(in_ref, table_ref, band_ref, out_ref):
    ctx = ctx_index()
    tokens = 1024
    lane = lax.broadcasted_iota(jnp.int32, (16, tokens), 1)
    table = table_ref[pl.ds(pl.multiple_of(ctx * 16, 16), 16), :]

    def column(k):
        return table[:, k : k + 1]

    def behind(block, k):
        if k == 0:
            return block
        return jnp.where(lane >= k, pltpu.roll(block, k, 1), 0.0)

    def ahead(block, k):
        if k == 0:
            return block
        return jnp.where(lane < tokens - k, pltpu.roll(block, tokens - k, 1), 0.0)

    def stacked(block):
        return jnp.concatenate([block[:, 128 * b : 128 * b + 128] for b in range(8)], axis=0)

    def flat(block):
        return jnp.concatenate([block[16 * b : 16 * b + 16] for b in range(8)], axis=1)

    grad_out = jnp.concatenate(
        [in_ref[i, 96:ROWS, :] for i in range(8)], axis=1
    ).astype(F32)
    feats = []
    mixed = []
    for proj in range(3):
        pieces = []
        for x in range(4):
            for half in range(2):
                start = (2 * proj + half) * 16
                pieces.append(
                    in_ref[2 * x, start : start + 16, :].astype(F32)
                    + in_ref[2 * x + 1, start : start + 16, :].astype(F32)
                )
        feat = jnp.concatenate(pieces, axis=1).astype(BF16).astype(F32)
        shifted = [behind(feat, k) for k in range(3)]
        feats.append(shifted)
        running = jnp.zeros((16, tokens), F32)
        for k in range(3):
            running = running + column(3 * k + proj) * shifted[k]
        mixed.append(running)
    query, key, value = mixed
    skip = column(9)
    product = (key * value).astype(BF16)
    dconv = (grad_out * query).astype(BF16)
    prod_rows = stacked(product)
    conv_rows = stacked(dconv)
    none = jnp.zeros((16, 128), BF16)
    prod_prev = jnp.concatenate([none, prod_rows[:112]], axis=0)
    conv_next = jnp.concatenate([conv_rows[16:], none], axis=0)
    forward = jnp.zeros((128, 128), F32)
    backward = jnp.zeros((128, 128), F32)
    over_last = (((1,), (1,)), ((), ()))
    over_first = (((0,), (0,)), ((), ()))
    for at, (left, right) in enumerate(
        ((prod_rows, conv_rows), (prod_rows, conv_rows), (prod_prev, conv_next), (prod_prev, conv_next))
    ):
        band = band_ref[at]
        forward = forward + jnp.dot(left, band, preferred_element_type=F32)
        backward = backward + lax.dot_general(right, band, over_last, preferred_element_type=F32)
    product_f = product.astype(F32)
    dconv_f = dconv.astype(F32)
    long_conv = flat(forward) + skip * product_f
    dproduct = flat(backward) + skip * dconv_f
    near = lax.dot_general(prod_rows, conv_rows, over_first, preferred_element_type=F32)
    far = lax.dot_general(prod_prev, conv_rows, over_first, preferred_element_type=F32)
    src = lax.broadcasted_iota(jnp.int32, (128, 128), 0)
    dst = lax.broadcasted_iota(jnp.int32, (128, 128), 1)
    cross = rolled_rows(jnp.where(dst >= src, near, far), True)
    filter_grad = jnp.sum(cross, axis=0, keepdims=True)
    skip_grad = jnp.sum(dconv_f * product_f, axis=1, keepdims=True)
    dmixed = (grad_out * long_conv, dproduct * value, dproduct * key)
    row16 = lax.broadcasted_iota(jnp.int32, (16, 128), 0)
    lane16 = lax.broadcasted_iota(jnp.int32, (16, 128), 1)
    small = jnp.where((lane16 & 15) == 9, skip_grad, 0.0)
    for proj in range(3):
        dfeat = jnp.zeros((16, tokens), F32)
        for k in range(3):
            dfeat = dfeat + column(3 * k + proj) * ahead(dmixed[proj], k)
            short = jnp.sum(dmixed[proj] * feats[proj][k], axis=1, keepdims=True)
            small = jnp.where((lane16 & 15) == 3 * k + proj, short, small)
        dfeat = dfeat.astype(BF16)
        for piece in range(8):
            start = (2 * proj + piece % 2) * 16
            for yh in range(2):
                out_ref[2 * (piece // 2) + yh, start : start + 16, :] = dfeat[
                    :, 128 * piece : 128 * piece + 128
                ]
    small_high = small.astype(BF16).astype(F32)
    small_both = jnp.where(lane16 < 16, small_high, small - small_high)
    filter_high = filter_grad.astype(BF16).astype(F32)
    filter_low = filter_grad - filter_high
    extra = jnp.where(lane16 < 32, small_both, 0.0)
    for at, (part, shift) in enumerate(
        ((filter_high, 0), (filter_low, 0), (filter_high, 32), (filter_low, 32))
    ):
        line = jnp.broadcast_to(part, (16, 128))
        if shift:
            line = pltpu.roll(line, shift, 1)
        extra = jnp.where((row16 == at) & (lane16 >= 32), line, extra)
    extra = extra.astype(BF16)
    for i in range(8):
        out_ref[i, 96:ROWS, :] = extra


def back_kernel(in_ref, w0, w1, w2, w3, own_ref, other_ref, filter_ref, small_ref):
    x = lax.axis_index("x")
    core = lax.axis_index("core")
    halves = []
    for half in range(2):
        columns = []
        for proj in range(3):
            start = (2 * proj + half) * 16
            block = jnp.concatenate([in_ref[i, start : start + 16, :] for i in range(8)], axis=0)
            columns.append(block.astype(F32).T.astype(BF16))
        halves.append(jnp.concatenate(columns, axis=1))
    rows = jnp.concatenate(halves, axis=0)
    for away, weight in enumerate((w0, w1, w2, w3)):
        block = lax.rem(x + away, 4)
        for ref, side in ((own_ref, core), (other_ref, 1 - core)):
            table = jnp.concatenate(
                [weight_rows(weight, proj, side) for proj in range(3)], axis=1
            )
            result = lax.dot_general(
                rows, table, (((1,), (1,)), ((), ())), preferred_element_type=F32
            ).astype(BF16)
            for half in range(2):
                for z in range(4):
                    ref[block, 1 - half, z] = result[
                        half * 128 : half * 128 + 128, z * 128 : z * 128 + 128
                    ]
    extra = [in_ref[i, 96:ROWS, :].astype(F32) for i in range(8)]
    turned = jnp.concatenate(extra, axis=0).T
    small_ref[...] = turned[0:16] + turned[16:32]
    lane = lax.broadcasted_iota(jnp.int32, (1, 128), 1)
    for i in range(8):
        late = extra[i][0:1] + extra[i][1:2]
        early = extra[i][2:3] + extra[i][3:4]
        early = pltpu.roll(jnp.broadcast_to(early, (8, 128)), 96, 1)[0:1]
        filter_ref[i : i + 1, :] = jnp.where(lane < 32, early, late)


def quarter_turn(back):
    route = []
    for yh, zh in np.ndindex(2, 2):
        source, target = 2 * yh + zh, 2 * zh + 1 - yh
        route.append((target, source) if back else (source, target))
    return route


def on_device(tokens, feat_weight, short_taps, long_filter, skip_gain, out_grad):
    pair = [(0, 1), (1, 0)]
    moved = lax.ppermute(tokens, ("yh", "zh"), quarter_turn(False))
    own = jnp.transpose(feat_weight, (1, 0, 2))
    weights = [own] + [
        lax.ppermute(own, "x", [(i, (i - away) % 4) for i in range(4)]) for away in (1, 2, 3)
    ]
    weights = [part.reshape(3, 4, 2, 128, 128) for part in weights]

    out_grad, *weights = lax.optimization_barrier((out_grad, *weights))
    grad_t, table, band = pl.pallas_call(
        prepare_kernel,
        out_shape=(
            jax.ShapeDtypeStruct((8, 16, HALF), BF16),
            jax.ShapeDtypeStruct((128, 128), F32),
            jax.ShapeDtypeStruct((4, 128, 128), BF16),
        ),
        in_specs=[VMEM] * 4,
        out_specs=(VMEM, VMEM, VMEM),
        cost_estimate=pl.CostEstimate(flops=50000000000, bytes_accessed=1048576, transcendentals=0),
        name="prepare",
    )(out_grad, short_taps.reshape(9, 128), skip_gain.reshape(1, 128), long_filter)

    copies = pl.pallas_call(
        copies_kernel,
        out_shape=jax.ShapeDtypeStruct((32, 128, 128), BF16),
        in_specs=[VMEM],
        out_specs=VMEM,
        compiler_params=params(40),
        cost_estimate=pl.CostEstimate(flops=10000000000, bytes_accessed=1 << 20, transcendentals=0),
        name="copies",
    )(moved)
    whole = lax.all_to_all(copies, PLANE, 0, 0, tiled=True).reshape(4, 2, 4, 128, 128)
    whole, grad_t, table, band = lax.optimization_barrier((whole, grad_t, table, band))
    across = lax.ppermute(whole, "core", pair)

    cost = pl.CostEstimate(flops=2 * 256 * 4096 * 384, bytes_accessed=5 << 20, transcendentals=0)
    mixed_shape = jax.ShapeDtypeStruct((8, ROWS, 128), BF16)
    partial = pl.pallas_call(
        project_kernel,
        out_shape=mixed_shape,
        in_specs=[VMEM] * 7,
        out_specs=VMEM,
        compiler_params=params(40),
        cost_estimate=cost,
        name="project",
    )(whole, across, *weights, grad_t)
    spread = lax.all_to_all(partial, CTX, 0, 0, tiled=True)

    cotangent = pl.pallas_call(
        mixer_kernel,
        out_shape=mixed_shape,
        in_specs=[VMEM] * 3,
        out_specs=VMEM,
        compiler_params=params(40),
        name="mixer",
    )(spread, table, band)
    gathered = lax.all_to_all(cotangent, CTX, 0, 0, tiled=True)

    back_shape = jax.ShapeDtypeStruct((4, 2, 4, 128, 128), BF16)
    back_own, back_other, filter_grad, small = pl.pallas_call(
        back_kernel,
        out_shape=(
            back_shape,
            back_shape,
            jax.ShapeDtypeStruct((8, 128), F32),
            jax.ShapeDtypeStruct((16, 128), F32),
        ),
        in_specs=[VMEM] * 5,
        out_specs=(VMEM,) * 4,
        compiler_params=params(40),
        cost_estimate=cost,
        name="back",
    )(gathered, *weights)
    received = lax.ppermute(back_other, "core", pair)
    back = (back_own.astype(F32) + received.astype(F32)).astype(BF16)
    parts = lax.all_to_all(back.reshape(32, 128, 128), PLANE, 0, 0, tiled=True)
    summed = jnp.sum(parts.astype(F32), axis=0).astype(BF16)
    input_grad = lax.ppermute(summed, ("yh", "zh"), quarter_turn(True))
    return input_grad, filter_grad, small[9], small[:9].reshape(3, 3, 128)


def solution(mesh):
    split = Mesh(np.asarray(mesh.devices).reshape(SIZES), AXES)
    in_specs = (
        P(CTX, TP),
        P(CTX, None, TP),
        P(None, None, TP),
        P(TP, None),
        P(TP),
        P(CTX, TP),
    )
    out_specs = (P(CTX, TP), P(TP, None), P(TP), P(None, None, TP))
    return jax.shard_map(
        on_device, mesh=split, in_specs=in_specs, out_specs=out_specs, check_vma=False
    )
```

time: 174 us -> 151 us (0.87)
  the two profiles are of different devices: /device:TPU:48 before, /device:TPU:16 now
where the time goes in v2:
time: 151 us; the launch traced here: 150 us
  blocking collectives  64.3 us (43%)
  starting transfers between devices  36.1 us (24%)
  waiting for transfers between devices  34.6 us (23%)
  Pallas kernels  6.91 us (5%)
  local copies, waits for them, and re-layouts  6.83 us (5%)
    all_to_all x1, blocking collectives, on_device(): parts = lax.all_to_all(back.reshape(32, 128, 128), PLANE, 0, 0, tiled=True)  33.6 us
    ppermute x3, waiting for transfers between devices, on_device(): lax.ppermute(own, 'x', [(i, (i - away) % 4) for i in range(4)])  18.2 us
    all_to_all x1, blocking collectives, on_device(): spread = lax.all_to_all(partial, CTX, 0, 0, tiled=True)  16.8 us
    all_to_all x1, blocking collectives, on_device(): gathered = lax.all_to_all(cotangent, CTX, 0, 0, tiled=True)  13.9 us
    ppermute x1, starting transfers between devices, on_device(): moved = lax.ppermute(tokens, ('yh', 'zh'), quarter_turn(False))  10.9 us
    ppermute x3, starting transfers between devices, on_device(): lax.ppermute(own, 'x', [(i, (i - away) % 4) for i in range(4)])  10.8 us
    all_to_all x1, starting transfers between devices, on_device(): lax.all_to_all(copies, PLANE, 0, 0, tiled=True).reshape(4, 2, 4, 128, 128)  8.1 us
    ppermute x1, waiting for transfers between devices, on_device(): input_grad = lax.ppermute(summed, ('yh', 'zh'), quarter_turn(True))  6.14 us
  transfers between devices with their start and end apart: 8, of which 6 were waited for; matrix products, arithmetic and copies ran while one was open for 2% of the time, Pallas kernels for 2%

profile of v2, /device:TPU:16, one launch (start us, length us, event | category | flops | bytes accessed | tf_op | source)
XLA Modules:
  0.0 149.9 jit_solution(15904017293992455939)
XLA Ops:
  0.6 10.9 %collective-permute-start = (bf16[128,128]{1,0:T(8,128)(2,1)}, bf16[128,128]{1,0:T(8,128)(2,1)S(1)}, u32[]{:S(2)}, u32[]{:S(2)}) collective-permute-start(bf16[128,128]{1,0:T(8,128)(2,1)} %param.6), channel_id=1, source_target_pairs={{0,8},{8,72},{64,0},{72,64},{1,9},{9,73},{65,1},{73,65},{2,10},{10... | collective-permute-start | bytes 98312 | tf_op jit(solution)/shard_map/ppermute | solution.py:255
  11.6 4.9 %collective-permute-start.2 = (bf16[3,1024,128]{2,1,0:T(8,128)(2,1)}, bf16[3,1024,128]{2,1,0:T(8,128)(2,1)S(1)}, u32[]{:S(2)}, u32[]{:S(2)}) collective-permute-start(bf16[3,1024,128]{2,1,0:T(8,128)(2,1)} %bitcast.14), channel_id=1, source_target_pairs={{0,256},{128,384},{256,0},{384,128},{1,257},{129,385},{257,1},{385... | collective-permute-start | bytes 2359304 | tf_op jit(solution)/shard_map/ppermute | solution.py:258
  16.5 3.1 %collective-permute-start.1 = (bf16[3,1024,128]{2,1,0:T(8,128)(2,1)}, bf16[3,1024,128]{2,1,0:T(8,128)(2,1)S(1)}, u32[]{:S(2)}, u32[]{:S(2)}) collective-permute-start(bf16[3,1024,128]{2,1,0:T(8,128)(2,1)} %bitcast.15), channel_id=1, source_target_pairs={{0,384},{128,0},{256,128},{384,256},{1,385},{129,1},{257,129},{385... | collective-permute-start | bytes 2359304 | tf_op jit(solution)/shard_map/ppermute | solution.py:258
  19.6 2.8 %collective-permute-start.3 = (bf16[3,1024,128]{2,1,0:T(8,128)(2,1)}, bf16[3,1024,128]{2,1,0:T(8,128)(2,1)S(1)}, u32[]{:S(2)}, u32[]{:S(2)}) collective-permute-start(bf16[3,1024,128]{2,1,0:T(8,128)(2,1)} %bitcast.16), channel_id=1, source_target_pairs={{0,128},{128,256},{256,384},{384,0},{1,129},{129,257},{257,385},{3... | collective-permute-start | bytes 2359304 | tf_op jit(solution)/shard_map/ppermute | solution.py:258
  22.4 1.3 reshape.40.taps_ref
  23.7 0.2 copies.1
  23.9 1.0 copy-done.4
  24.9 8.1 %all-to-all-start = ((bf16[32,128,128]{2,1,0:T(8,128)(2,1)}), bf16[32,128,128]{2,1,0:T(8,128)(2,1)S(1)}, u32[]{:S(2)}, u32[]{:S(2)}) async-start(bf16[32,128,128]{2,1,0:T(8,128)(2,1)} %copy-done.4), calls=%async_computation | async-start | bytes 2097152 | tf_op jit(solution)/shard_map/all_to_all | solution.py:285
  33.0 2.7 %collective-permute-done.2 = bf16[3,1024,128]{2,1,0:T(8,128)(2,1)S(1)} collective-permute-done((bf16[3,1024,128]{2,1,0:T(8,128)(2,1)}, bf16[3,1024,128]{2,1,0:T(8,128)(2,1)S(1)}, u32[]{:S(2)}, u32[]{:S(2)}) %collective-permute-start.2) | collective-permute-done | bytes 786464 | tf_op jit(solution)/shard_map/ppermute | solution.py:258
  35.7 15.5 %collective-permute-done.1 = bf16[3,1024,128]{2,1,0:T(8,128)(2,1)S(1)} collective-permute-done((bf16[3,1024,128]{2,1,0:T(8,128)(2,1)}, bf16[3,1024,128]{2,1,0:T(8,128)(2,1)S(1)}, u32[]{:S(2)}, u32[]{:S(2)}) %collective-permute-start.1) | collective-permute-done | bytes 786464 | tf_op jit(solution)/shard_map/ppermute | solution.py:258
  51.2 0.9 copy-done.1
  52.1 2.1 %prepare.1 = (bf16[8,16,128]{2,1,0:T(8,128)(2,1)}, f32[128,128]{1,0:T(8,128)}, bf16[4,128,128]{2,1,0:T(8,128)(2,1)}) custom-call(bf16[128,128]{1,0:T(8,128)(2,1)} %grad_ref, f32[9,128]{1,0:T(8,128)} %reshape.40.taps_ref, f32[1,128]{1,0:T(1,128)} %bitcast.27, f32[8,128]{1,0:T(8,128)} %filter_ref.1), custom_call_target="tpu_custom_call" | custom-call | flops 49999998976 | bytes 1048576 | tf_op jit(solution)/shard_map/prepare/pallas_call | solution.py:263
  54.2 5.0 %all-to-all-done = bf16[32,128,128]{2,1,0:T(8,128)(2,1)S(1)} async-done(((bf16[32,128,128]{2,1,0:T(8,128)(2,1)}), bf16[32,128,128]{2,1,0:T(8,128)(2,1)S(1)}, u32[]{:S(2)}, u32[]{:S(2)}) %all-to-all-start) | async-done | bytes 1048608 | tf_op jit(solution)/shard_map/all_to_all | solution.py:285
  59.2 1.9 %collective-permute-start.4 = (bf16[4,2,4,128,128]{4,3,2,1,0:T(8,128)(2,1)S(1)}, bf16[4,2,4,128,128]{4,3,2,1,0:T(8,128)(2,1)S(1)}, u32[]{:S(2)}, u32[]{:S(2)}) collective-permute-start(bf16[4,2,4,128,128]{4,3,2,1,0:T(8,128)(2,1)S(1)} %bitcast.12), channel_id=1, source_target_pairs={{0,1},{1,0},{2,3},{3,2},{4,5},{5,4},{6,7},{7,6},{8,9},{9,8},{10,11... | collective-permute-start | bytes 3145736 | tf_op jit(solution)/shard_map/ppermute | solution.py:287
  61.1 2.6 %collective-permute-done.4.other_ref = bf16[4,2,4,128,128]{4,3,2,1,0:T(8,128)(2,1)S(1)} collective-permute-done((bf16[4,2,4,128,128]{4,3,2,1,0:T(8,128)(2,1)S(1)}, bf16[4,2,4,128,128]{4,3,2,1,0:T(8,128)(2,1)S(1)}, u32[]{:S(2)}, u32[]{:S(2)}) %collective-permute-start.4) | collective-permute-done | bytes 1048608 | tf_op jit(solution)/shard_map/ppermute | solution.py:287
  63.8 1.1 copy-done.2
  64.9 0.8 copy-done.7
  65.7 1.9 %project.1 = bf16[8,112,128]{2,1,0:T(8,128)(2,1)S(1)} custom-call(bf16[4,2,4,128,128]{4,3,2,1,0:T(8,128)(2,1)S(1)} %bitcast.13, bf16[4,2,4,128,128]{4,3,2,1,0:T(8,128)(2,1)S(1)} %collective-permute-done.4.other_ref, bf16[3,4,2,128,128]{4,3,2,1,0:T(8,128)(2,1)S(1)} %bitcast.17, bf16[3,4,2,128,128]{4,3,2,1,0:T(8,128)(2,1)S(1)} %bitcast.21, ...), custom_call_target="tpu_custom_call" | custom-call | flops 805306368 | bytes 5242880 | tf_op jit(solution)/shard_map/project/pallas_call | solution.py:291
  67.5 16.8 %all_to_all.20.in_ref = bf16[8,112,128]{2,1,0:T(8,128)(2,1)S(1)} all-to-all(bf16[8,112,128]{2,1,0:T(8,128)(2,1)S(1)} %project.1), channel_id=1, replica_groups=mesh['x'=4,'yh'=2,'yl'=4,'zh'=2,'zl'=4,'core'=2] {'x','yh'}, dimensions={0} | all-to-all | bytes 458752 | tf_op jit(solution)/shard_map/all_to_all | solution.py:300
  84.3 0.9 mixer.1
  85.3 13.9 %all_to_all.21.in_ref = bf16[8,112,128]{2,1,0:T(8,128)(2,1)S(1)} all-to-all(bf16[8,112,128]{2,1,0:T(8,128)(2,1)S(1)} %mixer.1), channel_id=1, replica_groups=mesh['x'=4,'yh'=2,'yl'=4,'zh'=2,'zl'=4,'core'=2] {'x','yh'}, dimensions={0} | all-to-all | bytes 458752 | tf_op jit(solution)/shard_map/all_to_all | solution.py:310
  99.2 1.8 %back.1 = (bf16[4,2,4,128,128]{4,3,2,1,0:T(8,128)(2,1)S(1)}, bf16[4,2,4,128,128]{4,3,2,1,0:T(8,128)(2,1)S(1)}, f32[8,128]{1,0:T(8,128)}, f32[16,128]{1,0:T(8,128)S(1)}) custom-call(bf16[8,112,128]{2,1,0:T(8,128)(2,1)S(1)} %all_to_all.21.in_ref, bf16[3,4,2,128,128]{4,3,2,1,0:T(8,128)(2,1)S(1)} %bitcast.18, bf16[3,4,2,128,128]{4,3,2,1,0:T(8,128)(2,1)S(1)} %bitcast.22, ...), custom_call_target="tpu_custom_call" | custom-call | flops 805306368 | bytes 5242880 | tf_op jit(solution)/shard_map/back/pallas_call | solution.py:313
  101.0 1.9 %collective-permute-start.5 = (bf16[4,2,4,128,128]{4,3,2,1,0:T(8,128)(2,1)S(1)}, bf16[4,2,4,128,128]{4,3,2,1,0:T(8,128)(2,1)S(1)}, u32[]{:S(2)}, u32[]{:S(2)}) collective-permute-start(bf16[4,2,4,128,128]{4,3,2,1,0:T(8,128)(2,1)S(1)} %get-tuple-element.33), channel_id=1, source_target_pairs={{0,1},{1,0},{2,3},{3,2},{4,5},{5,4},{6,7},{7,6},{8,9},{9,8},{10,11... | collective-permute-start | bytes 3145736 | tf_op jit(solution)/shard_map/ppermute | solution.py:327
  102.9 2.6 %collective-permute-done.5 = bf16[4,2,4,128,128]{4,3,2,1,0:T(8,128)(2,1)S(1)} collective-permute-done((bf16[4,2,4,128,128]{4,3,2,1,0:T(8,128)(2,1)S(1)}, bf16[4,2,4,128,128]{4,3,2,1,0:T(8,128)(2,1)S(1)}, u32[]{:S(2)}, u32[]{:S(2)}) %collective-permute-start.5) | collective-permute-done | bytes 1048608 | tf_op jit(solution)/shard_map/ppermute | solution.py:327
  105.5 0.4 add_convert_fusion
  105.9 33.6 %all_to_all.22 = bf16[32,128,128]{2,1,0:T(8,128)(2,1)S(1)} all-to-all(bf16[32,128,128]{2,1,0:T(8,128)(2,1)S(1)} %bitcast.26), channel_id=1, replica_groups=mesh['x'=4,'yh'=2,'yl'=4,'zh'=2,'zl'=4,'core'=2] {'yl','zh','zl'}, dimensions={0} | all-to-all | bytes 2097152 | tf_op jit(solution)/shard_map/all_to_all | solution.py:329
  139.4 0.2 reduce_sum.12
  139.6 2.5 %collective-permute-start.6 = (bf16[128,128]{1,0:T(8,128)(2,1)S(1)}, bf16[128,128]{1,0:T(8,128)(2,1)S(1)}, u32[]{:S(2)}, u32[]{:S(2)}) collective-permute-start(bf16[128,128]{1,0:T(8,128)(2,1)S(1)} %reduce_sum.12), channel_id=1, source_target_pairs={{8,0},{72,8},{0,64},{64,72},{9,1},{73,9},{1,65},{65,73},{10,2},{74... | collective-permute-start | bytes 98312 | tf_op jit(solution)/shard_map/ppermute | solution.py:331
  142.1 0.5 slice_bitcast_fusion
  142.6 0.6 reshape.43
  143.2 6.1 %collective-permute-done.6 = bf16[128,128]{1,0:T(8,128)(2,1)S(1)} collective-permute-done((bf16[128,128]{1,0:T(8,128)(2,1)S(1)}, bf16[128,128]{1,0:T(8,128)(2,1)S(1)}, u32[]{:S(2)}, u32[]{:S(2)}) %collective-permute-start.6) | collective-permute-done | bytes 32800 | tf_op jit(solution)/shard_map/ppermute | solution.py:331
  149.3 0.6 copy.11
  (14 shorter events, 0.0 us)
Async XLA Ops:
  0.6 23.0 %collective-permute-start = (bf16[128,128]{1,0:T(8,128)(2,1)}, bf16[128,128]{1,0:T(8,128)(2,1)S(1)}, u32[]{:S(2)}, u32[]{:S(2)}) collective-permute-start(bf16[128,128]{1,0:T(8,128)(2,1)} %param.6), channel_id=1, source_target_pairs={{0,8},{8,72},{64,0},{72,64},{1,9},{9,73},{65,1},{73,65},{2,10},{10... | collective-permute-start | bytes 98312 | tf_op jit(solution)/shard_map/ppermute | solution.py:255
  11.6 24.1 %collective-permute-start.2 = (bf16[3,1024,128]{2,1,0:T(8,128)(2,1)}, bf16[3,1024,128]{2,1,0:T(8,128)(2,1)S(1)}, u32[]{:S(2)}, u32[]{:S(2)}) collective-permute-start(bf16[3,1024,128]{2,1,0:T(8,128)(2,1)} %bitcast.14), channel_id=1, source_target_pairs={{0,256},{128,384},{256,0},{384,128},{1,257},{129,385},{257,1},{385... | collective-permute-start | bytes 2359304 | tf_op jit(solution)/shard_map/ppermute | solution.py:258
  16.5 34.7 %collective-permute-start.1 = (bf16[3,1024,128]{2,1,0:T(8,128)(2,1)}, bf16[3,1024,128]{2,1,0:T(8,128)(2,1)S(1)}, u32[]{:S(2)}, u32[]{:S(2)}) collective-permute-start(bf16[3,1024,128]{2,1,0:T(8,128)(2,1)} %bitcast.15), channel_id=1, source_target_pairs={{0,384},{128,0},{256,128},{384,256},{1,385},{129,1},{257,129},{385... | collective-permute-start | bytes 2359304 | tf_op jit(solution)/shard_map/ppermute | solution.py:258
  19.6 31.6 %collective-permute-start.3 = (bf16[3,1024,128]{2,1,0:T(8,128)(2,1)}, bf16[3,1024,128]{2,1,0:T(8,128)(2,1)S(1)}, u32[]{:S(2)}, u32[]{:S(2)}) collective-permute-start(bf16[3,1024,128]{2,1,0:T(8,128)(2,1)} %bitcast.16), channel_id=1, source_target_pairs={{0,128},{128,256},{256,384},{384,0},{1,129},{129,257},{257,385},{3... | collective-permute-start | bytes 2359304 | tf_op jit(solution)/shard_map/ppermute | solution.py:258
  23.9 1.0 copy-start.4
  24.9 34.3 %all-to-all-start = ((bf16[32,128,128]{2,1,0:T(8,128)(2,1)}), bf16[32,128,128]{2,1,0:T(8,128)(2,1)S(1)}, u32[]{:S(2)}, u32[]{:S(2)}) async-start(bf16[32,128,128]{2,1,0:T(8,128)(2,1)} %copy-done.4), calls=%async_computation | async-start | bytes 2097152 | tf_op jit(solution)/shard_map/all_to_all | solution.py:285
  51.2 0.9 copy-start.1
  52.1 11.7 %copy-start = (bf16[1024,3,128]{2,0,1:T(8,128)(2,1)S(1)}, bf16[1024,3,128]{2,0,1:T(8,128)(2,1)}, u32[]{:S(2)}) copy-start(bf16[1024,3,128]{2,0,1:T(8,128)(2,1)} %param.7) | copy-start | bytes 2359300
  59.2 4.5 %collective-permute-start.4 = (bf16[4,2,4,128,128]{4,3,2,1,0:T(8,128)(2,1)S(1)}, bf16[4,2,4,128,128]{4,3,2,1,0:T(8,128)(2,1)S(1)}, u32[]{:S(2)}, u32[]{:S(2)}) collective-permute-start(bf16[4,2,4,128,128]{4,3,2,1,0:T(8,128)(2,1)S(1)} %bitcast.12), channel_id=1, source_target_pairs={{0,1},{1,0},{2,3},{3,2},{4,5},{5,4},{6,7},{7,6},{8,9},{9,8},{10,11... | collective-permute-start | bytes 3145736 | tf_op jit(solution)/shard_map/ppermute | solution.py:287
  63.8 1.1 copy-start.2
  64.9 0.8 copy-start.7
  65.7 18.7 %copy-start.5 = (bf16[4,128,128]{2,1,0:T(8,128)(2,1)S(1)}, bf16[4,128,128]{2,1,0:T(8,128)(2,1)}, u32[]{:S(2)}) copy-start(bf16[4,128,128]{2,1,0:T(8,128)(2,1)} %get-tuple-element.31.band_ref) | copy-start | bytes 393220
  65.7 18.7 %copy-start.6 = (f32[128,128]{1,0:T(8,128)S(1)}, f32[128,128]{1,0:T(8,128)}, u32[]{:S(2)}) copy-start(f32[128,128]{1,0:T(8,128)} %get-tuple-element.30.table_ref) | copy-start | bytes 196612
  67.5 31.7 %copy-start.3 = (bf16[3,1024,128]{2,1,0:T(8,128)(2,1)S(1)}, bf16[3,1024,128]{2,1,0:T(8,128)(2,1)}, u32[]{:S(2)}) copy-start(bf16[3,1024,128]{2,1,0:T(8,128)(2,1)} %copy-done.1) | copy-start | bytes 2359300
  101.0 4.5 %collective-permute-start.5 = (bf16[4,2,4,128,128]{4,3,2,1,0:T(8,128)(2,1)S(1)}, bf16[4,2,4,128,128]{4,3,2,1,0:T(8,128)(2,1)S(1)}, u32[]{:S(2)}, u32[]{:S(2)}) collective-permute-start(bf16[4,2,4,128,128]{4,3,2,1,0:T(8,128)(2,1)S(1)} %get-tuple-element.33), channel_id=1, source_target_pairs={{0,1},{1,0},{2,3},{3,2},{4,5},{5,4},{6,7},{7,6},{8,9},{9,8},{10,11... | collective-permute-start | bytes 3145736 | tf_op jit(solution)/shard_map/ppermute | solution.py:327
  139.6 9.7 %collective-permute-start.6 = (bf16[128,128]{1,0:T(8,128)(2,1)S(1)}, bf16[128,128]{1,0:T(8,128)(2,1)S(1)}, u32[]{:S(2)}, u32[]{:S(2)}) collective-permute-start(bf16[128,128]{1,0:T(8,128)(2,1)S(1)} %reduce_sum.12), channel_id=1, source_target_pairs={{8,0},{72,8},{0,64},{64,72},{9,1},{73,9},{1,65},{65,73},{10,2},{74... | collective-permute-start | bytes 98312 | tf_op jit(solution)/shard_map/ppermute | solution.py:331

commit v3 on v2

--- a/solution.py
+++ b/solution.py
@@ -7,11 +7,14 @@
 from jax.sharding import Mesh
 from jax.sharding import PartitionSpec as P
 
-AXES = ("x", "yh", "yl", "zh", "zl", "core")
-SIZES = (4, 2, 4, 2, 4, 2)
-CTX = ("x", "yh")
-TP = ("yl", "zh", "zl", "core")
-PLANE = ("yl", "zh", "zl")
+AXES = ("xh", "xl", "yh", "ylh", "yll", "zh", "z2", "zp", "core")
+SIZES = (2,) * 9
+X = ("xh", "xl")
+CTX = ("xh", "xl", "yh")
+TP = ("ylh", "yll", "zh", "z2", "zp", "core")
+SPREAD = ("ylh", "yll", "zh", "z2", "zp")
+RETURN = ("xh", "xl", "yh", "zp")
+COLUMNS = ("ylh", "yll", "zh", "z2")
 F32 = jnp.float32
 BF16 = jnp.bfloat16
 VMEM = pl.BlockSpec(memory_space=pltpu.VMEM)
@@ -33,8 +36,18 @@
     return table
 
 
+def x_index():
+    return 2 * lax.axis_index("xh") + lax.axis_index("xl")
+
+
 def ctx_index():
-    return 2 * lax.axis_index("x") + lax.axis_index("yh")
+    return 2 * x_index() + lax.axis_index("yh")
+
+
+def block_place(away, z):
+    high = lax.axis_index("xh") ^ away
+    odd = lax.axis_index("xl") ^ lax.axis_index("zp") ^ away ^ 1
+    return high, odd ^ (z % 2), z // 2
 
 
 def copies_kernel(in_ref, out_ref):
@@ -45,7 +58,7 @@
     ctx = ctx_index()
     grad_t_ref[...] = grad_ref[...].astype(F32).T.astype(BF16).reshape(8, 16, HALF)
     rows = jnp.concatenate(
-        [taps_ref[...], skip_ref[...], jnp.zeros((118, 128), F32)], axis=0
+        [taps_ref[0], taps_ref[1], taps_ref[2], skip_ref[...], jnp.zeros((118, 128), F32)], axis=0
     )
     table_ref[...] = rows.T
     band = rolled_rows(
@@ -66,11 +79,11 @@
 
 
 def project_kernel(own_ref, other_ref, w0, w1, w2, w3, grad_ref, out_ref):
-    x = lax.axis_index("x")
+    x = x_index()
     core = lax.axis_index("core")
     totals = [jnp.zeros((256, 128), F32) for _ in range(3)]
     for away, weight in enumerate((w0, w1, w2, w3)):
-        block = lax.rem(x + away, 4)
+        block = x ^ away
         for ref, side in ((own_ref, core), (other_ref, 1 - core)):
             rows = jnp.concatenate(
                 [
@@ -182,12 +195,13 @@
             short = jnp.sum(dmixed[proj] * feats[proj][k], axis=1, keepdims=True)
             small = jnp.where((lane16 & 15) == 3 * k + proj, short, small)
         dfeat = dfeat.astype(BF16)
-        for piece in range(8):
-            start = (2 * proj + piece % 2) * 16
-            for yh in range(2):
-                out_ref[2 * (piece // 2) + yh, start : start + 16, :] = dfeat[
-                    :, 128 * piece : 128 * piece + 128
-                ]
+        for ctx_to in range(8):
+            xh, xl = ctx_to // 4, ctx_to // 2 % 2
+            for zp in range(2):
+                for yh in range(2):
+                    piece = 128 * (4 * xh + 2 * (zp ^ xl) + yh)
+                    start = (2 * proj + yh) * 16
+                    out_ref[ctx_to, zp, start : start + 16, :] = dfeat[:, piece : piece + 128]
     small_high = small.astype(BF16).astype(F32)
     small_both = jnp.where(lane16 < 16, small_high, small - small_high)
     filter_high = filter_grad.astype(BF16).astype(F32)
@@ -202,36 +216,47 @@
         extra = jnp.where((row16 == at) & (lane16 >= 32), line, extra)
     extra = extra.astype(BF16)
     for i in range(8):
-        out_ref[i, 96:ROWS, :] = extra
-
-
-def back_kernel(in_ref, w0, w1, w2, w3, own_ref, other_ref, filter_ref, small_ref):
-    x = lax.axis_index("x")
+        for zp in range(2):
+            out_ref[i, zp, 96:ROWS, :] = extra
+
+
+def back_kernel(in_ref, w_own, w_x, w_z, own_ref, other_ref, filter_ref, small_ref):
+    zp = lax.axis_index("zp")
     core = lax.axis_index("core")
+    weights = ((w_own, w_z.at[0]), (w_x, w_z.at[1]))
     halves = []
     for half in range(2):
         columns = []
-        for proj in range(3):
-            start = (2 * proj + half) * 16
-            block = jnp.concatenate([in_ref[i, start : start + 16, :] for i in range(8)], axis=0)
-            columns.append(block.astype(F32).T.astype(BF16))
+        for over in range(2):
+            of_z = zp ^ over
+            for proj in range(3):
+                start = (2 * proj + half) * 16
+                block = jnp.concatenate(
+                    [in_ref[i, of_z, start : start + 16, :] for i in range(8)], axis=0
+                )
+                columns.append(block.astype(F32).T.astype(BF16))
         halves.append(jnp.concatenate(columns, axis=1))
     rows = jnp.concatenate(halves, axis=0)
-    for away, weight in enumerate((w0, w1, w2, w3)):
-        block = lax.rem(x + away, 4)
+    for away in range(2):
         for ref, side in ((own_ref, core), (other_ref, 1 - core)):
             table = jnp.concatenate(
-                [weight_rows(weight, proj, side) for proj in range(3)], axis=1
+                [
+                    weight_rows(weight, proj, side)
+                    for weight in weights[away]
+                    for proj in range(3)
+                ],
+                axis=1,
             )
             result = lax.dot_general(
                 rows, table, (((1,), (1,)), ((), ())), preferred_element_type=F32
             ).astype(BF16)
             for half in range(2):
                 for z in range(4):
-                    ref[block, 1 - half, z] = result[
+                    high, low, z2 = block_place(away, z)
+                    ref[high, low, 1 - half, z2] = result[
                         half * 128 : half * 128 + 128, z * 128 : z * 128 + 128
                     ]
-    extra = [in_ref[i, 96:ROWS, :].astype(F32) for i in range(8)]
+    extra = [in_ref[i, zp, 96:ROWS, :].astype(F32) for i in range(8)]
     turned = jnp.concatenate(extra, axis=0).T
     small_ref[...] = turned[0:16] + turned[16:32]
     lane = lax.broadcasted_iota(jnp.int32, (1, 128), 1)
@@ -242,24 +267,39 @@
         filter_ref[i : i + 1, :] = jnp.where(lane < 32, early, late)
 
 
-def quarter_turn(back):
+QUARTER_TURN = [(0, 1), (1, 3), (2, 0), (3, 2)]
+
+
+def flat_index(bits):
+    at = 0
+    for bit in bits:
+        at = 2 * at + bit
+    return at
+
+
+def grad_route():
     route = []
-    for yh, zh in np.ndindex(2, 2):
-        source, target = 2 * yh + zh, 2 * zh + 1 - yh
-        route.append((target, source) if back else (source, target))
+    for xh, xl, yh, ylh, yll, zh, z2, zp, c in np.ndindex(SIZES):
+        source = flat_index((xh, xl, yh, ylh, yll, zh, z2, zp, c))
+        low = xh ^ ylh ^ yll
+        moved = low ^ xl
+        target = flat_index((xh, low, zh, ylh, yll ^ zp ^ moved ^ 1, 1 - yh, z2, moved, c))
+        route.append((target, source))
     return route
 
 
 def on_device(tokens, feat_weight, short_taps, long_filter, skip_gain, out_grad):
     pair = [(0, 1), (1, 0)]
-    moved = lax.ppermute(tokens, ("yh", "zh"), quarter_turn(False))
+    moved = lax.ppermute(tokens, ("yh", "zh"), QUARTER_TURN)
     own = jnp.transpose(feat_weight, (1, 0, 2))
+    moved, late = lax.optimization_barrier((moved, own))
     weights = [own] + [
-        lax.ppermute(own, "x", [(i, (i - away) % 4) for i in range(4)]) for away in (1, 2, 3)
+        lax.ppermute(part, X, [(i, i ^ away) for i in range(4)])
+        for part, away in ((late, 1), (own, 2), (own, 3))
     ]
-    weights = [part.reshape(3, 4, 2, 128, 128) for part in weights]
-
-    out_grad, *weights = lax.optimization_barrier((out_grad, *weights))
+    w_z = lax.ppermute(jnp.stack([own, weights[3]]), "zp", pair)
+
+    out_grad, weights[2], weights[3] = lax.optimization_barrier((out_grad, weights[2], weights[3]))
     grad_t, table, band = pl.pallas_call(
         prepare_kernel,
         out_shape=(
@@ -269,10 +309,11 @@
         ),
         in_specs=[VMEM] * 4,
         out_specs=(VMEM, VMEM, VMEM),
-        cost_estimate=pl.CostEstimate(flops=50000000000, bytes_accessed=1048576, transcendentals=0),
+        cost_estimate=pl.CostEstimate(flops=20000000000, bytes_accessed=1048576, transcendentals=0),
         name="prepare",
-    )(out_grad, short_taps.reshape(9, 128), skip_gain.reshape(1, 128), long_filter)
-
+    )(out_grad, short_taps, skip_gain.reshape(1, 128), long_filter)
+
+    weights = [part.reshape(3, 4, 2, 128, 128) for part in weights]
     copies = pl.pallas_call(
         copies_kernel,
         out_shape=jax.ShapeDtypeStruct((32, 128, 128), BF16),
@@ -282,8 +323,10 @@
         cost_estimate=pl.CostEstimate(flops=10000000000, bytes_accessed=1 << 20, transcendentals=0),
         name="copies",
     )(moved)
-    whole = lax.all_to_all(copies, PLANE, 0, 0, tiled=True).reshape(4, 2, 4, 128, 128)
-    whole, grad_t, table, band = lax.optimization_barrier((whole, grad_t, table, band))
+    whole = lax.all_to_all(copies, SPREAD, 0, 0, tiled=True).reshape(4, 2, 4, 128, 128)
+    whole, grad_t, table, band, weights[1] = lax.optimization_barrier(
+        (whole, grad_t, table, band, weights[1])
+    )
     across = lax.ppermute(whole, "core", pair)
 
     cost = pl.CostEstimate(flops=2 * 256 * 4096 * 384, bytes_accessed=5 << 20, transcendentals=0)
@@ -301,15 +344,17 @@
 
     cotangent = pl.pallas_call(
         mixer_kernel,
-        out_shape=mixed_shape,
+        out_shape=jax.ShapeDtypeStruct((8, 2, ROWS, 128), BF16),
         in_specs=[VMEM] * 3,
         out_specs=VMEM,
         compiler_params=params(40),
         name="mixer",
     )(spread, table, band)
-    gathered = lax.all_to_all(cotangent, CTX, 0, 0, tiled=True)
-
-    back_shape = jax.ShapeDtypeStruct((4, 2, 4, 128, 128), BF16)
+    gathered = lax.all_to_all(
+        cotangent.reshape(16, ROWS, 128), RETURN, 0, 0, tiled=True
+    ).reshape(8, 2, ROWS, 128)
+
+    back_shape = jax.ShapeDtypeStruct((2, 2, 2, 2, 128, 128), BF16)
     back_own, back_other, filter_grad, small = pl.pallas_call(
         back_kernel,
         out_shape=(
@@ -318,17 +363,17 @@
             jax.ShapeDtypeStruct((8, 128), F32),
             jax.ShapeDtypeStruct((16, 128), F32),
         ),
-        in_specs=[VMEM] * 5,
+        in_specs=[VMEM] * 4,
         out_specs=(VMEM,) * 4,
         compiler_params=params(40),
         cost_estimate=cost,
         name="back",
-    )(gathered, *weights)
+    )(gathered, weights[0], weights[3], w_z.reshape(2, 3, 4, 2, 128, 128))
     received = lax.ppermute(back_other, "core", pair)
     back = (back_own.astype(F32) + received.astype(F32)).astype(BF16)
-    parts = lax.all_to_all(back.reshape(32, 128, 128), PLANE, 0, 0, tiled=True)
+    parts = lax.all_to_all(back.reshape(16, 128, 128), COLUMNS, 0, 0, tiled=True)
     summed = jnp.sum(parts.astype(F32), axis=0).astype(BF16)
-    input_grad = lax.ppermute(summed, ("yh", "zh"), quarter_turn(True))
+    input_grad = lax.ppermute(summed, AXES, grad_route())
     return input_grad, filter_grad, small[9], small[:9].reshape(3, 3, 128)
 
 

time: 151 us -> 147 us (0.974)
  the two profiles are of different devices: /device:TPU:16 before, /device:TPU:80 now
where the time goes in v3:
time: 147 us; the launch traced here: 146 us
  waiting for transfers between devices  48.2 us (33%)
  blocking collectives  41.7 us (28%)
  starting transfers between devices  41 us (28%)
  Pallas kernels  9.93 us (7%)
  local copies, waits for them, and re-layouts  2.72 us (2%)
  other arithmetic  1.5 us (1%)
    all_to_all x1, blocking collectives, on_device(): lax.all_to_all(back.reshape(16, 128, 128), COLUMNS, 0, 0, tiled=True)  24.2 us
    ppermute x3, waiting for transfers between devices, on_device(): lax.ppermute(part, X, [(i, i ^ away) for i in range(4)])  20.5 us
    all_to_all x1, blocking collectives, on_device(): spread = lax.all_to_all(partial, CTX, 0, 0, tiled=True)  17.6 us
    ppermute x1, starting transfers between devices, on_device(): moved = lax.ppermute(tokens, ('yh', 'zh'), QUARTER_TURN)  10 us
    ppermute x3, starting transfers between devices, on_device(): lax.ppermute(part, X, [(i, i ^ away) for i in range(4)])  9.82 us
    ppermute x1, waiting for transfers between devices, on_device(): w_z = lax.ppermute(jnp.stack([own, weights[3]]), 'zp', pair)  9.77 us
    ppermute x1, waiting for transfers between devices, on_device(): input_grad = lax.ppermute(summed, AXES, grad_route())  8.5 us
    all_to_all x1, starting transfers between devices, on_device(): lax.all_to_all(copies, SPREAD, 0, 0, tiled=True).reshape(4, 2, 4, 128, 128)  8.23 us
  transfers between devices with their start and end apart: 10, of which 7 were waited for; matrix products, arithmetic and copies ran while one was open for 2% of the time, Pallas kernels for 5%

profile of v3, /device:TPU:80, one launch (start us, length us, event | category | flops | bytes accessed | tf_op | source)
XLA Modules:
  0.0 145.9 jit_solution(3895192466844244986)
XLA Ops:
  0.6 10.0 %collective-permute-start = (bf16[128,128]{1,0:T(8,128)(2,1)}, bf16[128,128]{1,0:T(8,128)(2,1)S(1)}, u32[]{:S(2)}, u32[]{:S(2)}) collective-permute-start(bf16[128,128]{1,0:T(8,128)(2,1)} %param.6), channel_id=1, source_target_pairs={{0,8},{8,72},{64,0},{72,64},{1,9},{9,73},{65,1},{73,65},{2,10},{10... | collective-permute-start | bytes 98312 | tf_op jit(solution)/shard_map/ppermute | solution.py:293
  10.7 4.7 %collective-permute-start.2 = (bf16[3,1024,128]{2,1,0:T(8,128)(2,1)}, bf16[3,1024,128]{2,1,0:T(8,128)(2,1)S(1)}, u32[]{:S(2)}, u32[]{:S(2)}) collective-permute-start(bf16[3,1024,128]{2,1,0:T(8,128)(2,1)} %bitcast.18), channel_id=1, source_target_pairs={{0,384},{128,256},{256,128},{384,0},{1,385},{129,257},{257,129},{3... | collective-permute-start | bytes 2359304 | tf_op jit(solution)/shard_map/ppermute | solution.py:297
  15.3 2.7 %collective-permute-start.1 = (bf16[3,1024,128]{2,1,0:T(8,128)(2,1)}, bf16[3,1024,128]{2,1,0:T(8,128)(2,1)S(1)}, u32[]{:S(2)}, u32[]{:S(2)}) collective-permute-start(bf16[3,1024,128]{2,1,0:T(8,128)(2,1)} %bitcast.19), channel_id=1, source_target_pairs={{0,256},{128,384},{256,0},{384,128},{1,257},{129,385},{257,1},{385... | collective-permute-start | bytes 2359304 | tf_op jit(solution)/shard_map/ppermute | solution.py:297
  18.1 0.2 copies.1
  18.3 1.0 copy-done.1
  19.3 8.2 %all-to-all-start = ((bf16[32,128,128]{2,1,0:T(8,128)(2,1)}), bf16[32,128,128]{2,1,0:T(8,128)(2,1)S(1)}, u32[]{:S(2)}, u32[]{:S(2)}) async-start(bf16[32,128,128]{2,1,0:T(8,128)(2,1)} %copy-done.1), calls=%async_computation | async-start | bytes 2097152 | tf_op jit(solution)/shard_map/all_to_all | solution.py:326
  27.5 2.4 %collective-permute-start.3 = (bf16[3,1024,128]{2,1,0:T(8,128)(2,1)S(1)}, bf16[3,1024,128]{2,1,0:T(8,128)(2,1)}, u32[]{:S(2)}, u32[]{:S(2)}) collective-permute-start(bf16[3,1024,128]{2,1,0:T(8,128)(2,1)S(1)} %bitcast.20), channel_id=1, source_target_pairs={{0,128},{128,0},{256,384},{384,256},{1,129},{129,1},{257,385},{385... | collective-permute-start | bytes 2359304 | tf_op jit(solution)/shard_map/ppermute | solution.py:297
  30.0 19.9 %collective-permute-done.2 = bf16[3,1024,128]{2,1,0:T(8,128)(2,1)S(1)} collective-permute-done((bf16[3,1024,128]{2,1,0:T(8,128)(2,1)}, bf16[3,1024,128]{2,1,0:T(8,128)(2,1)S(1)}, u32[]{:S(2)}, u32[]{:S(2)}) %collective-permute-start.2) | collective-permute-done | bytes 786464 | tf_op jit(solution)/shard_map/ppermute | solution.py:297
  49.8 2.0 %prepare.1 = (bf16[8,16,128]{2,1,0:T(8,128)(2,1)}, f32[128,128]{1,0:T(8,128)}, bf16[4,128,128]{2,1,0:T(8,128)(2,1)}) custom-call(bf16[128,128]{1,0:T(8,128)(2,1)} %grad_ref, f32[3,3,128]{2,1,0:T(4,128)} %taps_ref.1, f32[1,128]{1,0:T(1,128)} %bitcast.33, f32[8,128]{1,0:T(8,128)} %filter_ref.1), custom_call_target="tpu_custom_call" | custom-call | flops 20000000000 | bytes 1048576 | tf_op jit(solution)/shard_map/prepare/pallas_call | solution.py:303
  51.8 0.6 collective-permute-done.3
  52.5 1.0 all-to-all-done
  53.5 1.9 %collective-permute-start.4 = (bf16[4,2,4,128,128]{4,3,2,1,0:T(8,128)(2,1)S(1)}, bf16[4,2,4,128,128]{4,3,2,1,0:T(8,128)(2,1)S(1)}, u32[]{:S(2)}, u32[]{:S(2)}) collective-permute-start(bf16[4,2,4,128,128]{4,3,2,1,0:T(8,128)(2,1)S(1)} %bitcast.27), channel_id=1, source_target_pairs={{0,1},{1,0},{2,3},{3,2},{4,5},{5,4},{6,7},{7,6},{8,9},{9,8},{10,11... | collective-permute-start | bytes 3145736 | tf_op jit(solution)/shard_map/ppermute | solution.py:330
  55.4 0.0 copy-start.4
  55.4 1.3 pad_maximum_fusion
  56.7 2.9 %collective-permute-start.5 = (bf16[2,3,1024,128]{3,2,1,0:T(8,128)(2,1)}, bf16[2,3,1024,128]{3,2,1,0:T(8,128)(2,1)}, u32[]{:S(2)}, u32[]{:S(2)}) collective-permute-start(bf16[2,3,1024,128]{3,2,1,0:T(8,128)(2,1)} %pad_maximum_fusion), channel_id=1, source_target_pairs={{0,2},{2,0},{1,3},{3,1},{4,6},{6,4},{5,7},{7,5},{8,10},{10,8},{9,1... | collective-permute-start | bytes 4718600 | tf_op jit(solution)/shard_map/ppermute | solution.py:300
  59.7 3.0 %project.1 = bf16[8,112,128]{2,1,0:T(8,128)(2,1)S(1)} custom-call(bf16[4,2,4,128,128]{4,3,2,1,0:T(8,128)(2,1)S(1)} %bitcast.28, bf16[4,2,4,128,128]{4,3,2,1,0:T(8,128)(2,1)S(1)} %collective-permute-done.4.other_ref, bf16[3,4,2,128,128]{4,3,2,1,0:T(8,128)(2,1)S(1)} %bitcast.22, bf16[3,4,2,128,128]{4,3,2,1,0:T(8,128)(2,1)} %bitcast.3.w1, ...), custom_call_target="tpu_custom_call" | custom-call | flops 805306368 | bytes 5242880 | tf_op jit(solution)/shard_map/project/pallas_call | solution.py:334
  62.7 17.6 %all_to_all.20.in_ref = bf16[8,112,128]{2,1,0:T(8,128)(2,1)S(1)} all-to-all(bf16[8,112,128]{2,1,0:T(8,128)(2,1)S(1)} %project.1), channel_id=1, replica_groups=mesh['xh'=2,'xl'=2,'yh'=2,'ylh'=2,'yll'=2,'zh'=2,'z2'=2,'zp'=2,'core'=2]..., dimensions={0} | all-to-all | bytes 458752 | tf_op jit(solution)/shard_map/all_to_all | solution.py:343
  80.3 1.7 %mixer.1 = bf16[8,2,112,128]{3,2,1,0:T(8,128)(2,1)} custom-call(bf16[8,112,128]{2,1,0:T(8,128)(2,1)S(1)} %all_to_all.20.in_ref, f32[128,128]{1,0:T(8,128)S(1)} %copy-done.3, bf16[4,128,128]{2,1,0:T(8,128)(2,1)S(1)} %copy-done.2), custom_call_target="tpu_custom_call" | custom-call | tf_op jit(solution)/shard_map/mixer/pallas_call | solution.py:345
  82.0 4.3 %all-to-all-start.2 = ((bf16[16,112,128]{2,1,0:T(8,128)(2,1)}), bf16[16,112,128]{2,1,0:T(8,128)(2,1)S(1)}, u32[]{:S(2)}, u32[]{:S(2)}) async-start(bf16[16,112,128]{2,1,0:T(8,128)(2,1)} %bitcast.7), calls=%async_computation.2 | async-start | bytes 917504 | tf_op jit(solution)/shard_map/all_to_all | solution.py:353
  86.3 9.8 %collective-permute-done.5 = bf16[2,3,1024,128]{3,2,1,0:T(8,128)(2,1)} collective-permute-done((bf16[2,3,1024,128]{3,2,1,0:T(8,128)(2,1)}, bf16[2,3,1024,128]{3,2,1,0:T(8,128)(2,1)}, u32[]{:S(2)}, u32[]{:S(2)}) %collective-permute-start.5) | collective-permute-done | bytes 1572896 | tf_op jit(solution)/shard_map/ppermute | solution.py:300
  96.1 6.5 %all-to-all-done.2 = bf16[16,112,128]{2,1,0:T(8,128)(2,1)S(1)} async-done(((bf16[16,112,128]{2,1,0:T(8,128)(2,1)}), bf16[16,112,128]{2,1,0:T(8,128)(2,1)S(1)}, u32[]{:S(2)}, u32[]{:S(2)}) %all-to-all-start.2) | async-done | bytes 458784 | tf_op jit(solution)/shard_map/all_to_all | solution.py:353
  102.6 2.9 %back.1 = (bf16[2,2,2,2,128,128]{5,4,3,2,1,0:T(8,128)(2,1)S(1)}, bf16[2,2,2,2,128,128]{5,4,3,2,1,0:T(8,128)(2,1)S(1)}, f32[8,128]{1,0:T(8,128)}, f32[16,128]{1,0:T(8,128)S(1)}) custom-call(bf16[8,2,112,128]{3,2,1,0:T(8,128)(2,1)S(1)} %bitcast.29, bf16[3,4,2,128,128]{4,3,2,1,0:T(8,128)(2,1)S(1)} %bitcast.23, bf16[3,4,2,128,128]{4,3,2,1,0:T(8,128)(2,1)S(1)} %bitcast.26, ...), custom_call_target="tpu_custom_call" | custom-call | flops 805306368 | bytes 5242880 | tf_op jit(solution)/shard_map/back/pallas_call | solution.py:358
  105.5 1.9 %collective-permute-start.6 = (bf16[2,2,2,2,128,128]{5,4,3,2,1,0:T(8,128)(2,1)S(1)}, bf16[2,2,2,2,128,128]{5,4,3,2,1,0:T(8,128)(2,1)S(1)}, u32[]{:S(2)}, u32[]{:S(2)}) collective-permute-start(bf16[2,2,2,2,128,128]{5,4,3,2,1,0:T(8,128)(2,1)S(1)} %get-tuple-element.35), channel_id=1, source_target_pairs={{0,1},{1,0},{2,3},{3,2},{4,5},{5,4},{6,7},{7,6},{8,9},{9,8},{10,11... | collective-permute-start | bytes 1572872 | tf_op jit(solution)/shard_map/ppermute | solution.py:372
  107.4 1.9 %collective-permute-done.6 = bf16[2,2,2,2,128,128]{5,4,3,2,1,0:T(8,128)(2,1)S(1)} collective-permute-done((bf16[2,2,2,2,128,128]{5,4,3,2,1,0:T(8,128)(2,1)S(1)}, bf16[2,2,2,2,128,128]{5,4,3,2,1,0:T(8,128)(2,1)S(1)}, u32[]{:S(2)}, u32[]{:S(2)}) %collective-permute-start.6) | collective-permute-done | bytes 524320 | tf_op jit(solution)/shard_map/ppermute | solution.py:372
  109.3 0.1 add_convert_fusion
  109.5 24.2 %all_to_all.21 = bf16[16,128,128]{2,1,0:T(8,128)(2,1)S(1)} all-to-all(bf16[16,128,128]{2,1,0:T(8,128)(2,1)S(1)} %bitcast.32), channel_id=1, replica_groups=mesh['xh'=2,'xl'=2,'yh'=2,'ylh'=2,'yll'=2,'zh'=2,'z2'=2,'zp'=2,'core'=2]..., dimensions={0} | all-to-all | bytes 1048576 | tf_op jit(solution)/shard_map/all_to_all | solution.py:374
  133.6 0.1 reduce_sum.12
  133.7 1.9 %collective-permute-start.7 = (bf16[128,128]{1,0:T(8,128)(2,1)S(1)}, bf16[128,128]{1,0:T(8,128)(2,1)S(1)}, u32[]{:S(2)}, u32[]{:S(2)}) collective-permute-start(bf16[128,128]{1,0:T(8,128)(2,1)S(1)} %reduce_sum.12), channel_id=1, source_target_pairs={{24,0},{25,1},{8,2},{9,3},{28,4},{29,5},{12,6},{13,7},{88,8},{89,9... | collective-permute-start | bytes 98312 | tf_op jit(solution)/shard_map/ppermute | solution.py:376
  135.7 0.5 slice_bitcast_fusion
  136.2 0.6 reshape.51
  136.8 8.5 %collective-permute-done.7 = bf16[128,128]{1,0:T(8,128)(2,1)S(1)} collective-permute-done((bf16[128,128]{1,0:T(8,128)(2,1)S(1)}, bf16[128,128]{1,0:T(8,128)(2,1)S(1)}, u32[]{:S(2)}, u32[]{:S(2)}) %collective-permute-start.7) | collective-permute-done | bytes 32800 | tf_op jit(solution)/shard_map/ppermute | solution.py:376
  145.3 0.6 copy.11
  (11 shorter events, 0.0 us)
Async XLA Ops:
  0.6 17.4 %collective-permute-start = (bf16[128,128]{1,0:T(8,128)(2,1)}, bf16[128,128]{1,0:T(8,128)(2,1)S(1)}, u32[]{:S(2)}, u32[]{:S(2)}) collective-permute-start(bf16[128,128]{1,0:T(8,128)(2,1)} %param.6), channel_id=1, source_target_pairs={{0,8},{8,72},{64,0},{72,64},{1,9},{9,73},{65,1},{73,65},{2,10},{10... | collective-permute-start | bytes 98312 | tf_op jit(solution)/shard_map/ppermute | solution.py:293
  10.7 39.2 %collective-permute-start.2 = (bf16[3,1024,128]{2,1,0:T(8,128)(2,1)}, bf16[3,1024,128]{2,1,0:T(8,128)(2,1)S(1)}, u32[]{:S(2)}, u32[]{:S(2)}) collective-permute-start(bf16[3,1024,128]{2,1,0:T(8,128)(2,1)} %bitcast.18), channel_id=1, source_target_pairs={{0,384},{128,256},{256,128},{384,0},{1,385},{129,257},{257,129},{3... | collective-permute-start | bytes 2359304 | tf_op jit(solution)/shard_map/ppermute | solution.py:297
  15.3 34.5 %collective-permute-start.1 = (bf16[3,1024,128]{2,1,0:T(8,128)(2,1)}, bf16[3,1024,128]{2,1,0:T(8,128)(2,1)S(1)}, u32[]{:S(2)}, u32[]{:S(2)}) collective-permute-start(bf16[3,1024,128]{2,1,0:T(8,128)(2,1)} %bitcast.19), channel_id=1, source_target_pairs={{0,256},{128,384},{256,0},{384,128},{1,257},{129,385},{257,1},{385... | collective-permute-start | bytes 2359304 | tf_op jit(solution)/shard_map/ppermute | solution.py:297
  18.3 1.0 copy-start.1
  19.3 8.2 %copy-start = (bf16[1024,3,128]{2,0,1:T(8,128)(2,1)S(1)}, bf16[1024,3,128]{2,0,1:T(8,128)(2,1)}, u32[]{:S(2)}) copy-start(bf16[1024,3,128]{2,0,1:T(8,128)(2,1)} %param.7) | copy-start | bytes 2359300
  19.3 34.2 %all-to-all-start = ((bf16[32,128,128]{2,1,0:T(8,128)(2,1)}), bf16[32,128,128]{2,1,0:T(8,128)(2,1)S(1)}, u32[]{:S(2)}, u32[]{:S(2)}) async-start(bf16[32,128,128]{2,1,0:T(8,128)(2,1)} %copy-done.1), calls=%async_computation | async-start | bytes 2097152 | tf_op jit(solution)/shard_map/all_to_all | solution.py:326
  27.5 25.0 %collective-permute-start.3 = (bf16[3,1024,128]{2,1,0:T(8,128)(2,1)S(1)}, bf16[3,1024,128]{2,1,0:T(8,128)(2,1)}, u32[]{:S(2)}, u32[]{:S(2)}) collective-permute-start(bf16[3,1024,128]{2,1,0:T(8,128)(2,1)S(1)} %bitcast.20), channel_id=1, source_target_pairs={{0,128},{128,0},{256,384},{384,256},{1,129},{129,1},{257,385},{385... | collective-permute-start | bytes 2359304 | tf_op jit(solution)/shard_map/ppermute | solution.py:297
  53.5 6.1 %collective-permute-start.4 = (bf16[4,2,4,128,128]{4,3,2,1,0:T(8,128)(2,1)S(1)}, bf16[4,2,4,128,128]{4,3,2,1,0:T(8,128)(2,1)S(1)}, u32[]{:S(2)}, u32[]{:S(2)}) collective-permute-start(bf16[4,2,4,128,128]{4,3,2,1,0:T(8,128)(2,1)S(1)} %bitcast.27), channel_id=1, source_target_pairs={{0,1},{1,0},{2,3},{3,2},{4,5},{5,4},{6,7},{7,6},{8,9},{9,8},{10,11... | collective-permute-start | bytes 3145736 | tf_op jit(solution)/shard_map/ppermute | solution.py:330
  55.4 4.2 %copy-start.4 = (bf16[8,16,128]{2,1,0:T(8,128)(2,1)S(1)}, bf16[8,16,128]{2,1,0:T(8,128)(2,1)}, u32[]{:S(2)}) copy-start(bf16[8,16,128]{2,1,0:T(8,128)(2,1)} %get-tuple-element.31.grad_ref) | copy-start | bytes 98308
  56.7 39.4 %collective-permute-start.5 = (bf16[2,3,1024,128]{3,2,1,0:T(8,128)(2,1)}, bf16[2,3,1024,128]{3,2,1,0:T(8,128)(2,1)}, u32[]{:S(2)}, u32[]{:S(2)}) collective-permute-start(bf16[2,3,1024,128]{3,2,1,0:T(8,128)(2,1)} %pad_maximum_fusion), channel_id=1, source_target_pairs={{0,2},{2,0},{1,3},{3,1},{4,6},{6,4},{5,7},{7,5},{8,10},{10,8},{9,1... | collective-permute-start | bytes 4718600 | tf_op jit(solution)/shard_map/ppermute | solution.py:300
  59.7 20.6 %copy-start.2 = (bf16[4,128,128]{2,1,0:T(8,128)(2,1)S(1)}, bf16[4,128,128]{2,1,0:T(8,128)(2,1)}, u32[]{:S(2)}) copy-start(bf16[4,128,128]{2,1,0:T(8,128)(2,1)} %get-tuple-element.33.band_ref) | copy-start | bytes 393220
  59.7 20.6 %copy-start.3 = (f32[128,128]{1,0:T(8,128)S(1)}, f32[128,128]{1,0:T(8,128)}, u32[]{:S(2)}) copy-start(f32[128,128]{1,0:T(8,128)} %get-tuple-element.32.table_ref) | copy-start | bytes 196612
  82.0 20.6 %all-to-all-start.2 = ((bf16[16,112,128]{2,1,0:T(8,128)(2,1)}), bf16[16,112,128]{2,1,0:T(8,128)(2,1)S(1)}, u32[]{:S(2)}, u32[]{:S(2)}) async-start(bf16[16,112,128]{2,1,0:T(8,128)(2,1)} %bitcast.7), calls=%async_computation.2 | async-start | bytes 917504 | tf_op jit(solution)/shard_map/all_to_all | solution.py:353
  105.5 3.8 %collective-permute-start.6 = (bf16[2,2,2,2,128,128]{5,4,3,2,1,0:T(8,128)(2,1)S(1)}, bf16[2,2,2,2,128,128]{5,4,3,2,1,0:T(8,128)(2,1)S(1)}, u32[]{:S(2)}, u32[]{:S(2)}) collective-permute-start(bf16[2,2,2,2,128,128]{5,4,3,2,1,0:T(8,128)(2,1)S(1)} %get-tuple-element.35), channel_id=1, source_target_pairs={{0,1},{1,0},{2,3},{3,2},{4,5},{5,4},{6,7},{7,6},{8,9},{9,8},{10,11... | collective-permute-start | bytes 1572872 | tf_op jit(solution)/shard_map/ppermute | solution.py:372
  133.7 11.5 %collective-permute-start.7 = (bf16[128,128]{1,0:T(8,128)(2,1)S(1)}, bf16[128,128]{1,0:T(8,128)(2,1)S(1)}, u32[]{:S(2)}, u32[]{:S(2)}) collective-permute-start(bf16[128,128]{1,0:T(8,128)(2,1)S(1)} %reduce_sum.12), channel_id=1, source_target_pairs={{24,0},{25,1},{8,2},{9,3},{28,4},{29,5},{12,6},{13,7},{88,8},{89,9... | collective-permute-start | bytes 98312 | tf_op jit(solution)/shard_map/ppermute | solution.py:376

commit v4 on v3

--- a/solution.py
+++ b/solution.py
@@ -18,7 +18,7 @@
 F32 = jnp.float32
 BF16 = jnp.bfloat16
 VMEM = pl.BlockSpec(memory_space=pltpu.VMEM)
-SMEM = pl.BlockSpec(memory_space=pltpu.SMEM)
+ANY = pl.BlockSpec(memory_space=pl.ANY)
 ROWS = 112
 HALF = 128
 
@@ -54,15 +54,17 @@
     out_ref[...] = jnp.broadcast_to(in_ref[...][None], (32, 128, 128))
 
 
-def prepare_kernel(grad_ref, taps_ref, skip_ref, filter_ref, grad_t_ref, table_ref, band_ref):
-    ctx = ctx_index()
-    grad_t_ref[...] = grad_ref[...].astype(F32).T.astype(BF16).reshape(8, 16, HALF)
+def table_kernel(taps_ref, skip_ref, table_ref):
     rows = jnp.concatenate(
         [taps_ref[0], taps_ref[1], taps_ref[2], skip_ref[...], jnp.zeros((118, 128), F32)], axis=0
     )
     table_ref[...] = rows.T
+
+
+def prepare_kernel(grad_ref, filter_ref, grad_t_ref, band_ref):
+    grad_t_ref[...] = grad_ref[...].astype(F32).T.astype(BF16).reshape(8, 16, HALF)
     band = rolled_rows(
-        jnp.broadcast_to(filter_ref[pl.ds(ctx, 1), :], (128, 128)), False
+        jnp.broadcast_to(filter_ref[pl.ds(ctx_index(), 1), :], (128, 128)), False
     )
     src = lax.broadcasted_iota(jnp.int32, (128, 128), 0)
     dst = lax.broadcasted_iota(jnp.int32, (128, 128), 1)
@@ -78,11 +80,15 @@
     return jnp.concatenate([weight[proj, z, side] for z in range(4)], axis=0)
 
 
-def project_kernel(own_ref, other_ref, w0, w1, w2, w3, grad_ref, out_ref):
+def project_kernel(own_ref, other_ref, w0, w1_far, w2, w3, grad_ref, out_ref, w1, sem):
+    copy = pltpu.make_async_copy(w1_far, w1, sem)
+    copy.start()
     x = x_index()
     core = lax.axis_index("core")
     totals = [jnp.zeros((256, 128), F32) for _ in range(3)]
-    for away, weight in enumerate((w0, w1, w2, w3)):
+    for away, weight in ((0, w0), (2, w2), (3, w3), (1, w1)):
+        if away == 1:
+            copy.wait()
         block = x ^ away
         for ref, side in ((own_ref, core), (other_ref, 1 - core)):
             rows = jnp.concatenate(
@@ -220,7 +226,15 @@
             out_ref[i, zp, 96:ROWS, :] = extra
 
 
-def back_kernel(in_ref, w_own, w_x, w_z, own_ref, other_ref, filter_ref, small_ref):
+def back_kernel(
+    in_ref, w_own, w_x, w_far, own_ref, other_ref, filter_ref, small_ref, w_z, sems
+):
+    copies = [
+        pltpu.make_async_copy(w_far.at[k // 3, k % 3], w_z.at[k // 3, k % 3], sems.at[k])
+        for k in range(6)
+    ]
+    for copy in copies:
+        copy.start()
     zp = lax.axis_index("zp")
     core = lax.axis_index("core")
     weights = ((w_own, w_z.at[0]), (w_x, w_z.at[1]))
@@ -238,6 +252,8 @@
         halves.append(jnp.concatenate(columns, axis=1))
     rows = jnp.concatenate(halves, axis=0)
     for away in range(2):
+        for copy in copies[3 * away : 3 * away + 3]:
+            copy.wait()
         for ref, side in ((own_ref, core), (other_ref, 1 - core)):
             table = jnp.concatenate(
                 [
@@ -297,21 +313,30 @@
         lax.ppermute(part, X, [(i, i ^ away) for i in range(4)])
         for part, away in ((late, 1), (own, 2), (own, 3))
     ]
-    w_z = lax.ppermute(jnp.stack([own, weights[3]]), "zp", pair)
-
-    out_grad, weights[2], weights[3] = lax.optimization_barrier((out_grad, weights[2], weights[3]))
-    grad_t, table, band = pl.pallas_call(
+    pair_rows = jnp.stack([own, weights[3]])
+
+    grad_t, band = pl.pallas_call(
         prepare_kernel,
         out_shape=(
             jax.ShapeDtypeStruct((8, 16, HALF), BF16),
-            jax.ShapeDtypeStruct((128, 128), F32),
             jax.ShapeDtypeStruct((4, 128, 128), BF16),
         ),
-        in_specs=[VMEM] * 4,
-        out_specs=(VMEM, VMEM, VMEM),
-        cost_estimate=pl.CostEstimate(flops=20000000000, bytes_accessed=1048576, transcendentals=0),
+        in_specs=[VMEM] * 2,
+        out_specs=(VMEM,) * 2,
         name="prepare",
-    )(out_grad, short_taps, skip_gain.reshape(1, 128), long_filter)
+    )(out_grad, long_filter)
+    weights[2], pair_rows = lax.optimization_barrier((weights[2], pair_rows))
+    short_taps, weights[2], weights[3] = lax.optimization_barrier(
+        (short_taps, weights[2], weights[3])
+    )
+    table = pl.pallas_call(
+        table_kernel,
+        out_shape=jax.ShapeDtypeStruct((128, 128), F32),
+        in_specs=[VMEM] * 2,
+        out_specs=VMEM,
+        cost_estimate=pl.CostEstimate(flops=20000000000, bytes_accessed=1 << 20, transcendentals=0),
+        name="table",
+    )(short_taps, skip_gain.reshape(1, 128))
 
     weights = [part.reshape(3, 4, 2, 128, 128) for part in weights]
     copies = pl.pallas_call(
@@ -324,9 +349,10 @@
         name="copies",
     )(moved)
     whole = lax.all_to_all(copies, SPREAD, 0, 0, tiled=True).reshape(4, 2, 4, 128, 128)
-    whole, grad_t, table, band, weights[1] = lax.optimization_barrier(
-        (whole, grad_t, table, band, weights[1])
-    )
+    whole, grad_t, table, band, weights[1], pair_rows = lax.optimization_barrier(
+        (whole, grad_t, table, band, weights[1], pair_rows)
+    )
+    w_z = lax.ppermute(pair_rows, "zp", pair).reshape(2, 3, 4, 2, 128, 128)
     across = lax.ppermute(whole, "core", pair)
 
     cost = pl.CostEstimate(flops=2 * 256 * 4096 * 384, bytes_accessed=5 << 20, transcendentals=0)
@@ -334,8 +360,9 @@
     partial = pl.pallas_call(
         project_kernel,
         out_shape=mixed_shape,
-        in_specs=[VMEM] * 7,
+        in_specs=[VMEM] * 3 + [ANY] + [VMEM] * 3,
         out_specs=VMEM,
+        scratch_shapes=[pltpu.VMEM((3, 4, 2, 128, 128), BF16), pltpu.SemaphoreType.DMA],
         compiler_params=params(40),
         cost_estimate=cost,
         name="project",
@@ -363,12 +390,13 @@
             jax.ShapeDtypeStruct((8, 128), F32),
             jax.ShapeDtypeStruct((16, 128), F32),
         ),
-        in_specs=[VMEM] * 4,
+        in_specs=[VMEM] * 3 + [ANY],
         out_specs=(VMEM,) * 4,
+        scratch_shapes=[pltpu.VMEM((2, 3, 4, 2, 128, 128), BF16), pltpu.SemaphoreType.DMA((6,))],
         compiler_params=params(40),
         cost_estimate=cost,
         name="back",
-    )(gathered, weights[0], weights[3], w_z.reshape(2, 3, 4, 2, 128, 128))
+    )(gathered, weights[0], weights[3], w_z)
     received = lax.ppermute(back_other, "core", pair)
     back = (back_own.astype(F32) + received.astype(F32)).astype(BF16)
     parts = lax.all_to_all(back.reshape(16, 128, 128), COLUMNS, 0, 0, tiled=True)

time: 147 us -> 145 us (0.986)
  waiting for transfers between devices: 48.2 us -> 46.6 us
    ppermute x3, waiting for transfers between devices: 20.5 us -> 17.9 us  [on_device(): lax.ppermute(part, X, [(i, i ^ away) for i in range(4)])]
    pallas_call x1 -> x2, Pallas kernels: 3.03 us -> 3.46 us  [the longest x1 2.04 us: on_device(): pl.pallas_call(project_kernel, out_shape=mixed_shape, in_specs=[VMEM] * 3...]
  transfers between devices with their start and end apart: 10 -> 10, of which waited for: 7 -> 6; matrix products, arithmetic and copies ran while one was open for 2% -> 2% of each run, Pallas kernels for 5% -> 5%
where the time goes in v4:
time: 145 us
  waiting for transfers between devices  46.6 us (32%)
  blocking collectives  41.7 us (29%)
  starting transfers between devices  41.1 us (28%)
  Pallas kernels  10.2 us (7%)
  local copies, waits for them, and re-layouts  2.74 us (2%)
  other arithmetic  1.53 us (1%)
    all_to_all x1, blocking collectives, on_device(): lax.all_to_all(back.reshape(16, 128, 128), COLUMNS, 0, 0, tiled=True)  24.2 us
    ppermute x3, waiting for transfers between devices, on_device(): lax.ppermute(part, X, [(i, i ^ away) for i in range(4)])  17.9 us
    all_to_all x1, blocking collectives, on_device(): spread = lax.all_to_all(partial, CTX, 0, 0, tiled=True)  17.6 us
    ppermute x1, waiting for transfers between devices, on_device(): w_z = lax.ppermute(pair_rows, 'zp', pair).reshape(2, 3, 4, 2, 128, 128)  10.8 us
    ppermute x1, starting transfers between devices, on_device(): moved = lax.ppermute(tokens, ('yh', 'zh'), QUARTER_TURN)  10 us
    ppermute x3, starting transfers between devices, on_device(): lax.ppermute(part, X, [(i, i ^ away) for i in range(4)])  9.81 us
    ppermute x1, waiting for transfers between devices, on_device(): input_grad = lax.ppermute(summed, AXES, grad_route())  8.58 us
    all_to_all x1, starting transfers between devices, on_device(): lax.all_to_all(copies, SPREAD, 0, 0, tiled=True).reshape(4, 2, 4, 128, 128)  8.23 us
  transfers between devices with their start and end apart: 10, of which 6 were waited for; matrix products, arithmetic and copies ran while one was open for 2% of the time, Pallas kernels for 5%

profile of v4, /device:TPU:80, one launch (start us, length us, event | category | flops | bytes accessed | tf_op | source)
XLA Modules:
  0.0 144.6 jit_solution(17960180574731820164)
XLA Ops:
  0.6 10.0 %collective-permute-start = (bf16[128,128]{1,0:T(8,128)(2,1)}, bf16[128,128]{1,0:T(8,128)(2,1)S(1)}, u32[]{:S(2)}, u32[]{:S(2)}) collective-permute-start(bf16[128,128]{1,0:T(8,128)(2,1)} %param.6), channel_id=1, source_target_pairs={{0,8},{8,72},{64,0},{72,64},{1,9},{9,73},{65,1},{73,65},{2,10},{10... | collective-permute-start | bytes 98312 | tf_op jit(solution)/shard_map/ppermute | solution.py:309
  10.7 4.7 %collective-permute-start.2 = (bf16[3,1024,128]{2,1,0:T(8,128)(2,1)}, bf16[3,1024,128]{2,1,0:T(8,128)(2,1)S(1)}, u32[]{:S(2)}, u32[]{:S(2)}) collective-permute-start(bf16[3,1024,128]{2,1,0:T(8,128)(2,1)} %bitcast.18), channel_id=1, source_target_pairs={{0,384},{128,256},{256,128},{384,0},{1,385},{129,257},{257,129},{3... | collective-permute-start | bytes 2359304 | tf_op jit(solution)/shard_map/ppermute | solution.py:313
  15.3 2.7 %collective-permute-start.1 = (bf16[3,1024,128]{2,1,0:T(8,128)(2,1)}, bf16[3,1024,128]{2,1,0:T(8,128)(2,1)S(1)}, u32[]{:S(2)}, u32[]{:S(2)}) collective-permute-start(bf16[3,1024,128]{2,1,0:T(8,128)(2,1)} %bitcast.19), channel_id=1, source_target_pairs={{0,256},{128,384},{256,0},{384,128},{1,257},{129,385},{257,1},{385... | collective-permute-start | bytes 2359304 | tf_op jit(solution)/shard_map/ppermute | solution.py:313
  18.0 0.0 collective-permute-done.in_ref
  18.1 0.2 copies.1
  18.3 1.0 copy-done.1
  19.3 8.2 %all-to-all-start = ((bf16[32,128,128]{2,1,0:T(8,128)(2,1)}), bf16[32,128,128]{2,1,0:T(8,128)(2,1)S(1)}, u32[]{:S(2)}, u32[]{:S(2)}) async-start(bf16[32,128,128]{2,1,0:T(8,128)(2,1)} %copy-done.1), calls=%async_computation | async-start | bytes 2097152 | tf_op jit(solution)/shard_map/all_to_all | solution.py:351
  27.5 1.9 %prepare.1 = (bf16[8,16,128]{2,1,0:T(8,128)(2,1)}, bf16[4,128,128]{2,1,0:T(8,128)(2,1)}) custom-call(bf16[128,128]{1,0:T(8,128)(2,1)} %grad_ref.1, f32[8,128]{1,0:T(8,128)} %filter_ref.1), custom_call_target="tpu_custom_call" | custom-call | tf_op jit(solution)/shard_map/prepare/pallas_call | solution.py:318
  29.4 2.4 %collective-permute-start.3 = (bf16[3,1024,128]{2,1,0:T(8,128)(2,1)S(1)}, bf16[3,1024,128]{2,1,0:T(8,128)(2,1)}, u32[]{:S(2)}, u32[]{:S(2)}) collective-permute-start(bf16[3,1024,128]{2,1,0:T(8,128)(2,1)S(1)} %bitcast.20), channel_id=1, source_target_pairs={{0,128},{128,0},{256,384},{384,256},{1,129},{129,1},{257,385},{385... | collective-permute-start | bytes 2359304 | tf_op jit(solution)/shard_map/ppermute | solution.py:313
  31.9 17.9 %collective-permute-done.2 = bf16[3,1024,128]{2,1,0:T(8,128)(2,1)S(1)} collective-permute-done((bf16[3,1024,128]{2,1,0:T(8,128)(2,1)}, bf16[3,1024,128]{2,1,0:T(8,128)(2,1)S(1)}, u32[]{:S(2)}, u32[]{:S(2)}) %collective-permute-start.2) | collective-permute-done | bytes 786464 | tf_op jit(solution)/shard_map/ppermute | solution.py:313
  49.8 1.3 pad_maximum_fusion
  51.1 1.4 table.1.table_ref
  52.6 1.0 all-to-all-done
  53.5 1.9 %collective-permute-start.4 = (bf16[4,2,4,128,128]{4,3,2,1,0:T(8,128)(2,1)S(1)}, bf16[4,2,4,128,128]{4,3,2,1,0:T(8,128)(2,1)S(1)}, u32[]{:S(2)}, u32[]{:S(2)}) collective-permute-start(bf16[4,2,4,128,128]{4,3,2,1,0:T(8,128)(2,1)S(1)} %bitcast.27), channel_id=1, source_target_pairs={{0,1},{1,0},{2,3},{3,2},{4,5},{5,4},{6,7},{7,6},{8,9},{9,8},{10,11... | collective-permute-start | bytes 3145736 | tf_op jit(solution)/shard_map/ppermute | solution.py:356
  55.4 2.9 %collective-permute-start.5 = (bf16[2,3,1024,128]{3,2,1,0:T(8,128)(2,1)}, bf16[2,3,1024,128]{3,2,1,0:T(8,128)(2,1)}, u32[]{:S(2)}, u32[]{:S(2)}) collective-permute-start(bf16[2,3,1024,128]{3,2,1,0:T(8,128)(2,1)} %pad_maximum_fusion), channel_id=1, source_target_pairs={{0,2},{2,0},{1,3},{3,1},{4,6},{6,4},{5,7},{7,5},{8,10},{10,8},{9,1... | collective-permute-start | bytes 4718600 | tf_op jit(solution)/shard_map/ppermute | solution.py:355
  58.4 2.0 %project.1 = bf16[8,112,128]{2,1,0:T(8,128)(2,1)S(1)} custom-call(bf16[4,2,4,128,128]{4,3,2,1,0:T(8,128)(2,1)S(1)} %bitcast.28, bf16[4,2,4,128,128]{4,3,2,1,0:T(8,128)(2,1)S(1)} %collective-permute-done.4.other_ref, bf16[3,4,2,128,128]{4,3,2,1,0:T(8,128)(2,1)S(1)} %bitcast.22, bf16[3,4,2,128,128]{4,3,2,1,0:T(8,128)(2,1)} %bitcast.5.w1_far, ...), custom_call_target="tpu_custom_call" | custom-call | flops 805306368 | bytes 5242880 | tf_op jit(solution)/shard_map/project/pallas_call | solution.py:360
  60.5 17.6 %all_to_all.20.in_ref = bf16[8,112,128]{2,1,0:T(8,128)(2,1)S(1)} all-to-all(bf16[8,112,128]{2,1,0:T(8,128)(2,1)S(1)} %project.1), channel_id=1, replica_groups=mesh['xh'=2,'xl'=2,'yh'=2,'ylh'=2,'yll'=2,'zh'=2,'z2'=2,'zp'=2,'core'=2]..., dimensions={0} | all-to-all | bytes 458752 | tf_op jit(solution)/shard_map/all_to_all | solution.py:370
  78.0 1.7 %mixer.1 = bf16[8,2,112,128]{3,2,1,0:T(8,128)(2,1)} custom-call(bf16[8,112,128]{2,1,0:T(8,128)(2,1)S(1)} %all_to_all.20.in_ref, f32[128,128]{1,0:T(8,128)S(1)} %copy-done.3, bf16[4,128,128]{2,1,0:T(8,128)(2,1)S(1)} %copy-done.2), custom_call_target="tpu_custom_call" | custom-call | tf_op jit(solution)/shard_map/mixer/pallas_call | solution.py:372
  79.8 4.3 %all-to-all-start.2 = ((bf16[16,112,128]{2,1,0:T(8,128)(2,1)}), bf16[16,112,128]{2,1,0:T(8,128)(2,1)S(1)}, u32[]{:S(2)}, u32[]{:S(2)}) async-start(bf16[16,112,128]{2,1,0:T(8,128)(2,1)} %bitcast.9), calls=%async_computation.2 | async-start | bytes 917504 | tf_op jit(solution)/shard_map/all_to_all | solution.py:380
  84.1 10.8 %collective-permute-done.5 = bf16[2,3,1024,128]{3,2,1,0:T(8,128)(2,1)} collective-permute-done((bf16[2,3,1024,128]{3,2,1,0:T(8,128)(2,1)}, bf16[2,3,1024,128]{3,2,1,0:T(8,128)(2,1)}, u32[]{:S(2)}, u32[]{:S(2)}) %collective-permute-start.5) | collective-permute-done | bytes 1572896 | tf_op jit(solution)/shard_map/ppermute | solution.py:355
  94.8 6.5 %all-to-all-done.2 = bf16[16,112,128]{2,1,0:T(8,128)(2,1)S(1)} async-done(((bf16[16,112,128]{2,1,0:T(8,128)(2,1)}), bf16[16,112,128]{2,1,0:T(8,128)(2,1)S(1)}, u32[]{:S(2)}, u32[]{:S(2)}) %all-to-all-start.2) | async-done | bytes 458784 | tf_op jit(solution)/shard_map/all_to_all | solution.py:380
  101.3 2.9 %back.1 = (bf16[2,2,2,2,128,128]{5,4,3,2,1,0:T(8,128)(2,1)S(1)}, bf16[2,2,2,2,128,128]{5,4,3,2,1,0:T(8,128)(2,1)S(1)}, f32[8,128]{1,0:T(8,128)}, f32[16,128]{1,0:T(8,128)S(1)}) custom-call(bf16[8,2,112,128]{3,2,1,0:T(8,128)(2,1)S(1)} %bitcast.29, bf16[3,4,2,128,128]{4,3,2,1,0:T(8,128)(2,1)S(1)} %bitcast.23, bf16[3,4,2,128,128]{4,3,2,1,0:T(8,128)(2,1)S(1)} %bitcast.26, ...), custom_call_target="tpu_custom_call" | custom-call | flops 805306368 | bytes 5242880 | tf_op jit(solution)/shard_map/back/pallas_call | solution.py:385
  104.2 1.9 %collective-permute-start.6 = (bf16[2,2,2,2,128,128]{5,4,3,2,1,0:T(8,128)(2,1)S(1)}, bf16[2,2,2,2,128,128]{5,4,3,2,1,0:T(8,128)(2,1)S(1)}, u32[]{:S(2)}, u32[]{:S(2)}) collective-permute-start(bf16[2,2,2,2,128,128]{5,4,3,2,1,0:T(8,128)(2,1)S(1)} %get-tuple-element.39), channel_id=1, source_target_pairs={{0,1},{1,0},{2,3},{3,2},{4,5},{5,4},{6,7},{7,6},{8,9},{9,8},{10,11... | collective-permute-start | bytes 1572872 | tf_op jit(solution)/shard_map/ppermute | solution.py:400
  106.1 1.9 %collective-permute-done.6 = bf16[2,2,2,2,128,128]{5,4,3,2,1,0:T(8,128)(2,1)S(1)} collective-permute-done((bf16[2,2,2,2,128,128]{5,4,3,2,1,0:T(8,128)(2,1)S(1)}, bf16[2,2,2,2,128,128]{5,4,3,2,1,0:T(8,128)(2,1)S(1)}, u32[]{:S(2)}, u32[]{:S(2)}) %collective-permute-start.6) | collective-permute-done | bytes 524320 | tf_op jit(solution)/shard_map/ppermute | solution.py:400
  108.0 0.1 add_convert_fusion
  108.2 24.2 %all_to_all.21 = bf16[16,128,128]{2,1,0:T(8,128)(2,1)S(1)} all-to-all(bf16[16,128,128]{2,1,0:T(8,128)(2,1)S(1)} %bitcast.32), channel_id=1, replica_groups=mesh['xh'=2,'xl'=2,'yh'=2,'ylh'=2,'yll'=2,'zh'=2,'z2'=2,'zp'=2,'core'=2]..., dimensions={0} | all-to-all | bytes 1048576 | tf_op jit(solution)/shard_map/all_to_all | solution.py:402
  132.3 0.1 reduce_sum.12
  132.4 1.9 %collective-permute-start.7 = (bf16[128,128]{1,0:T(8,128)(2,1)S(1)}, bf16[128,128]{1,0:T(8,128)(2,1)S(1)}, u32[]{:S(2)}, u32[]{:S(2)}) collective-permute-start(bf16[128,128]{1,0:T(8,128)(2,1)S(1)} %reduce_sum.12), channel_id=1, source_target_pairs={{24,0},{25,1},{8,2},{9,3},{28,4},{29,5},{12,6},{13,7},{88,8},{89,9... | collective-permute-start | bytes 98312 | tf_op jit(solution)/shard_map/ppermute | solution.py:404
  134.3 0.5 slice_bitcast_fusion
  134.8 0.6 reshape.51
  135.4 8.6 %collective-permute-done.7 = bf16[128,128]{1,0:T(8,128)(2,1)S(1)} collective-permute-done((bf16[128,128]{1,0:T(8,128)(2,1)S(1)}, bf16[128,128]{1,0:T(8,128)(2,1)S(1)}, u32[]{:S(2)}, u32[]{:S(2)}) %collective-permute-start.7) | collective-permute-done | bytes 32800 | tf_op jit(solution)/shard_map/ppermute | solution.py:404
  144.0 0.6 copy.11
  (12 shorter events, 0.0 us)
Async XLA Ops:
  0.6 17.4 %collective-permute-start = (bf16[128,128]{1,0:T(8,128)(2,1)}, bf16[128,128]{1,0:T(8,128)(2,1)S(1)}, u32[]{:S(2)}, u32[]{:S(2)}) collective-permute-start(bf16[128,128]{1,0:T(8,128)(2,1)} %param.6), channel_id=1, source_target_pairs={{0,8},{8,72},{64,0},{72,64},{1,9},{9,73},{65,1},{73,65},{2,10},{10... | collective-permute-start | bytes 98312 | tf_op jit(solution)/shard_map/ppermute | solution.py:309
  10.7 39.2 %collective-permute-start.2 = (bf16[3,1024,128]{2,1,0:T(8,128)(2,1)}, bf16[3,1024,128]{2,1,0:T(8,128)(2,1)S(1)}, u32[]{:S(2)}, u32[]{:S(2)}) collective-permute-start(bf16[3,1024,128]{2,1,0:T(8,128)(2,1)} %bitcast.18), channel_id=1, source_target_pairs={{0,384},{128,256},{256,128},{384,0},{1,385},{129,257},{257,129},{3... | collective-permute-start | bytes 2359304 | tf_op jit(solution)/shard_map/ppermute | solution.py:313
  15.3 35.8 %collective-permute-start.1 = (bf16[3,1024,128]{2,1,0:T(8,128)(2,1)}, bf16[3,1024,128]{2,1,0:T(8,128)(2,1)S(1)}, u32[]{:S(2)}, u32[]{:S(2)}) collective-permute-start(bf16[3,1024,128]{2,1,0:T(8,128)(2,1)} %bitcast.19), channel_id=1, source_target_pairs={{0,256},{128,384},{256,0},{384,128},{1,257},{129,385},{257,1},{385... | collective-permute-start | bytes 2359304 | tf_op jit(solution)/shard_map/ppermute | solution.py:313
  18.3 1.0 copy-start.1
  19.3 10.1 %copy-start = (bf16[1024,3,128]{2,0,1:T(8,128)(2,1)S(1)}, bf16[1024,3,128]{2,0,1:T(8,128)(2,1)}, u32[]{:S(2)}) copy-start(bf16[1024,3,128]{2,0,1:T(8,128)(2,1)} %param.7) | copy-start | bytes 2359300
  19.3 34.2 %all-to-all-start = ((bf16[32,128,128]{2,1,0:T(8,128)(2,1)}), bf16[32,128,128]{2,1,0:T(8,128)(2,1)S(1)}, u32[]{:S(2)}, u32[]{:S(2)}) async-start(bf16[32,128,128]{2,1,0:T(8,128)(2,1)} %copy-done.1), calls=%async_computation | async-start | bytes 2097152 | tf_op jit(solution)/shard_map/all_to_all | solution.py:351
  29.4 23.1 %collective-permute-start.3 = (bf16[3,1024,128]{2,1,0:T(8,128)(2,1)S(1)}, bf16[3,1024,128]{2,1,0:T(8,128)(2,1)}, u32[]{:S(2)}, u32[]{:S(2)}) collective-permute-start(bf16[3,1024,128]{2,1,0:T(8,128)(2,1)S(1)} %bitcast.20), channel_id=1, source_target_pairs={{0,128},{128,0},{256,384},{384,256},{1,129},{129,1},{257,385},{385... | collective-permute-start | bytes 2359304 | tf_op jit(solution)/shard_map/ppermute | solution.py:313
  51.1 7.3 %copy-start.4 = (bf16[8,16,128]{2,1,0:T(8,128)(2,1)S(1)}, bf16[8,16,128]{2,1,0:T(8,128)(2,1)}, u32[]{:S(2)}) copy-start(bf16[8,16,128]{2,1,0:T(8,128)(2,1)} %get-tuple-element.34.grad_ref) | copy-start | bytes 98308
  53.5 4.9 %collective-permute-start.4 = (bf16[4,2,4,128,128]{4,3,2,1,0:T(8,128)(2,1)S(1)}, bf16[4,2,4,128,128]{4,3,2,1,0:T(8,128)(2,1)S(1)}, u32[]{:S(2)}, u32[]{:S(2)}) collective-permute-start(bf16[4,2,4,128,128]{4,3,2,1,0:T(8,128)(2,1)S(1)} %bitcast.27), channel_id=1, source_target_pairs={{0,1},{1,0},{2,3},{3,2},{4,5},{5,4},{6,7},{7,6},{8,9},{9,8},{10,11... | collective-permute-start | bytes 3145736 | tf_op jit(solution)/shard_map/ppermute | solution.py:356
  55.4 39.4 %collective-permute-start.5 = (bf16[2,3,1024,128]{3,2,1,0:T(8,128)(2,1)}, bf16[2,3,1024,128]{3,2,1,0:T(8,128)(2,1)}, u32[]{:S(2)}, u32[]{:S(2)}) collective-permute-start(bf16[2,3,1024,128]{3,2,1,0:T(8,128)(2,1)} %pad_maximum_fusion), channel_id=1, source_target_pairs={{0,2},{2,0},{1,3},{3,1},{4,6},{6,4},{5,7},{7,5},{8,10},{10,8},{9,1... | collective-permute-start | bytes 4718600 | tf_op jit(solution)/shard_map/ppermute | solution.py:355
  58.4 19.6 %copy-start.2 = (bf16[4,128,128]{2,1,0:T(8,128)(2,1)S(1)}, bf16[4,128,128]{2,1,0:T(8,128)(2,1)}, u32[]{:S(2)}) copy-start(bf16[4,128,128]{2,1,0:T(8,128)(2,1)} %get-tuple-element.36.band_ref) | copy-start | bytes 393220
  58.4 19.6 %copy-start.3 = (f32[128,128]{1,0:T(8,128)S(1)}, f32[128,128]{1,0:T(8,128)}, u32[]{:S(2)}) copy-start(f32[128,128]{1,0:T(8,128)} %table.1.table_ref) | copy-start | bytes 196612
  79.8 21.6 %all-to-all-start.2 = ((bf16[16,112,128]{2,1,0:T(8,128)(2,1)}), bf16[16,112,128]{2,1,0:T(8,128)(2,1)S(1)}, u32[]{:S(2)}, u32[]{:S(2)}) async-start(bf16[16,112,128]{2,1,0:T(8,128)(2,1)} %bitcast.9), calls=%async_computation.2 | async-start | bytes 917504 | tf_op jit(solution)/shard_map/all_to_all | solution.py:380
  104.2 3.8 %collective-permute-start.6 = (bf16[2,2,2,2,128,128]{5,4,3,2,1,0:T(8,128)(2,1)S(1)}, bf16[2,2,2,2,128,128]{5,4,3,2,1,0:T(8,128)(2,1)S(1)}, u32[]{:S(2)}, u32[]{:S(2)}) collective-permute-start(bf16[2,2,2,2,128,128]{5,4,3,2,1,0:T(8,128)(2,1)S(1)} %get-tuple-element.39), channel_id=1, source_target_pairs={{0,1},{1,0},{2,3},{3,2},{4,5},{5,4},{6,7},{7,6},{8,9},{9,8},{10,11... | collective-permute-start | bytes 1572872 | tf_op jit(solution)/shard_map/ppermute | solution.py:400
  132.4 11.6 %collective-permute-start.7 = (bf16[128,128]{1,0:T(8,128)(2,1)S(1)}, bf16[128,128]{1,0:T(8,128)(2,1)S(1)}, u32[]{:S(2)}, u32[]{:S(2)}) collective-permute-start(bf16[128,128]{1,0:T(8,128)(2,1)S(1)} %reduce_sum.12), channel_id=1, source_target_pairs={{24,0},{25,1},{8,2},{9,3},{28,4},{29,5},{12,6},{13,7},{88,8},{89,9... | collective-permute-start | bytes 98312 | tf_op jit(solution)/shard_map/ppermute | solution.py:404

commit v5 on v4

--- a/solution.py
+++ b/solution.py
@@ -311,10 +311,11 @@
     moved, late = lax.optimization_barrier((moved, own))
     weights = [own] + [
         lax.ppermute(part, X, [(i, i ^ away) for i in range(4)])
-        for part, away in ((late, 1), (own, 2), (own, 3))
+        for part, away in ((late, 1), (own, 2), (late, 3))
     ]
     pair_rows = jnp.stack([own, weights[3]])
 
+    out_grad, short_taps, weights[2] = lax.optimization_barrier((out_grad, short_taps, weights[2]))
     grad_t, band = pl.pallas_call(
         prepare_kernel,
         out_shape=(
@@ -325,10 +326,6 @@
         out_specs=(VMEM,) * 2,
         name="prepare",
     )(out_grad, long_filter)
-    weights[2], pair_rows = lax.optimization_barrier((weights[2], pair_rows))
-    short_taps, weights[2], weights[3] = lax.optimization_barrier(
-        (short_taps, weights[2], weights[3])
-    )
     table = pl.pallas_call(
         table_kernel,
         out_shape=jax.ShapeDtypeStruct((128, 128), F32),

time: 145 us -> 144 us (level)
  waiting for transfers between devices: 46.6 us -> 41.5 us
  blocking collectives: 41.7 us -> 43.9 us
  starting transfers between devices: 41.1 us -> 43 us
    ppermute x3, waiting for transfers between devices: 17.9 us -> 14.8 us  [on_device(): lax.ppermute(part, X, [(i, i ^ away) for i in range(4)])]
    all_to_all x1, blocking collectives: 17.6 us -> 19.6 us  [on_device(): spread = lax.all_to_all(partial, CTX, 0, 0, tiled=True)]
    ppermute x1, waiting for transfers between devices: 10.8 us -> 8.81 us  [on_device(): w_z = lax.ppermute(pair_rows, 'zp', pair).reshape(2, 3, 4, 2, 128, 128)]
    ppermute x3, starting transfers between devices: 9.81 us -> 11.7 us  [on_device(): lax.ppermute(part, X, [(i, i ^ away) for i in range(4)])]
  transfers between devices with their start and end apart: 10 -> 10, of which waited for: 6 -> 7; matrix products, arithmetic and copies ran while one was open for 2% -> 2% of each run, Pallas kernels for 5% -> 5%
where the time goes in v5:
time: 144 us
  blocking collectives  43.9 us (30%)
  starting transfers between devices  43 us (30%)
  waiting for transfers between devices  41.5 us (29%)
  Pallas kernels  10.2 us (7%)
  local copies, waits for them, and re-layouts  2.74 us (2%)
  other arithmetic  1.53 us (1%)
    all_to_all x1, blocking collectives, on_device(): lax.all_to_all(back.reshape(16, 128, 128), COLUMNS, 0, 0, tiled=True)  24.3 us
    all_to_all x1, blocking collectives, on_device(): spread = lax.all_to_all(partial, CTX, 0, 0, tiled=True)  19.6 us
    ppermute x3, waiting for transfers between devices, on_device(): lax.ppermute(part, X, [(i, i ^ away) for i in range(4)])  14.8 us
    ppermute x3, starting transfers between devices, on_device(): lax.ppermute(part, X, [(i, i ^ away) for i in range(4)])  11.7 us
    ppermute x1, starting transfers between devices, on_device(): moved = lax.ppermute(tokens, ('yh', 'zh'), QUARTER_TURN)  10 us
    ppermute x1, waiting for transfers between devices, on_device(): w_z = lax.ppermute(pair_rows, 'zp', pair).reshape(2, 3, 4, 2, 128, 128)  8.81 us
    ppermute x1, waiting for transfers between devices, on_device(): input_grad = lax.ppermute(summed, AXES, grad_route())  8.59 us
    all_to_all x1, starting transfers between devices, on_device(): lax.all_to_all(copies, SPREAD, 0, 0, tiled=True).reshape(4, 2, 4, 128, 128)  8.34 us
  transfers between devices with their start and end apart: 10, of which 7 were waited for; matrix products, arithmetic and copies ran while one was open for 2% of the time, Pallas kernels for 5%

profile of v5, /device:TPU:80, one launch (start us, length us, event | category | flops | bytes accessed | tf_op | source)
XLA Modules:
  0.0 143.6 jit_solution(13309949166727803694)
XLA Ops:
  0.6 10.0 %collective-permute-start = (bf16[128,128]{1,0:T(8,128)(2,1)}, bf16[128,128]{1,0:T(8,128)(2,1)S(1)}, u32[]{:S(2)}, u32[]{:S(2)}) collective-permute-start(bf16[128,128]{1,0:T(8,128)(2,1)} %param.6), channel_id=1, source_target_pairs={{0,8},{8,72},{64,0},{72,64},{1,9},{9,73},{65,1},{73,65},{2,10},{10... | collective-permute-start | bytes 98312 | tf_op jit(solution)/shard_map/ppermute | solution.py:309
  10.7 4.9 %collective-permute-start.1 = (bf16[3,1024,128]{2,1,0:T(8,128)(2,1)}, bf16[3,1024,128]{2,1,0:T(8,128)(2,1)S(1)}, u32[]{:S(2)}, u32[]{:S(2)}) collective-permute-start(bf16[3,1024,128]{2,1,0:T(8,128)(2,1)} %bitcast.18), channel_id=1, source_target_pairs={{0,256},{128,384},{256,0},{384,128},{1,257},{129,385},{257,1},{385... | collective-permute-start | bytes 2359304 | tf_op jit(solution)/shard_map/ppermute | solution.py:313
  15.6 0.2 copies.1
  15.9 1.0 copy-done.1
  16.9 8.3 %all-to-all-start = ((bf16[32,128,128]{2,1,0:T(8,128)(2,1)}), bf16[32,128,128]{2,1,0:T(8,128)(2,1)S(1)}, u32[]{:S(2)}, u32[]{:S(2)}) async-start(bf16[32,128,128]{2,1,0:T(8,128)(2,1)} %copy-done.1), calls=%async_computation | async-start | bytes 2097152 | tf_op jit(solution)/shard_map/all_to_all | solution.py:348
  25.2 4.7 %collective-permute-start.3 = (bf16[3,1024,128]{2,1,0:T(8,128)(2,1)S(1)}, bf16[3,1024,128]{2,1,0:T(8,128)(2,1)S(1)}, u32[]{:S(2)}, u32[]{:S(2)}) collective-permute-start(bf16[3,1024,128]{2,1,0:T(8,128)(2,1)S(1)} %bitcast.19), channel_id=1, source_target_pairs={{0,384},{128,256},{256,128},{384,0},{1,385},{129,257},{257,129},{3... | collective-permute-start | bytes 2359304 | tf_op jit(solution)/shard_map/ppermute | solution.py:313
  29.9 2.1 %collective-permute-start.2 = (bf16[3,1024,128]{2,1,0:T(8,128)(2,1)S(1)}, bf16[3,1024,128]{2,1,0:T(8,128)(2,1)}, u32[]{:S(2)}, u32[]{:S(2)}) collective-permute-start(bf16[3,1024,128]{2,1,0:T(8,128)(2,1)S(1)} %bitcast.20), channel_id=1, source_target_pairs={{0,128},{128,0},{256,384},{384,256},{1,129},{129,1},{257,385},{385... | collective-permute-start | bytes 2359304 | tf_op jit(solution)/shard_map/ppermute | solution.py:313
  32.0 1.9 %collective-permute-done.1 = bf16[3,1024,128]{2,1,0:T(8,128)(2,1)S(1)} collective-permute-done((bf16[3,1024,128]{2,1,0:T(8,128)(2,1)}, bf16[3,1024,128]{2,1,0:T(8,128)(2,1)S(1)}, u32[]{:S(2)}, u32[]{:S(2)}) %collective-permute-start.1) | collective-permute-done | bytes 786464 | tf_op jit(solution)/shard_map/ppermute | solution.py:313
  33.9 1.4 table.1.table_ref
  35.4 1.9 %prepare.1 = (bf16[8,16,128]{2,1,0:T(8,128)(2,1)}, bf16[4,128,128]{2,1,0:T(8,128)(2,1)}) custom-call(bf16[128,128]{1,0:T(8,128)(2,1)} %grad_ref, f32[8,128]{1,0:T(8,128)} %filter_ref.1), custom_call_target="tpu_custom_call" | custom-call | tf_op jit(solution)/shard_map/prepare/pallas_call | solution.py:319
  37.3 12.9 %collective-permute-done.3 = bf16[3,1024,128]{2,1,0:T(8,128)(2,1)S(1)} collective-permute-done((bf16[3,1024,128]{2,1,0:T(8,128)(2,1)S(1)}, bf16[3,1024,128]{2,1,0:T(8,128)(2,1)S(1)}, u32[]{:S(2)}, u32[]{:S(2)}) %collective-permute-start.3) | collective-permute-done | bytes 786464 | tf_op jit(solution)/shard_map/ppermute | solution.py:313
  50.1 1.3 pad_maximum_fusion
  51.4 0.1 all-to-all-done
  51.6 1.9 %collective-permute-start.4 = (bf16[4,2,4,128,128]{4,3,2,1,0:T(8,128)(2,1)S(1)}, bf16[4,2,4,128,128]{4,3,2,1,0:T(8,128)(2,1)S(1)}, u32[]{:S(2)}, u32[]{:S(2)}) collective-permute-start(bf16[4,2,4,128,128]{4,3,2,1,0:T(8,128)(2,1)S(1)} %bitcast.27), channel_id=1, source_target_pairs={{0,1},{1,0},{2,3},{3,2},{4,5},{5,4},{6,7},{7,6},{8,9},{9,8},{10,11... | collective-permute-start | bytes 3145736 | tf_op jit(solution)/shard_map/ppermute | solution.py:353
  53.5 2.8 %collective-permute-start.5 = (bf16[2,3,1024,128]{3,2,1,0:T(8,128)(2,1)}, bf16[2,3,1024,128]{3,2,1,0:T(8,128)(2,1)}, u32[]{:S(2)}, u32[]{:S(2)}) collective-permute-start(bf16[2,3,1024,128]{3,2,1,0:T(8,128)(2,1)} %pad_maximum_fusion), channel_id=1, source_target_pairs={{0,2},{2,0},{1,3},{3,1},{4,6},{6,4},{5,7},{7,5},{8,10},{10,8},{9,1... | collective-permute-start | bytes 4718600 | tf_op jit(solution)/shard_map/ppermute | solution.py:352
  56.4 2.0 %project.1 = bf16[8,112,128]{2,1,0:T(8,128)(2,1)S(1)} custom-call(bf16[4,2,4,128,128]{4,3,2,1,0:T(8,128)(2,1)S(1)} %bitcast.28, bf16[4,2,4,128,128]{4,3,2,1,0:T(8,128)(2,1)S(1)} %collective-permute-done.4.other_ref, bf16[3,4,2,128,128]{4,3,2,1,0:T(8,128)(2,1)S(1)} %bitcast.22, bf16[3,4,2,128,128]{4,3,2,1,0:T(8,128)(2,1)} %bitcast.3.w1_far, ...), custom_call_target="tpu_custom_call" | custom-call | flops 805306368 | bytes 5242880 | tf_op jit(solution)/shard_map/project/pallas_call | solution.py:357
  58.4 19.6 %all_to_all.20.in_ref = bf16[8,112,128]{2,1,0:T(8,128)(2,1)S(1)} all-to-all(bf16[8,112,128]{2,1,0:T(8,128)(2,1)S(1)} %project.1), channel_id=1, replica_groups=mesh['xh'=2,'xl'=2,'yh'=2,'ylh'=2,'yll'=2,'zh'=2,'z2'=2,'zp'=2,'core'=2]..., dimensions={0} | all-to-all | bytes 458752 | tf_op jit(solution)/shard_map/all_to_all | solution.py:367
  78.0 1.7 %mixer.1 = bf16[8,2,112,128]{3,2,1,0:T(8,128)(2,1)} custom-call(bf16[8,112,128]{2,1,0:T(8,128)(2,1)S(1)} %all_to_all.20.in_ref, f32[128,128]{1,0:T(8,128)S(1)} %copy-done.3, bf16[4,128,128]{2,1,0:T(8,128)(2,1)S(1)} %copy-done.2), custom_call_target="tpu_custom_call" | custom-call | tf_op jit(solution)/shard_map/mixer/pallas_call | solution.py:369
  79.8 4.3 %all-to-all-start.2 = ((bf16[16,112,128]{2,1,0:T(8,128)(2,1)}), bf16[16,112,128]{2,1,0:T(8,128)(2,1)S(1)}, u32[]{:S(2)}, u32[]{:S(2)}) async-start(bf16[16,112,128]{2,1,0:T(8,128)(2,1)} %bitcast.9), calls=%async_computation.2 | async-start | bytes 917504 | tf_op jit(solution)/shard_map/all_to_all | solution.py:377
  84.1 8.8 %collective-permute-done.5 = bf16[2,3,1024,128]{3,2,1,0:T(8,128)(2,1)} collective-permute-done((bf16[2,3,1024,128]{3,2,1,0:T(8,128)(2,1)}, bf16[2,3,1024,128]{3,2,1,0:T(8,128)(2,1)}, u32[]{:S(2)}, u32[]{:S(2)}) %collective-permute-start.5) | collective-permute-done | bytes 1572896 | tf_op jit(solution)/shard_map/ppermute | solution.py:352
  92.9 7.3 %all-to-all-done.2 = bf16[16,112,128]{2,1,0:T(8,128)(2,1)S(1)} async-done(((bf16[16,112,128]{2,1,0:T(8,128)(2,1)}), bf16[16,112,128]{2,1,0:T(8,128)(2,1)S(1)}, u32[]{:S(2)}, u32[]{:S(2)}) %all-to-all-start.2) | async-done | bytes 458784 | tf_op jit(solution)/shard_map/all_to_all | solution.py:377
  100.2 2.9 %back.1 = (bf16[2,2,2,2,128,128]{5,4,3,2,1,0:T(8,128)(2,1)S(1)}, bf16[2,2,2,2,128,128]{5,4,3,2,1,0:T(8,128)(2,1)S(1)}, f32[8,128]{1,0:T(8,128)}, f32[16,128]{1,0:T(8,128)S(1)}) custom-call(bf16[8,2,112,128]{3,2,1,0:T(8,128)(2,1)S(1)} %bitcast.29, bf16[3,4,2,128,128]{4,3,2,1,0:T(8,128)(2,1)S(1)} %bitcast.23, bf16[3,4,2,128,128]{4,3,2,1,0:T(8,128)(2,1)S(1)} %bitcast.26, ...), custom_call_target="tpu_custom_call" | custom-call | flops 805306368 | bytes 5242880 | tf_op jit(solution)/shard_map/back/pallas_call | solution.py:382
  103.0 1.9 %collective-permute-start.6 = (bf16[2,2,2,2,128,128]{5,4,3,2,1,0:T(8,128)(2,1)S(1)}, bf16[2,2,2,2,128,128]{5,4,3,2,1,0:T(8,128)(2,1)S(1)}, u32[]{:S(2)}, u32[]{:S(2)}) collective-permute-start(bf16[2,2,2,2,128,128]{5,4,3,2,1,0:T(8,128)(2,1)S(1)} %get-tuple-element.35), channel_id=1, source_target_pairs={{0,1},{1,0},{2,3},{3,2},{4,5},{5,4},{6,7},{7,6},{8,9},{9,8},{10,11... | collective-permute-start | bytes 1572872 | tf_op jit(solution)/shard_map/ppermute | solution.py:397
  105.0 1.9 %collective-permute-done.6 = bf16[2,2,2,2,128,128]{5,4,3,2,1,0:T(8,128)(2,1)S(1)} collective-permute-done((bf16[2,2,2,2,128,128]{5,4,3,2,1,0:T(8,128)(2,1)S(1)}, bf16[2,2,2,2,128,128]{5,4,3,2,1,0:T(8,128)(2,1)S(1)}, u32[]{:S(2)}, u32[]{:S(2)}) %collective-permute-start.6) | collective-permute-done | bytes 524320 | tf_op jit(solution)/shard_map/ppermute | solution.py:397
  106.8 0.1 add_convert_fusion
  107.0 24.3 %all_to_all.21 = bf16[16,128,128]{2,1,0:T(8,128)(2,1)S(1)} all-to-all(bf16[16,128,128]{2,1,0:T(8,128)(2,1)S(1)} %bitcast.32), channel_id=1, replica_groups=mesh['xh'=2,'xl'=2,'yh'=2,'ylh'=2,'yll'=2,'zh'=2,'z2'=2,'zp'=2,'core'=2]..., dimensions={0} | all-to-all | bytes 1048576 | tf_op jit(solution)/shard_map/all_to_all | solution.py:399
  131.3 0.1 reduce_sum.12
  131.4 1.9 %collective-permute-start.7 = (bf16[128,128]{1,0:T(8,128)(2,1)S(1)}, bf16[128,128]{1,0:T(8,128)(2,1)S(1)}, u32[]{:S(2)}, u32[]{:S(2)}) collective-permute-start(bf16[128,128]{1,0:T(8,128)(2,1)S(1)} %reduce_sum.12), channel_id=1, source_target_pairs={{24,0},{25,1},{8,2},{9,3},{28,4},{29,5},{12,6},{13,7},{88,8},{89,9... | collective-permute-start | bytes 98312 | tf_op jit(solution)/shard_map/ppermute | solution.py:401
  133.3 0.5 slice_bitcast_fusion
  133.8 0.6 reshape.51
  134.4 8.6 %collective-permute-done.7 = bf16[128,128]{1,0:T(8,128)(2,1)S(1)} collective-permute-done((bf16[128,128]{1,0:T(8,128)(2,1)S(1)}, bf16[128,128]{1,0:T(8,128)(2,1)S(1)}, u32[]{:S(2)}, u32[]{:S(2)}) %collective-permute-start.7) | collective-permute-done | bytes 32800 | tf_op jit(solution)/shard_map/ppermute | solution.py:401
  143.0 0.6 copy.11
  (12 shorter events, 0.0 us)
Async XLA Ops:
  0.6 15.0 %collective-permute-start = (bf16[128,128]{1,0:T(8,128)(2,1)}, bf16[128,128]{1,0:T(8,128)(2,1)S(1)}, u32[]{:S(2)}, u32[]{:S(2)}) collective-permute-start(bf16[128,128]{1,0:T(8,128)(2,1)} %param.6), channel_id=1, source_target_pairs={{0,8},{8,72},{64,0},{72,64},{1,9},{9,73},{65,1},{73,65},{2,10},{10... | collective-permute-start | bytes 98312 | tf_op jit(solution)/shard_map/ppermute | solution.py:309
  10.7 23.3 %collective-permute-start.1 = (bf16[3,1024,128]{2,1,0:T(8,128)(2,1)}, bf16[3,1024,128]{2,1,0:T(8,128)(2,1)S(1)}, u32[]{:S(2)}, u32[]{:S(2)}) collective-permute-start(bf16[3,1024,128]{2,1,0:T(8,128)(2,1)} %bitcast.18), channel_id=1, source_target_pairs={{0,256},{128,384},{256,0},{384,128},{1,257},{129,385},{257,1},{385... | collective-permute-start | bytes 2359304 | tf_op jit(solution)/shard_map/ppermute | solution.py:313
  15.8 1.0 copy-start.1
  16.8 8.4 %copy-start = (bf16[1024,3,128]{2,0,1:T(8,128)(2,1)S(1)}, bf16[1024,3,128]{2,0,1:T(8,128)(2,1)}, u32[]{:S(2)}) copy-start(bf16[1024,3,128]{2,0,1:T(8,128)(2,1)} %param.7) | copy-start | bytes 2359300
  16.9 34.7 %all-to-all-start = ((bf16[32,128,128]{2,1,0:T(8,128)(2,1)}), bf16[32,128,128]{2,1,0:T(8,128)(2,1)S(1)}, u32[]{:S(2)}, u32[]{:S(2)}) async-start(bf16[32,128,128]{2,1,0:T(8,128)(2,1)} %copy-done.1), calls=%async_computation | async-start | bytes 2097152 | tf_op jit(solution)/shard_map/all_to_all | solution.py:348
  25.2 24.9 %collective-permute-start.3 = (bf16[3,1024,128]{2,1,0:T(8,128)(2,1)S(1)}, bf16[3,1024,128]{2,1,0:T(8,128)(2,1)S(1)}, u32[]{:S(2)}, u32[]{:S(2)}) collective-permute-start(bf16[3,1024,128]{2,1,0:T(8,128)(2,1)S(1)} %bitcast.19), channel_id=1, source_target_pairs={{0,384},{128,256},{256,128},{384,0},{1,385},{129,257},{257,129},{3... | collective-permute-start | bytes 2359304 | tf_op jit(solution)/shard_map/ppermute | solution.py:313
  29.9 21.6 %collective-permute-start.2 = (bf16[3,1024,128]{2,1,0:T(8,128)(2,1)S(1)}, bf16[3,1024,128]{2,1,0:T(8,128)(2,1)}, u32[]{:S(2)}, u32[]{:S(2)}) collective-permute-start(bf16[3,1024,128]{2,1,0:T(8,128)(2,1)S(1)} %bitcast.20), channel_id=1, source_target_pairs={{0,128},{128,0},{256,384},{384,256},{1,129},{129,1},{257,385},{385... | collective-permute-start | bytes 2359304 | tf_op jit(solution)/shard_map/ppermute | solution.py:313
  50.1 6.2 %copy-start.4 = (bf16[8,16,128]{2,1,0:T(8,128)(2,1)S(1)}, bf16[8,16,128]{2,1,0:T(8,128)(2,1)}, u32[]{:S(2)}) copy-start(bf16[8,16,128]{2,1,0:T(8,128)(2,1)} %get-tuple-element.30.grad_ref) | copy-start | bytes 98308
  51.6 4.8 %collective-permute-start.4 = (bf16[4,2,4,128,128]{4,3,2,1,0:T(8,128)(2,1)S(1)}, bf16[4,2,4,128,128]{4,3,2,1,0:T(8,128)(2,1)S(1)}, u32[]{:S(2)}, u32[]{:S(2)}) collective-permute-start(bf16[4,2,4,128,128]{4,3,2,1,0:T(8,128)(2,1)S(1)} %bitcast.27), channel_id=1, source_target_pairs={{0,1},{1,0},{2,3},{3,2},{4,5},{5,4},{6,7},{7,6},{8,9},{9,8},{10,11... | collective-permute-start | bytes 3145736 | tf_op jit(solution)/shard_map/ppermute | solution.py:353
  53.5 39.4 %collective-permute-start.5 = (bf16[2,3,1024,128]{3,2,1,0:T(8,128)(2,1)}, bf16[2,3,1024,128]{3,2,1,0:T(8,128)(2,1)}, u32[]{:S(2)}, u32[]{:S(2)}) collective-permute-start(bf16[2,3,1024,128]{3,2,1,0:T(8,128)(2,1)} %pad_maximum_fusion), channel_id=1, source_target_pairs={{0,2},{2,0},{1,3},{3,1},{4,6},{6,4},{5,7},{7,5},{8,10},{10,8},{9,1... | collective-permute-start | bytes 4718600 | tf_op jit(solution)/shard_map/ppermute | solution.py:352
  56.3 21.7 %copy-start.2 = (bf16[4,128,128]{2,1,0:T(8,128)(2,1)S(1)}, bf16[4,128,128]{2,1,0:T(8,128)(2,1)}, u32[]{:S(2)}) copy-start(bf16[4,128,128]{2,1,0:T(8,128)(2,1)} %get-tuple-element.32.band_ref) | copy-start | bytes 393220
  56.4 21.7 %copy-start.3 = (f32[128,128]{1,0:T(8,128)S(1)}, f32[128,128]{1,0:T(8,128)}, u32[]{:S(2)}) copy-start(f32[128,128]{1,0:T(8,128)} %table.1.table_ref) | copy-start | bytes 196612
  79.8 20.4 %all-to-all-start.2 = ((bf16[16,112,128]{2,1,0:T(8,128)(2,1)}), bf16[16,112,128]{2,1,0:T(8,128)(2,1)S(1)}, u32[]{:S(2)}, u32[]{:S(2)}) async-start(bf16[16,112,128]{2,1,0:T(8,128)(2,1)} %bitcast.9), calls=%async_computation.2 | async-start | bytes 917504 | tf_op jit(solution)/shard_map/all_to_all | solution.py:377
  103.0 3.8 %collective-permute-start.6 = (bf16[2,2,2,2,128,128]{5,4,3,2,1,0:T(8,128)(2,1)S(1)}, bf16[2,2,2,2,128,128]{5,4,3,2,1,0:T(8,128)(2,1)S(1)}, u32[]{:S(2)}, u32[]{:S(2)}) collective-permute-start(bf16[2,2,2,2,128,128]{5,4,3,2,1,0:T(8,128)(2,1)S(1)} %get-tuple-element.35), channel_id=1, source_target_pairs={{0,1},{1,0},{2,3},{3,2},{4,5},{5,4},{6,7},{7,6},{8,9},{9,8},{10,11... | collective-permute-start | bytes 1572872 | tf_op jit(solution)/shard_map/ppermute | solution.py:397
  131.4 11.6 %collective-permute-start.7 = (bf16[128,128]{1,0:T(8,128)(2,1)S(1)}, bf16[128,128]{1,0:T(8,128)(2,1)S(1)}, u32[]{:S(2)}, u32[]{:S(2)}) collective-permute-start(bf16[128,128]{1,0:T(8,128)(2,1)S(1)} %reduce_sum.12), channel_id=1, source_target_pairs={{24,0},{25,1},{8,2},{9,3},{28,4},{29,5},{12,6},{13,7},{88,8},{89,9... | collective-permute-start | bytes 98312 | tf_op jit(solution)/shard_map/ppermute | solution.py:401

commit v6 on v5

--- a/solution.py
+++ b/solution.py
@@ -13,7 +13,7 @@
 CTX = ("xh", "xl", "yh")
 TP = ("ylh", "yll", "zh", "z2", "zp", "core")
 SPREAD = ("ylh", "yll", "zh", "z2", "zp")
-RETURN = ("xh", "xl", "yh", "zp")
+RETURN = ("zp", "xh", "xl", "yh")
 COLUMNS = ("ylh", "yll", "zh", "z2")
 F32 = jnp.float32
 BF16 = jnp.bfloat16
@@ -76,18 +76,44 @@
         band_ref[place_at + 1] = (part - high.astype(F32)).astype(BF16)
 
 
+def arrived_kernel(in_ref, out_ref, tile, sem):
+    del out_ref
+    copy = pltpu.make_async_copy(in_ref.at[0, 0, 0, 0], tile, sem)
+    copy.start()
+    copy.wait()
+
+
+def arrived(weight):
+    return pl.pallas_call(
+        arrived_kernel,
+        out_shape=jax.ShapeDtypeStruct(weight.shape, weight.dtype),
+        in_specs=[ANY],
+        out_specs=ANY,
+        input_output_aliases={0: 0},
+        scratch_shapes=[pltpu.VMEM((128, 128), BF16), pltpu.SemaphoreType.DMA],
+        cost_estimate=pl.CostEstimate(flops=20000000000, bytes_accessed=1 << 16, transcendentals=0),
+        name="arrived",
+    )(weight)
+
+
 def weight_rows(weight, proj, side):
     return jnp.concatenate([weight[proj, z, side] for z in range(4)], axis=0)
 
 
-def project_kernel(own_ref, other_ref, w0, w1_far, w2, w3, grad_ref, out_ref, w1, sem):
-    copy = pltpu.make_async_copy(w1_far, w1, sem)
+def project_kernel(own_ref, other_ref, w0, w1, w2_late, w3, grad_ref, out_ref, w2, sem, grad_sems):
+    copy = pltpu.make_async_copy(w2_late, w2, sem)
     copy.start()
+    grads = [
+        pltpu.make_async_copy(grad_ref.at[k], out_ref.at[k, 96:ROWS], grad_sems.at[k])
+        for k in range(8)
+    ]
+    for grad in grads:
+        grad.start()
     x = x_index()
     core = lax.axis_index("core")
     totals = [jnp.zeros((256, 128), F32) for _ in range(3)]
-    for away, weight in ((0, w0), (2, w2), (3, w3), (1, w1)):
-        if away == 1:
+    for away, weight in ((0, w0), (1, w1), (3, w3), (2, w2)):
+        if away == 2:
             copy.wait()
         block = x ^ away
         for ref, side in ((own_ref, core), (other_ref, 1 - core)):
@@ -110,8 +136,8 @@
                 out_ref[group, start : start + 16, :] = turned[
                     group * 16 : group * 16 + 16, half * 128 : half * 128 + 128
                 ]
-    for group in range(8):
-        out_ref[group, 96:ROWS, :] = grad_ref[group]
+    for grad in grads:
+        grad.wait()
 
 
 def mixer_kernel(in_ref, table_ref, band_ref, out_ref):
@@ -207,7 +233,7 @@
                 for yh in range(2):
                     piece = 128 * (4 * xh + 2 * (zp ^ xl) + yh)
                     start = (2 * proj + yh) * 16
-                    out_ref[ctx_to, zp, start : start + 16, :] = dfeat[:, piece : piece + 128]
+                    out_ref[zp, ctx_to, start : start + 16, :] = dfeat[:, piece : piece + 128]
     small_high = small.astype(BF16).astype(F32)
     small_both = jnp.where(lane16 < 16, small_high, small - small_high)
     filter_high = filter_grad.astype(BF16).astype(F32)
@@ -223,7 +249,7 @@
     extra = extra.astype(BF16)
     for i in range(8):
         for zp in range(2):
-            out_ref[i, zp, 96:ROWS, :] = extra
+            out_ref[zp, i, 96:ROWS, :] = extra
 
 
 def back_kernel(
@@ -246,7 +272,7 @@
             for proj in range(3):
                 start = (2 * proj + half) * 16
                 block = jnp.concatenate(
-                    [in_ref[i, of_z, start : start + 16, :] for i in range(8)], axis=0
+                    [in_ref[of_z, i, start : start + 16, :] for i in range(8)], axis=0
                 )
                 columns.append(block.astype(F32).T.astype(BF16))
         halves.append(jnp.concatenate(columns, axis=1))
@@ -272,7 +298,7 @@
                     ref[high, low, 1 - half, z2] = result[
                         half * 128 : half * 128 + 128, z * 128 : z * 128 + 128
                     ]
-    extra = [in_ref[i, zp, 96:ROWS, :].astype(F32) for i in range(8)]
+    extra = [in_ref[zp, i, 96:ROWS, :].astype(F32) for i in range(8)]
     turned = jnp.concatenate(extra, axis=0).T
     small_ref[...] = turned[0:16] + turned[16:32]
     lane = lax.broadcasted_iota(jnp.int32, (1, 128), 1)
@@ -311,11 +337,13 @@
     moved, late = lax.optimization_barrier((moved, own))
     weights = [own] + [
         lax.ppermute(part, X, [(i, i ^ away) for i in range(4)])
-        for part, away in ((late, 1), (own, 2), (late, 3))
+        for part, away in ((own, 1), (late, 2), (own, 3))
     ]
     pair_rows = jnp.stack([own, weights[3]])
 
-    out_grad, short_taps, weights[2] = lax.optimization_barrier((out_grad, short_taps, weights[2]))
+    out_grad, short_taps, weights[1], weights[3] = lax.optimization_barrier(
+        (out_grad, short_taps, weights[1], weights[3])
+    )
     grad_t, band = pl.pallas_call(
         prepare_kernel,
         out_shape=(
@@ -346,10 +374,10 @@
         name="copies",
     )(moved)
     whole = lax.all_to_all(copies, SPREAD, 0, 0, tiled=True).reshape(4, 2, 4, 128, 128)
-    whole, grad_t, table, band, weights[1], pair_rows = lax.optimization_barrier(
-        (whole, grad_t, table, band, weights[1], pair_rows)
-    )
     w_z = lax.ppermute(pair_rows, "zp", pair).reshape(2, 3, 4, 2, 128, 128)
+    whole, grad_t, table, band, weights[2] = lax.optimization_barrier(
+        (whole, grad_t, table, band, weights[2])
+    )
     across = lax.ppermute(whole, "core", pair)
 
     cost = pl.CostEstimate(flops=2 * 256 * 4096 * 384, bytes_accessed=5 << 20, transcendentals=0)
@@ -357,9 +385,13 @@
     partial = pl.pallas_call(
         project_kernel,
         out_shape=mixed_shape,
-        in_specs=[VMEM] * 3 + [ANY] + [VMEM] * 3,
+        in_specs=[VMEM] * 4 + [ANY, VMEM, ANY],
         out_specs=VMEM,
-        scratch_shapes=[pltpu.VMEM((3, 4, 2, 128, 128), BF16), pltpu.SemaphoreType.DMA],
+        scratch_shapes=[
+            pltpu.VMEM((3, 4, 2, 128, 128), BF16),
+            pltpu.SemaphoreType.DMA,
+            pltpu.SemaphoreType.DMA((8,)),
+        ],
         compiler_params=params(40),
         cost_estimate=cost,
         name="project",
@@ -368,7 +400,7 @@
 
     cotangent = pl.pallas_call(
         mixer_kernel,
-        out_shape=jax.ShapeDtypeStruct((8, 2, ROWS, 128), BF16),
+        out_shape=jax.ShapeDtypeStruct((2, 8, ROWS, 128), BF16),
         in_specs=[VMEM] * 3,
         out_specs=VMEM,
         compiler_params=params(40),
@@ -376,7 +408,7 @@
     )(spread, table, band)
     gathered = lax.all_to_all(
         cotangent.reshape(16, ROWS, 128), RETURN, 0, 0, tiled=True
-    ).reshape(8, 2, ROWS, 128)
+    ).reshape(2, 8, ROWS, 128)
 
     back_shape = jax.ShapeDtypeStruct((2, 2, 2, 2, 128, 128), BF16)
     back_own, back_other, filter_grad, small = pl.pallas_call(
@@ -393,7 +425,7 @@
         compiler_params=params(40),
         cost_estimate=cost,
         name="back",
-    )(gathered, weights[0], weights[3], w_z)
+    )(gathered, weights[0], weights[3], arrived(w_z))
     received = lax.ppermute(back_other, "core", pair)
     back = (back_own.astype(F32) + received.astype(F32)).astype(BF16)
     parts = lax.all_to_all(back.reshape(16, 128, 128), COLUMNS, 0, 0, tiled=True)

time: 144 us -> 143 us (level)
  starting transfers between devices: 43 us -> 40.8 us
  blocking collectives: 43.9 us -> 41.8 us
    ppermute x1, waiting for transfers between devices: 8.81 us -> 0.01 us  [on_device(): w_z = lax.ppermute(pair_rows, 'zp', pair).reshape(2, 3, 4, 2, 128, 128)]
    all_to_all x1, waiting for transfers between devices: 7.27 us -> 14.2 us  [on_device(): lax.all_to_all(cotangent.reshape(16, ROWS, 128), RETURN, 0, 0, tiled=True)]
    ppermute x1, waiting for transfers between devices: 0.01 us -> 2.63 us  [on_device(): across = lax.ppermute(whole, 'core', pair)]
    all_to_all x1, blocking collectives: 19.6 us -> 18 us  [on_device(): spread = lax.all_to_all(partial, CTX, 0, 0, tiled=True)]
    pallas_call x2 -> x3, Pallas kernels: 3.78 us -> 4.66 us  [the longest x1 2.15 us: on_device(): pl.pallas_call(project_kernel, out_shape=mixed_shape, in_specs=[VMEM] * 4...]
  transfers between devices with their start and end apart: 10 -> 10, of which waited for: 7 -> 8; matrix products, arithmetic and copies ran while one was open for 2% -> 2% of each run, Pallas kernels for 5% -> 6%
where the time goes in v6:
time: 143 us; the launch traced here: 142 us
  waiting for transfers between devices  42.9 us (30%)
  blocking collectives  41.8 us (29%)
  starting transfers between devices  40.8 us (29%)
  Pallas kernels  11.1 us (8%)
  local copies, waits for them, and re-layouts  3.51 us (2%)
  other arithmetic  1.5 us (1%)
    all_to_all x1, blocking collectives, on_device(): lax.all_to_all(back.reshape(16, 128, 128), COLUMNS, 0, 0, tiled=True)  23.8 us
    all_to_all x1, blocking collectives, on_device(): spread = lax.all_to_all(partial, CTX, 0, 0, tiled=True)  18 us
    ppermute x3, waiting for transfers between devices, on_device(): lax.ppermute(part, X, [(i, i ^ away) for i in range(4)])  15.4 us
    all_to_all x1, waiting for transfers between devices, on_device(): lax.all_to_all(cotangent.reshape(16, ROWS, 128), RETURN, 0, 0, tiled=True)  14.2 us
    ppermute x3, starting transfers between devices, on_device(): lax.ppermute(part, X, [(i, i ^ away) for i in range(4)])  10.4 us
    ppermute x1, starting transfers between devices, on_device(): moved = lax.ppermute(tokens, ('yh', 'zh'), QUARTER_TURN)  10 us
    ppermute x1, waiting for transfers between devices, on_device(): input_grad = lax.ppermute(summed, AXES, grad_route())  8.56 us
    all_to_all x1, starting transfers between devices, on_device(): lax.all_to_all(copies, SPREAD, 0, 0, tiled=True).reshape(4, 2, 4, 128, 128)  8.23 us
  transfers between devices with their start and end apart: 10, of which 8 were waited for; matrix products, arithmetic and copies ran while one was open for 2% of the time, Pallas kernels for 6%

profile of v6, /device:TPU:80, one launch (start us, length us, event | category | flops | bytes accessed | tf_op | source)
XLA Modules:
  0.0 142.4 jit_solution(10230716439399518013)
XLA Ops:
  0.6 10.0 %collective-permute-start = (bf16[128,128]{1,0:T(8,128)(2,1)}, bf16[128,128]{1,0:T(8,128)(2,1)S(1)}, u32[]{:S(2)}, u32[]{:S(2)}) collective-permute-start(bf16[128,128]{1,0:T(8,128)(2,1)} %param.6), channel_id=1, source_target_pairs={{0,8},{8,72},{64,0},{72,64},{1,9},{9,73},{65,1},{73,65},{2,10},{10... | collective-permute-start | bytes 98312 | tf_op jit(solution)/shard_map/ppermute | solution.py:335
  10.7 4.7 %collective-permute-start.2 = (bf16[3,1024,128]{2,1,0:T(8,128)(2,1)}, bf16[3,1024,128]{2,1,0:T(8,128)(2,1)S(1)}, u32[]{:S(2)}, u32[]{:S(2)}) collective-permute-start(bf16[3,1024,128]{2,1,0:T(8,128)(2,1)} %bitcast.18), channel_id=1, source_target_pairs={{0,384},{128,256},{256,128},{384,0},{1,385},{129,257},{257,129},{3... | collective-permute-start | bytes 2359304 | tf_op jit(solution)/shard_map/ppermute | solution.py:339
  15.3 2.1 %collective-permute-start.1 = (bf16[3,1024,128]{2,1,0:T(8,128)(2,1)}, bf16[3,1024,128]{2,1,0:T(8,128)(2,1)S(1)}, u32[]{:S(2)}, u32[]{:S(2)}) collective-permute-start(bf16[3,1024,128]{2,1,0:T(8,128)(2,1)} %bitcast.19), channel_id=1, source_target_pairs={{0,128},{128,0},{256,384},{384,256},{1,129},{129,1},{257,385},{385... | collective-permute-start | bytes 2359304 | tf_op jit(solution)/shard_map/ppermute | solution.py:339
  17.7 1.0 copy-done.1
  18.7 8.2 %all-to-all-start = ((bf16[32,128,128]{2,1,0:T(8,128)(2,1)}), bf16[32,128,128]{2,1,0:T(8,128)(2,1)S(1)}, u32[]{:S(2)}, u32[]{:S(2)}) async-start(bf16[32,128,128]{2,1,0:T(8,128)(2,1)} %copy-done.1), calls=%async_computation | async-start | bytes 2097152 | tf_op jit(solution)/shard_map/all_to_all | solution.py:376
  27.0 3.6 %collective-permute-start.3 = (bf16[3,1024,128]{2,1,0:T(8,128)(2,1)S(1)}, bf16[3,1024,128]{2,1,0:T(8,128)(2,1)}, u32[]{:S(2)}, u32[]{:S(2)}) collective-permute-start(bf16[3,1024,128]{2,1,0:T(8,128)(2,1)S(1)} %bitcast.20), channel_id=1, source_target_pairs={{0,256},{128,384},{256,0},{384,128},{1,257},{129,385},{257,1},{385... | collective-permute-start | bytes 2359304 | tf_op jit(solution)/shard_map/ppermute | solution.py:339
  30.6 2.4 %collective-permute-done.2 = bf16[3,1024,128]{2,1,0:T(8,128)(2,1)S(1)} collective-permute-done((bf16[3,1024,128]{2,1,0:T(8,128)(2,1)}, bf16[3,1024,128]{2,1,0:T(8,128)(2,1)S(1)}, u32[]{:S(2)}, u32[]{:S(2)}) %collective-permute-start.2) | collective-permute-done | bytes 786464 | tf_op jit(solution)/shard_map/ppermute | solution.py:339
  33.0 4.9 %collective-permute-done.1 = bf16[3,1024,128]{2,1,0:T(8,128)(2,1)S(1)} collective-permute-done((bf16[3,1024,128]{2,1,0:T(8,128)(2,1)}, bf16[3,1024,128]{2,1,0:T(8,128)(2,1)S(1)}, u32[]{:S(2)}, u32[]{:S(2)}) %collective-permute-start.1) | collective-permute-done | bytes 786464 | tf_op jit(solution)/shard_map/ppermute | solution.py:339
  37.9 1.3 pad_maximum_fusion
  39.2 2.5 %collective-permute-start.5 = (bf16[2,3,1024,128]{3,2,1,0:T(8,128)(2,1)}, bf16[2,3,1024,128]{3,2,1,0:T(8,128)(2,1)}, u32[]{:S(2)}, u32[]{:S(2)}) collective-permute-start(bf16[2,3,1024,128]{3,2,1,0:T(8,128)(2,1)} %pad_maximum_fusion), channel_id=1, source_target_pairs={{0,2},{2,0},{1,3},{3,1},{4,6},{6,4},{5,7},{7,5},{8,10},{10,8},{9,1... | collective-permute-start | bytes 4718600 | tf_op jit(solution)/shard_map/ppermute | solution.py:377
  41.7 1.4 table.1.table_ref
  43.1 1.9 %prepare.1 = (bf16[8,16,128]{2,1,0:T(8,128)(2,1)}, bf16[4,128,128]{2,1,0:T(8,128)(2,1)}) custom-call(bf16[128,128]{1,0:T(8,128)(2,1)} %grad_ref, f32[8,128]{1,0:T(8,128)} %filter_ref.1), custom_call_target="tpu_custom_call" | custom-call | tf_op jit(solution)/shard_map/prepare/pallas_call | solution.py:347
  45.0 8.1 %collective-permute-done.3 = bf16[3,1024,128]{2,1,0:T(8,128)(2,1)} collective-permute-done((bf16[3,1024,128]{2,1,0:T(8,128)(2,1)S(1)}, bf16[3,1024,128]{2,1,0:T(8,128)(2,1)}, u32[]{:S(2)}, u32[]{:S(2)}) %collective-permute-start.3) | collective-permute-done | bytes 786464 | tf_op jit(solution)/shard_map/ppermute | solution.py:339
  53.0 0.3 all-to-all-done
  53.3 1.9 %collective-permute-start.4 = (bf16[4,2,4,128,128]{4,3,2,1,0:T(8,128)(2,1)S(1)}, bf16[4,2,4,128,128]{4,3,2,1,0:T(8,128)(2,1)S(1)}, u32[]{:S(2)}, u32[]{:S(2)}) collective-permute-start(bf16[4,2,4,128,128]{4,3,2,1,0:T(8,128)(2,1)S(1)} %bitcast.27), channel_id=1, source_target_pairs={{0,1},{1,0},{2,3},{3,2},{4,5},{5,4},{6,7},{7,6},{8,9},{9,8},{10,11... | collective-permute-start | bytes 3145736 | tf_op jit(solution)/shard_map/ppermute | solution.py:381
  55.2 2.6 %collective-permute-done.4.other_ref = bf16[4,2,4,128,128]{4,3,2,1,0:T(8,128)(2,1)S(1)} collective-permute-done((bf16[4,2,4,128,128]{4,3,2,1,0:T(8,128)(2,1)S(1)}, bf16[4,2,4,128,128]{4,3,2,1,0:T(8,128)(2,1)S(1)}, u32[]{:S(2)}, u32[]{:S(2)}) %collective-permute-start.4) | collective-permute-done | bytes 1048608 | tf_op jit(solution)/shard_map/ppermute | solution.py:381
  57.8 0.8 copy-done.4
  58.6 2.1 %project.1 = bf16[8,112,128]{2,1,0:T(8,128)(2,1)S(1)} custom-call(bf16[4,2,4,128,128]{4,3,2,1,0:T(8,128)(2,1)S(1)} %bitcast.28, bf16[4,2,4,128,128]{4,3,2,1,0:T(8,128)(2,1)S(1)} %collective-permute-done.4.other_ref, bf16[3,4,2,128,128]{4,3,2,1,0:T(8,128)(2,1)S(1)} %bitcast.22, bf16[3,4,2,128,128]{4,3,2,1,0:T(8,128)(2,1)S(1)} %bitcast.30, ...), custom_call_target="tpu_custom_call" | custom-call | flops 805306368 | bytes 5242880 | tf_op jit(solution)/shard_map/project/pallas_call | solution.py:385
  60.8 18.0 %all_to_all.20.in_ref = bf16[8,112,128]{2,1,0:T(8,128)(2,1)S(1)} all-to-all(bf16[8,112,128]{2,1,0:T(8,128)(2,1)S(1)} %project.1), channel_id=1, replica_groups=mesh['xh'=2,'xl'=2,'yh'=2,'ylh'=2,'yll'=2,'zh'=2,'z2'=2,'zp'=2,'core'=2]..., dimensions={0} | all-to-all | bytes 458752 | tf_op jit(solution)/shard_map/all_to_all | solution.py:399
  78.7 1.7 %mixer.1 = bf16[2,8,112,128]{3,2,1,0:T(8,128)(2,1)} custom-call(bf16[8,112,128]{2,1,0:T(8,128)(2,1)S(1)} %all_to_all.20.in_ref, f32[128,128]{1,0:T(8,128)S(1)} %copy-done.3, bf16[4,128,128]{2,1,0:T(8,128)(2,1)S(1)} %copy-done.2), custom_call_target="tpu_custom_call" | custom-call | tf_op jit(solution)/shard_map/mixer/pallas_call | solution.py:401
  80.5 3.9 %all-to-all-start.2 = ((bf16[16,112,128]{2,1,0:T(8,128)(2,1)}), bf16[16,112,128]{2,1,0:T(8,128)(2,1)S(1)}, u32[]{:S(2)}, u32[]{:S(2)}) async-start(bf16[16,112,128]{2,1,0:T(8,128)(2,1)} %bitcast.7), calls=%async_computation.2 | async-start | bytes 917504 | tf_op jit(solution)/shard_map/all_to_all | solution.py:409
  84.4 0.8 arrived.1.w_far
  85.2 14.2 %all-to-all-done.2 = bf16[16,112,128]{2,1,0:T(8,128)(2,1)S(1)} async-done(((bf16[16,112,128]{2,1,0:T(8,128)(2,1)}), bf16[16,112,128]{2,1,0:T(8,128)(2,1)S(1)}, u32[]{:S(2)}, u32[]{:S(2)}) %all-to-all-start.2) | async-done | bytes 458784 | tf_op jit(solution)/shard_map/all_to_all | solution.py:409
  99.4 2.9 %back.1 = (bf16[2,2,2,2,128,128]{5,4,3,2,1,0:T(8,128)(2,1)S(1)}, bf16[2,2,2,2,128,128]{5,4,3,2,1,0:T(8,128)(2,1)S(1)}, f32[8,128]{1,0:T(8,128)}, f32[16,128]{1,0:T(8,128)S(1)}) custom-call(bf16[2,8,112,128]{3,2,1,0:T(8,128)(2,1)S(1)} %bitcast.29, bf16[3,4,2,128,128]{4,3,2,1,0:T(8,128)(2,1)S(1)} %bitcast.23, bf16[3,4,2,128,128]{4,3,2,1,0:T(8,128)(2,1)S(1)} %bitcast.26, ...), custom_call_target="tpu_custom_call" | custom-call | flops 805306368 | bytes 5242880 | tf_op jit(solution)/shard_map/back/pallas_call | solution.py:414
  102.3 1.9 %collective-permute-start.6 = (bf16[2,2,2,2,128,128]{5,4,3,2,1,0:T(8,128)(2,1)S(1)}, bf16[2,2,2,2,128,128]{5,4,3,2,1,0:T(8,128)(2,1)S(1)}, u32[]{:S(2)}, u32[]{:S(2)}) collective-permute-start(bf16[2,2,2,2,128,128]{5,4,3,2,1,0:T(8,128)(2,1)S(1)} %get-tuple-element.35), channel_id=1, source_target_pairs={{0,1},{1,0},{2,3},{3,2},{4,5},{5,4},{6,7},{7,6},{8,9},{9,8},{10,11... | collective-permute-start | bytes 1572872 | tf_op jit(solution)/shard_map/ppermute | solution.py:429
  104.2 1.9 %collective-permute-done.6 = bf16[2,2,2,2,128,128]{5,4,3,2,1,0:T(8,128)(2,1)S(1)} collective-permute-done((bf16[2,2,2,2,128,128]{5,4,3,2,1,0:T(8,128)(2,1)S(1)}, bf16[2,2,2,2,128,128]{5,4,3,2,1,0:T(8,128)(2,1)S(1)}, u32[]{:S(2)}, u32[]{:S(2)}) %collective-permute-start.6) | collective-permute-done | bytes 524320 | tf_op jit(solution)/shard_map/ppermute | solution.py:429
  106.2 23.8 %all_to_all.21 = bf16[16,128,128]{2,1,0:T(8,128)(2,1)S(1)} all-to-all(bf16[16,128,128]{2,1,0:T(8,128)(2,1)S(1)} %bitcast.32), channel_id=1, replica_groups=mesh['xh'=2,'xl'=2,'yh'=2,'ylh'=2,'yll'=2,'zh'=2,'z2'=2,'zp'=2,'core'=2]..., dimensions={0} | all-to-all | bytes 1048576 | tf_op jit(solution)/shard_map/all_to_all | solution.py:431
  130.2 1.9 %collective-permute-start.7 = (bf16[128,128]{1,0:T(8,128)(2,1)S(1)}, bf16[128,128]{1,0:T(8,128)(2,1)S(1)}, u32[]{:S(2)}, u32[]{:S(2)}) collective-permute-start(bf16[128,128]{1,0:T(8,128)(2,1)S(1)} %reduce_sum.12), channel_id=1, source_target_pairs={{24,0},{25,1},{8,2},{9,3},{28,4},{29,5},{12,6},{13,7},{88,8},{89,9... | collective-permute-start | bytes 98312 | tf_op jit(solution)/shard_map/ppermute | solution.py:433
  132.1 0.5 slice_bitcast_fusion
  132.6 0.6 reshape.51
  133.2 8.6 %collective-permute-done.7 = bf16[128,128]{1,0:T(8,128)(2,1)S(1)} collective-permute-done((bf16[128,128]{1,0:T(8,128)(2,1)S(1)}, bf16[128,128]{1,0:T(8,128)(2,1)S(1)}, u32[]{:S(2)}, u32[]{:S(2)}) %collective-permute-start.7) | collective-permute-done | bytes 32800 | tf_op jit(solution)/shard_map/ppermute | solution.py:433
  141.8 0.6 copy.13
  (13 shorter events, 0.5 us)
Async XLA Ops:
  0.6 16.8 %collective-permute-start = (bf16[128,128]{1,0:T(8,128)(2,1)}, bf16[128,128]{1,0:T(8,128)(2,1)S(1)}, u32[]{:S(2)}, u32[]{:S(2)}) collective-permute-start(bf16[128,128]{1,0:T(8,128)(2,1)} %param.6), channel_id=1, source_target_pairs={{0,8},{8,72},{64,0},{72,64},{1,9},{9,73},{65,1},{73,65},{2,10},{10... | collective-permute-start | bytes 98312 | tf_op jit(solution)/shard_map/ppermute | solution.py:335
  10.7 22.3 %collective-permute-start.2 = (bf16[3,1024,128]{2,1,0:T(8,128)(2,1)}, bf16[3,1024,128]{2,1,0:T(8,128)(2,1)S(1)}, u32[]{:S(2)}, u32[]{:S(2)}) collective-permute-start(bf16[3,1024,128]{2,1,0:T(8,128)(2,1)} %bitcast.18), channel_id=1, source_target_pairs={{0,384},{128,256},{256,128},{384,0},{1,385},{129,257},{257,129},{3... | collective-permute-start | bytes 2359304 | tf_op jit(solution)/shard_map/ppermute | solution.py:339
  15.3 22.6 %collective-permute-start.1 = (bf16[3,1024,128]{2,1,0:T(8,128)(2,1)}, bf16[3,1024,128]{2,1,0:T(8,128)(2,1)S(1)}, u32[]{:S(2)}, u32[]{:S(2)}) collective-permute-start(bf16[3,1024,128]{2,1,0:T(8,128)(2,1)} %bitcast.19), channel_id=1, source_target_pairs={{0,128},{128,0},{256,384},{384,256},{1,129},{129,1},{257,385},{385... | collective-permute-start | bytes 2359304 | tf_op jit(solution)/shard_map/ppermute | solution.py:339
  17.7 1.0 copy-start.1
  18.7 8.2 %copy-start = (bf16[1024,3,128]{2,0,1:T(8,128)(2,1)S(1)}, bf16[1024,3,128]{2,0,1:T(8,128)(2,1)}, u32[]{:S(2)}) copy-start(bf16[1024,3,128]{2,0,1:T(8,128)(2,1)} %param.7) | copy-start | bytes 2359300
  18.7 34.6 %all-to-all-start = ((bf16[32,128,128]{2,1,0:T(8,128)(2,1)}), bf16[32,128,128]{2,1,0:T(8,128)(2,1)S(1)}, u32[]{:S(2)}, u32[]{:S(2)}) async-start(bf16[32,128,128]{2,1,0:T(8,128)(2,1)} %copy-done.1), calls=%async_computation | async-start | bytes 2097152 | tf_op jit(solution)/shard_map/all_to_all | solution.py:376
  27.0 26.0 %collective-permute-start.3 = (bf16[3,1024,128]{2,1,0:T(8,128)(2,1)S(1)}, bf16[3,1024,128]{2,1,0:T(8,128)(2,1)}, u32[]{:S(2)}, u32[]{:S(2)}) collective-permute-start(bf16[3,1024,128]{2,1,0:T(8,128)(2,1)S(1)} %bitcast.20), channel_id=1, source_target_pairs={{0,256},{128,384},{256,0},{384,128},{1,257},{129,385},{257,1},{385... | collective-permute-start | bytes 2359304 | tf_op jit(solution)/shard_map/ppermute | solution.py:339
  39.2 45.2 %collective-permute-start.5 = (bf16[2,3,1024,128]{3,2,1,0:T(8,128)(2,1)}, bf16[2,3,1024,128]{3,2,1,0:T(8,128)(2,1)}, u32[]{:S(2)}, u32[]{:S(2)}) collective-permute-start(bf16[2,3,1024,128]{3,2,1,0:T(8,128)(2,1)} %pad_maximum_fusion), channel_id=1, source_target_pairs={{0,2},{2,0},{1,3},{3,1},{4,6},{6,4},{5,7},{7,5},{8,10},{10,8},{9,1... | collective-permute-start | bytes 4718600 | tf_op jit(solution)/shard_map/ppermute | solution.py:377
  53.3 4.5 %collective-permute-start.4 = (bf16[4,2,4,128,128]{4,3,2,1,0:T(8,128)(2,1)S(1)}, bf16[4,2,4,128,128]{4,3,2,1,0:T(8,128)(2,1)S(1)}, u32[]{:S(2)}, u32[]{:S(2)}) collective-permute-start(bf16[4,2,4,128,128]{4,3,2,1,0:T(8,128)(2,1)S(1)} %bitcast.27), channel_id=1, source_target_pairs={{0,1},{1,0},{2,3},{3,2},{4,5},{5,4},{6,7},{7,6},{8,9},{9,8},{10,11... | collective-permute-start | bytes 3145736 | tf_op jit(solution)/shard_map/ppermute | solution.py:381
  57.8 0.8 copy-start.4
  58.6 20.1 %copy-start.2 = (bf16[4,128,128]{2,1,0:T(8,128)(2,1)S(1)}, bf16[4,128,128]{2,1,0:T(8,128)(2,1)}, u32[]{:S(2)}) copy-start(bf16[4,128,128]{2,1,0:T(8,128)(2,1)} %get-tuple-element.33.band_ref) | copy-start | bytes 393220
  58.6 20.1 %copy-start.3 = (f32[128,128]{1,0:T(8,128)S(1)}, f32[128,128]{1,0:T(8,128)}, u32[]{:S(2)}) copy-start(f32[128,128]{1,0:T(8,128)} %table.1.table_ref) | copy-start | bytes 196612
  80.5 18.9 %all-to-all-start.2 = ((bf16[16,112,128]{2,1,0:T(8,128)(2,1)}), bf16[16,112,128]{2,1,0:T(8,128)(2,1)S(1)}, u32[]{:S(2)}, u32[]{:S(2)}) async-start(bf16[16,112,128]{2,1,0:T(8,128)(2,1)} %bitcast.7), calls=%async_computation.2 | async-start | bytes 917504 | tf_op jit(solution)/shard_map/all_to_all | solution.py:409
  102.3 3.8 %collective-permute-start.6 = (bf16[2,2,2,2,128,128]{5,4,3,2,1,0:T(8,128)(2,1)S(1)}, bf16[2,2,2,2,128,128]{5,4,3,2,1,0:T(8,128)(2,1)S(1)}, u32[]{:S(2)}, u32[]{:S(2)}) collective-permute-start(bf16[2,2,2,2,128,128]{5,4,3,2,1,0:T(8,128)(2,1)S(1)} %get-tuple-element.35), channel_id=1, source_target_pairs={{0,1},{1,0},{2,3},{3,2},{4,5},{5,4},{6,7},{7,6},{8,9},{9,8},{10,11... | collective-permute-start | bytes 1572872 | tf_op jit(solution)/shard_map/ppermute | solution.py:429
  130.2 11.6 %collective-permute-start.7 = (bf16[128,128]{1,0:T(8,128)(2,1)S(1)}, bf16[128,128]{1,0:T(8,128)(2,1)S(1)}, u32[]{:S(2)}, u32[]{:S(2)}) collective-permute-start(bf16[128,128]{1,0:T(8,128)(2,1)S(1)} %reduce_sum.12), channel_id=1, source_target_pairs={{24,0},{25,1},{8,2},{9,3},{28,4},{29,5},{12,6},{13,7},{88,8},{89,9... | collective-permute-start | bytes 98312 | tf_op jit(solution)/shard_map/ppermute | solution.py:433

commit v7 on v6

--- a/solution.py
+++ b/solution.py
@@ -61,8 +61,7 @@
     table_ref[...] = rows.T
 
 
-def prepare_kernel(grad_ref, filter_ref, grad_t_ref, band_ref):
-    grad_t_ref[...] = grad_ref[...].astype(F32).T.astype(BF16).reshape(8, 16, HALF)
+def prepare_kernel(filter_ref, band_ref):
     band = rolled_rows(
         jnp.broadcast_to(filter_ref[pl.ds(ctx_index(), 1), :], (128, 128)), False
     )
@@ -100,15 +99,9 @@
     return jnp.concatenate([weight[proj, z, side] for z in range(4)], axis=0)
 
 
-def project_kernel(own_ref, other_ref, w0, w1, w2_late, w3, grad_ref, out_ref, w2, sem, grad_sems):
+def project_kernel(own_ref, other_ref, w0, w1, w2_late, w3, grad_ref, out_ref, w2, sem):
     copy = pltpu.make_async_copy(w2_late, w2, sem)
     copy.start()
-    grads = [
-        pltpu.make_async_copy(grad_ref.at[k], out_ref.at[k, 96:ROWS], grad_sems.at[k])
-        for k in range(8)
-    ]
-    for grad in grads:
-        grad.start()
     x = x_index()
     core = lax.axis_index("core")
     totals = [jnp.zeros((256, 128), F32) for _ in range(3)]
@@ -136,8 +129,9 @@
                 out_ref[group, start : start + 16, :] = turned[
                     group * 16 : group * 16 + 16, half * 128 : half * 128 + 128
                 ]
-    for grad in grads:
-        grad.wait()
+    turned = grad_ref[...].astype(F32).T.astype(BF16)
+    for group in range(8):
+        out_ref[group, 96:ROWS, :] = turned[group * 16 : group * 16 + 16]
 
 
 def mixer_kernel(in_ref, table_ref, band_ref, out_ref):
@@ -341,19 +335,16 @@
     ]
     pair_rows = jnp.stack([own, weights[3]])
 
-    out_grad, short_taps, weights[1], weights[3] = lax.optimization_barrier(
-        (out_grad, short_taps, weights[1], weights[3])
+    long_filter, short_taps, weights[1], weights[3] = lax.optimization_barrier(
+        (long_filter, short_taps, weights[1], weights[3])
     )
-    grad_t, band = pl.pallas_call(
+    band = pl.pallas_call(
         prepare_kernel,
-        out_shape=(
-            jax.ShapeDtypeStruct((8, 16, HALF), BF16),
-            jax.ShapeDtypeStruct((4, 128, 128), BF16),
-        ),
-        in_specs=[VMEM] * 2,
-        out_specs=(VMEM,) * 2,
+        out_shape=jax.ShapeDtypeStruct((4, 128, 128), BF16),
+        in_specs=[VMEM],
+        out_specs=VMEM,
         name="prepare",
-    )(out_grad, long_filter)
+    )(long_filter)
     table = pl.pallas_call(
         table_kernel,
         out_shape=jax.ShapeDtypeStruct((128, 128), F32),
@@ -375,9 +366,7 @@
     )(moved)
     whole = lax.all_to_all(copies, SPREAD, 0, 0, tiled=True).reshape(4, 2, 4, 128, 128)
     w_z = lax.ppermute(pair_rows, "zp", pair).reshape(2, 3, 4, 2, 128, 128)
-    whole, grad_t, table, band, weights[2] = lax.optimization_barrier(
-        (whole, grad_t, table, band, weights[2])
-    )
+    whole, table, band, weights[2] = lax.optimization_barrier((whole, table, band, weights[2]))
     across = lax.ppermute(whole, "core", pair)
 
     cost = pl.CostEstimate(flops=2 * 256 * 4096 * 384, bytes_accessed=5 << 20, transcendentals=0)
@@ -385,17 +374,16 @@
     partial = pl.pallas_call(
         project_kernel,
         out_shape=mixed_shape,
-        in_specs=[VMEM] * 4 + [ANY, VMEM, ANY],
+        in_specs=[VMEM] * 4 + [ANY, VMEM, VMEM],
         out_specs=VMEM,
         scratch_shapes=[
             pltpu.VMEM((3, 4, 2, 128, 128), BF16),
             pltpu.SemaphoreType.DMA,
-            pltpu.SemaphoreType.DMA((8,)),
         ],
         compiler_params=params(40),
         cost_estimate=cost,
         name="project",
-    )(whole, across, *weights, grad_t)
+    )(whole, across, *weights, out_grad)
     spread = lax.all_to_all(partial, CTX, 0, 0, tiled=True)
 
     cotangent = pl.pallas_call(

time: 143 us -> 142 us (level)
  transfers between devices with their start and end apart: 10 -> 10, of which waited for: 8 -> 9; matrix products, arithmetic and copies ran while one was open for 2% -> 2% of each run, Pallas kernels for 6% -> 6%
where the time goes in v7:
time: 142 us
  waiting for transfers between devices  43 us (30%)
  blocking collectives  41.8 us (29%)
  starting transfers between devices  40.8 us (29%)
  Pallas kernels  10.8 us (8%)
  local copies, waits for them, and re-layouts  2.74 us (2%)
  other arithmetic  1.49 us (1%)
    all_to_all x1, blocking collectives, on_device(): lax.all_to_all(back.reshape(16, 128, 128), COLUMNS, 0, 0, tiled=True)  23.8 us
    all_to_all x1, blocking collectives, on_device(): spread = lax.all_to_all(partial, CTX, 0, 0, tiled=True)  18 us
    ppermute x3, waiting for transfers between devices, on_device(): lax.ppermute(part, X, [(i, i ^ away) for i in range(4)])  15.5 us
    all_to_all x1, waiting for transfers between devices, on_device(): lax.all_to_all(cotangent.reshape(16, ROWS, 128), RETURN, 0, 0, tiled=True)  13.2 us
    ppermute x3, starting transfers between devices, on_device(): lax.ppermute(part, X, [(i, i ^ away) for i in range(4)])  10.4 us
    ppermute x1, starting transfers between devices, on_device(): moved = lax.ppermute(tokens, ('yh', 'zh'), QUARTER_TURN)  10 us
    ppermute x1, waiting for transfers between devices, on_device(): input_grad = lax.ppermute(summed, AXES, grad_route())  8.56 us
    all_to_all x1, starting transfers between devices, on_device(): lax.all_to_all(copies, SPREAD, 0, 0, tiled=True).reshape(4, 2, 4, 128, 128)  8.22 us
  transfers between devices with their start and end apart: 10, of which 9 were waited for; matrix products, arithmetic and copies ran while one was open for 2% of the time, Pallas kernels for 6%

profile of v7, /device:TPU:80, one launch (start us, length us, event | category | flops | bytes accessed | tf_op | source)
XLA Modules:
  0.0 141.5 jit_solution(9956638714327631244)
XLA Ops:
  0.6 10.0 %collective-permute-start = (bf16[128,128]{1,0:T(8,128)(2,1)}, bf16[128,128]{1,0:T(8,128)(2,1)S(1)}, u32[]{:S(2)}, u32[]{:S(2)}) collective-permute-start(bf16[128,128]{1,0:T(8,128)(2,1)} %param.6), channel_id=1, source_target_pairs={{0,8},{8,72},{64,0},{72,64},{1,9},{9,73},{65,1},{73,65},{2,10},{10... | collective-permute-start | bytes 98312 | tf_op jit(solution)/shard_map/ppermute | solution.py:329
  10.7 4.7 %collective-permute-start.2 = (bf16[3,1024,128]{2,1,0:T(8,128)(2,1)}, bf16[3,1024,128]{2,1,0:T(8,128)(2,1)S(1)}, u32[]{:S(2)}, u32[]{:S(2)}) collective-permute-start(bf16[3,1024,128]{2,1,0:T(8,128)(2,1)} %bitcast.18), channel_id=1, source_target_pairs={{0,384},{128,256},{256,128},{384,0},{1,385},{129,257},{257,129},{3... | collective-permute-start | bytes 2359304 | tf_op jit(solution)/shard_map/ppermute | solution.py:333
  15.3 2.1 %collective-permute-start.1 = (bf16[3,1024,128]{2,1,0:T(8,128)(2,1)}, bf16[3,1024,128]{2,1,0:T(8,128)(2,1)S(1)}, u32[]{:S(2)}, u32[]{:S(2)}) collective-permute-start(bf16[3,1024,128]{2,1,0:T(8,128)(2,1)} %bitcast.19), channel_id=1, source_target_pairs={{0,128},{128,0},{256,384},{384,256},{1,129},{129,1},{257,385},{385... | collective-permute-start | bytes 2359304 | tf_op jit(solution)/shard_map/ppermute | solution.py:333
  17.7 1.0 copy-done.1
  18.7 8.2 %all-to-all-start = ((bf16[32,128,128]{2,1,0:T(8,128)(2,1)}), bf16[32,128,128]{2,1,0:T(8,128)(2,1)S(1)}, u32[]{:S(2)}, u32[]{:S(2)}) async-start(bf16[32,128,128]{2,1,0:T(8,128)(2,1)} %copy-done.1), calls=%async_computation | async-start | bytes 2097152 | tf_op jit(solution)/shard_map/all_to_all | solution.py:367
  27.0 3.6 %collective-permute-start.3 = (bf16[3,1024,128]{2,1,0:T(8,128)(2,1)S(1)}, bf16[3,1024,128]{2,1,0:T(8,128)(2,1)}, u32[]{:S(2)}, u32[]{:S(2)}) collective-permute-start(bf16[3,1024,128]{2,1,0:T(8,128)(2,1)S(1)} %bitcast.20), channel_id=1, source_target_pairs={{0,256},{128,384},{256,0},{384,128},{1,257},{129,385},{257,1},{385... | collective-permute-start | bytes 2359304 | tf_op jit(solution)/shard_map/ppermute | solution.py:333
  30.6 2.4 %collective-permute-done.2 = bf16[3,1024,128]{2,1,0:T(8,128)(2,1)S(1)} collective-permute-done((bf16[3,1024,128]{2,1,0:T(8,128)(2,1)}, bf16[3,1024,128]{2,1,0:T(8,128)(2,1)S(1)}, u32[]{:S(2)}, u32[]{:S(2)}) %collective-permute-start.2) | collective-permute-done | bytes 786464 | tf_op jit(solution)/shard_map/ppermute | solution.py:333
  33.0 4.9 %collective-permute-done.1 = bf16[3,1024,128]{2,1,0:T(8,128)(2,1)S(1)} collective-permute-done((bf16[3,1024,128]{2,1,0:T(8,128)(2,1)}, bf16[3,1024,128]{2,1,0:T(8,128)(2,1)S(1)}, u32[]{:S(2)}, u32[]{:S(2)}) %collective-permute-start.1) | collective-permute-done | bytes 786464 | tf_op jit(solution)/shard_map/ppermute | solution.py:333
  37.9 1.3 pad_maximum_fusion
  39.2 2.5 %collective-permute-start.5 = (bf16[2,3,1024,128]{3,2,1,0:T(8,128)(2,1)}, bf16[2,3,1024,128]{3,2,1,0:T(8,128)(2,1)}, u32[]{:S(2)}, u32[]{:S(2)}) collective-permute-start(bf16[2,3,1024,128]{3,2,1,0:T(8,128)(2,1)} %pad_maximum_fusion), channel_id=1, source_target_pairs={{0,2},{2,0},{1,3},{3,1},{4,6},{6,4},{5,7},{7,5},{8,10},{10,8},{9,1... | collective-permute-start | bytes 4718600 | tf_op jit(solution)/shard_map/ppermute | solution.py:368
  41.7 1.4 %table.1.table_ref = f32[128,128]{1,0:T(8,128)} custom-call(f32[3,3,128]{2,1,0:T(4,128)} %taps_ref, f32[1,128]{1,0:T(1,128)} %bitcast.33), custom_call_target="tpu_custom_call" | custom-call | flops 20000000000 | bytes 1048576 | tf_op jit(solution)/shard_map/table/pallas_call | solution.py:348
  43.1 1.8 %prepare.1.band_ref = bf16[4,128,128]{2,1,0:T(8,128)(2,1)} custom-call(f32[8,128]{1,0:T(8,128)} %filter_ref), custom_call_target="tpu_custom_call" | custom-call | tf_op jit(solution)/shard_map/prepare/pallas_call | solution.py:341
  44.9 8.1 %collective-permute-done.3 = bf16[3,1024,128]{2,1,0:T(8,128)(2,1)} collective-permute-done((bf16[3,1024,128]{2,1,0:T(8,128)(2,1)S(1)}, bf16[3,1024,128]{2,1,0:T(8,128)(2,1)}, u32[]{:S(2)}, u32[]{:S(2)}) %collective-permute-start.3) | collective-permute-done | bytes 786464 | tf_op jit(solution)/shard_map/ppermute | solution.py:333
  53.0 0.2 all-to-all-done
  53.3 1.9 %collective-permute-start.4 = (bf16[4,2,4,128,128]{4,3,2,1,0:T(8,128)(2,1)S(1)}, bf16[4,2,4,128,128]{4,3,2,1,0:T(8,128)(2,1)S(1)}, u32[]{:S(2)}, u32[]{:S(2)}) collective-permute-start(bf16[4,2,4,128,128]{4,3,2,1,0:T(8,128)(2,1)S(1)} %bitcast.27), channel_id=1, source_target_pairs={{0,1},{1,0},{2,3},{3,2},{4,5},{5,4},{6,7},{7,6},{8,9},{9,8},{10,11... | collective-permute-start | bytes 3145736 | tf_op jit(solution)/shard_map/ppermute | solution.py:370
  55.2 2.6 %collective-permute-done.4.other_ref = bf16[4,2,4,128,128]{4,3,2,1,0:T(8,128)(2,1)S(1)} collective-permute-done((bf16[4,2,4,128,128]{4,3,2,1,0:T(8,128)(2,1)S(1)}, bf16[4,2,4,128,128]{4,3,2,1,0:T(8,128)(2,1)S(1)}, u32[]{:S(2)}, u32[]{:S(2)}) %collective-permute-start.4) | collective-permute-done | bytes 1048608 | tf_op jit(solution)/shard_map/ppermute | solution.py:370
  57.8 2.0 %project.1 = bf16[8,112,128]{2,1,0:T(8,128)(2,1)S(1)} custom-call(bf16[4,2,4,128,128]{4,3,2,1,0:T(8,128)(2,1)S(1)} %bitcast.28, bf16[4,2,4,128,128]{4,3,2,1,0:T(8,128)(2,1)S(1)} %collective-permute-done.4.other_ref, bf16[3,4,2,128,128]{4,3,2,1,0:T(8,128)(2,1)S(1)} %bitcast.22, bf16[3,4,2,128,128]{4,3,2,1,0:T(8,128)(2,1)S(1)} %bitcast.30, ...), custom_call_target="tpu_custom_call" | custom-call | flops 805306368 | bytes 5242880 | tf_op jit(solution)/shard_map/project/pallas_call | solution.py:374
  59.9 18.0 %all_to_all.20.in_ref = bf16[8,112,128]{2,1,0:T(8,128)(2,1)S(1)} all-to-all(bf16[8,112,128]{2,1,0:T(8,128)(2,1)S(1)} %project.1), channel_id=1, replica_groups=mesh['xh'=2,'xl'=2,'yh'=2,'ylh'=2,'yll'=2,'zh'=2,'z2'=2,'zp'=2,'core'=2]..., dimensions={0} | all-to-all | bytes 458752 | tf_op jit(solution)/shard_map/all_to_all | solution.py:387
  77.8 1.7 %mixer.1 = bf16[2,8,112,128]{3,2,1,0:T(8,128)(2,1)} custom-call(bf16[8,112,128]{2,1,0:T(8,128)(2,1)S(1)} %all_to_all.20.in_ref, f32[128,128]{1,0:T(8,128)S(1)} %copy-done.3, bf16[4,128,128]{2,1,0:T(8,128)(2,1)S(1)} %copy-done.2), custom_call_target="tpu_custom_call" | custom-call | tf_op jit(solution)/shard_map/mixer/pallas_call | solution.py:389
  79.6 3.9 %all-to-all-start.2 = ((bf16[16,112,128]{2,1,0:T(8,128)(2,1)}), bf16[16,112,128]{2,1,0:T(8,128)(2,1)S(1)}, u32[]{:S(2)}, u32[]{:S(2)}) async-start(bf16[16,112,128]{2,1,0:T(8,128)(2,1)} %bitcast.7), calls=%async_computation.2 | async-start | bytes 917504 | tf_op jit(solution)/shard_map/all_to_all | solution.py:397
  83.5 1.1 collective-permute-done.5
  84.6 0.8 arrived.1.w_far
  85.3 13.2 %all-to-all-done.2 = bf16[16,112,128]{2,1,0:T(8,128)(2,1)S(1)} async-done(((bf16[16,112,128]{2,1,0:T(8,128)(2,1)}), bf16[16,112,128]{2,1,0:T(8,128)(2,1)S(1)}, u32[]{:S(2)}, u32[]{:S(2)}) %all-to-all-start.2) | async-done | bytes 458784 | tf_op jit(solution)/shard_map/all_to_all | solution.py:397
  98.6 2.9 %back.1 = (bf16[2,2,2,2,128,128]{5,4,3,2,1,0:T(8,128)(2,1)S(1)}, bf16[2,2,2,2,128,128]{5,4,3,2,1,0:T(8,128)(2,1)S(1)}, f32[8,128]{1,0:T(8,128)}, f32[16,128]{1,0:T(8,128)S(1)}) custom-call(bf16[2,8,112,128]{3,2,1,0:T(8,128)(2,1)S(1)} %bitcast.29, bf16[3,4,2,128,128]{4,3,2,1,0:T(8,128)(2,1)S(1)} %bitcast.23, bf16[3,4,2,128,128]{4,3,2,1,0:T(8,128)(2,1)S(1)} %bitcast.26, ...), custom_call_target="tpu_custom_call" | custom-call | flops 805306368 | bytes 5242880 | tf_op jit(solution)/shard_map/back/pallas_call | solution.py:402
  101.4 1.9 %collective-permute-start.6 = (bf16[2,2,2,2,128,128]{5,4,3,2,1,0:T(8,128)(2,1)S(1)}, bf16[2,2,2,2,128,128]{5,4,3,2,1,0:T(8,128)(2,1)S(1)}, u32[]{:S(2)}, u32[]{:S(2)}) collective-permute-start(bf16[2,2,2,2,128,128]{5,4,3,2,1,0:T(8,128)(2,1)S(1)} %get-tuple-element.29), channel_id=1, source_target_pairs={{0,1},{1,0},{2,3},{3,2},{4,5},{5,4},{6,7},{7,6},{8,9},{9,8},{10,11... | collective-permute-start | bytes 1572872 | tf_op jit(solution)/shard_map/ppermute | solution.py:417
  103.3 1.9 %collective-permute-done.6 = bf16[2,2,2,2,128,128]{5,4,3,2,1,0:T(8,128)(2,1)S(1)} collective-permute-done((bf16[2,2,2,2,128,128]{5,4,3,2,1,0:T(8,128)(2,1)S(1)}, bf16[2,2,2,2,128,128]{5,4,3,2,1,0:T(8,128)(2,1)S(1)}, u32[]{:S(2)}, u32[]{:S(2)}) %collective-permute-start.6) | collective-permute-done | bytes 524320 | tf_op jit(solution)/shard_map/ppermute | solution.py:417
  105.4 23.8 %all_to_all.21 = bf16[16,128,128]{2,1,0:T(8,128)(2,1)S(1)} all-to-all(bf16[16,128,128]{2,1,0:T(8,128)(2,1)S(1)} %bitcast.32), channel_id=1, replica_groups=mesh['xh'=2,'xl'=2,'yh'=2,'ylh'=2,'yll'=2,'zh'=2,'z2'=2,'zp'=2,'core'=2]..., dimensions={0} | all-to-all | bytes 1048576 | tf_op jit(solution)/shard_map/all_to_all | solution.py:419
  129.3 1.9 %collective-permute-start.7 = (bf16[128,128]{1,0:T(8,128)(2,1)S(1)}, bf16[128,128]{1,0:T(8,128)(2,1)S(1)}, u32[]{:S(2)}, u32[]{:S(2)}) collective-permute-start(bf16[128,128]{1,0:T(8,128)(2,1)S(1)} %reduce_sum.12), channel_id=1, source_target_pairs={{24,0},{25,1},{8,2},{9,3},{28,4},{29,5},{12,6},{13,7},{88,8},{89,9... | collective-permute-start | bytes 98312 | tf_op jit(solution)/shard_map/ppermute | solution.py:421
  131.2 0.5 slice_bitcast_fusion
  131.7 0.6 reshape.51
  132.3 8.6 %collective-permute-done.7 = bf16[128,128]{1,0:T(8,128)(2,1)S(1)} collective-permute-done((bf16[128,128]{1,0:T(8,128)(2,1)S(1)}, bf16[128,128]{1,0:T(8,128)(2,1)S(1)}, u32[]{:S(2)}, u32[]{:S(2)}) %collective-permute-start.7) | collective-permute-done | bytes 32800 | tf_op jit(solution)/shard_map/ppermute | solution.py:421
  140.9 0.6 copy.13
  (13 shorter events, 0.5 us)
Async XLA Ops:
  0.6 16.8 %collective-permute-start = (bf16[128,128]{1,0:T(8,128)(2,1)}, bf16[128,128]{1,0:T(8,128)(2,1)S(1)}, u32[]{:S(2)}, u32[]{:S(2)}) collective-permute-start(bf16[128,128]{1,0:T(8,128)(2,1)} %param.6), channel_id=1, source_target_pairs={{0,8},{8,72},{64,0},{72,64},{1,9},{9,73},{65,1},{73,65},{2,10},{10... | collective-permute-start | bytes 98312 | tf_op jit(solution)/shard_map/ppermute | solution.py:329
  10.7 22.3 %collective-permute-start.2 = (bf16[3,1024,128]{2,1,0:T(8,128)(2,1)}, bf16[3,1024,128]{2,1,0:T(8,128)(2,1)S(1)}, u32[]{:S(2)}, u32[]{:S(2)}) collective-permute-start(bf16[3,1024,128]{2,1,0:T(8,128)(2,1)} %bitcast.18), channel_id=1, source_target_pairs={{0,384},{128,256},{256,128},{384,0},{1,385},{129,257},{257,129},{3... | collective-permute-start | bytes 2359304 | tf_op jit(solution)/shard_map/ppermute | solution.py:333
  15.3 22.6 %collective-permute-start.1 = (bf16[3,1024,128]{2,1,0:T(8,128)(2,1)}, bf16[3,1024,128]{2,1,0:T(8,128)(2,1)S(1)}, u32[]{:S(2)}, u32[]{:S(2)}) collective-permute-start(bf16[3,1024,128]{2,1,0:T(8,128)(2,1)} %bitcast.19), channel_id=1, source_target_pairs={{0,128},{128,0},{256,384},{384,256},{1,129},{129,1},{257,385},{385... | collective-permute-start | bytes 2359304 | tf_op jit(solution)/shard_map/ppermute | solution.py:333
  17.7 1.0 copy-start.1
  18.7 8.2 %copy-start = (bf16[1024,3,128]{2,0,1:T(8,128)(2,1)S(1)}, bf16[1024,3,128]{2,0,1:T(8,128)(2,1)}, u32[]{:S(2)}) copy-start(bf16[1024,3,128]{2,0,1:T(8,128)(2,1)} %param.7) | copy-start | bytes 2359300
  18.7 34.5 %all-to-all-start = ((bf16[32,128,128]{2,1,0:T(8,128)(2,1)}), bf16[32,128,128]{2,1,0:T(8,128)(2,1)S(1)}, u32[]{:S(2)}, u32[]{:S(2)}) async-start(bf16[32,128,128]{2,1,0:T(8,128)(2,1)} %copy-done.1), calls=%async_computation | async-start | bytes 2097152 | tf_op jit(solution)/shard_map/all_to_all | solution.py:367
  27.0 26.1 %collective-permute-start.3 = (bf16[3,1024,128]{2,1,0:T(8,128)(2,1)S(1)}, bf16[3,1024,128]{2,1,0:T(8,128)(2,1)}, u32[]{:S(2)}, u32[]{:S(2)}) collective-permute-start(bf16[3,1024,128]{2,1,0:T(8,128)(2,1)S(1)} %bitcast.20), channel_id=1, source_target_pairs={{0,256},{128,384},{256,0},{384,128},{1,257},{129,385},{257,1},{385... | collective-permute-start | bytes 2359304 | tf_op jit(solution)/shard_map/ppermute | solution.py:333
  39.2 45.4 %collective-permute-start.5 = (bf16[2,3,1024,128]{3,2,1,0:T(8,128)(2,1)}, bf16[2,3,1024,128]{3,2,1,0:T(8,128)(2,1)}, u32[]{:S(2)}, u32[]{:S(2)}) collective-permute-start(bf16[2,3,1024,128]{3,2,1,0:T(8,128)(2,1)} %pad_maximum_fusion), channel_id=1, source_target_pairs={{0,2},{2,0},{1,3},{3,1},{4,6},{6,4},{5,7},{7,5},{8,10},{10,8},{9,1... | collective-permute-start | bytes 4718600 | tf_op jit(solution)/shard_map/ppermute | solution.py:368
  41.6 16.2 %copy-start.4 = (bf16[128,128]{1,0:T(8,128)(2,1)S(1)}, bf16[128,128]{1,0:T(8,128)(2,1)}, u32[]{:S(2)}) copy-start(bf16[128,128]{1,0:T(8,128)(2,1)} %grad_ref.1) | copy-start | bytes 98308
  53.3 4.5 %collective-permute-start.4 = (bf16[4,2,4,128,128]{4,3,2,1,0:T(8,128)(2,1)S(1)}, bf16[4,2,4,128,128]{4,3,2,1,0:T(8,128)(2,1)S(1)}, u32[]{:S(2)}, u32[]{:S(2)}) collective-permute-start(bf16[4,2,4,128,128]{4,3,2,1,0:T(8,128)(2,1)S(1)} %bitcast.27), channel_id=1, source_target_pairs={{0,1},{1,0},{2,3},{3,2},{4,5},{5,4},{6,7},{7,6},{8,9},{9,8},{10,11... | collective-permute-start | bytes 3145736 | tf_op jit(solution)/shard_map/ppermute | solution.py:370
  57.8 20.0 %copy-start.2 = (bf16[4,128,128]{2,1,0:T(8,128)(2,1)S(1)}, bf16[4,128,128]{2,1,0:T(8,128)(2,1)}, u32[]{:S(2)}) copy-start(bf16[4,128,128]{2,1,0:T(8,128)(2,1)} %prepare.1.band_ref) | copy-start | bytes 393220
  57.8 20.0 %copy-start.3 = (f32[128,128]{1,0:T(8,128)S(1)}, f32[128,128]{1,0:T(8,128)}, u32[]{:S(2)}) copy-start(f32[128,128]{1,0:T(8,128)} %table.1.table_ref) | copy-start | bytes 196612
  79.6 19.0 %all-to-all-start.2 = ((bf16[16,112,128]{2,1,0:T(8,128)(2,1)}), bf16[16,112,128]{2,1,0:T(8,128)(2,1)S(1)}, u32[]{:S(2)}, u32[]{:S(2)}) async-start(bf16[16,112,128]{2,1,0:T(8,128)(2,1)} %bitcast.7), calls=%async_computation.2 | async-start | bytes 917504 | tf_op jit(solution)/shard_map/all_to_all | solution.py:397
  101.4 3.8 %collective-permute-start.6 = (bf16[2,2,2,2,128,128]{5,4,3,2,1,0:T(8,128)(2,1)S(1)}, bf16[2,2,2,2,128,128]{5,4,3,2,1,0:T(8,128)(2,1)S(1)}, u32[]{:S(2)}, u32[]{:S(2)}) collective-permute-start(bf16[2,2,2,2,128,128]{5,4,3,2,1,0:T(8,128)(2,1)S(1)} %get-tuple-element.29), channel_id=1, source_target_pairs={{0,1},{1,0},{2,3},{3,2},{4,5},{5,4},{6,7},{7,6},{8,9},{9,8},{10,11... | collective-permute-start | bytes 1572872 | tf_op jit(solution)/shard_map/ppermute | solution.py:417
  129.3 11.6 %collective-permute-start.7 = (bf16[128,128]{1,0:T(8,128)(2,1)S(1)}, bf16[128,128]{1,0:T(8,128)(2,1)S(1)}, u32[]{:S(2)}, u32[]{:S(2)}) collective-permute-start(bf16[128,128]{1,0:T(8,128)(2,1)S(1)} %reduce_sum.12), channel_id=1, source_target_pairs={{24,0},{25,1},{8,2},{9,3},{28,4},{29,5},{12,6},{13,7},{88,8},{89,9... | collective-permute-start | bytes 98312 | tf_op jit(solution)/shard_map/ppermute | solution.py:421
